TPU v7x, 256 devices: a whole 4x4x8 slice. The times are simulated.
256 devices in a mesh: grp: 8 (over x, y_hi), row: 4 (over y_lo, core), col: 8 (over z).
Axes of the slice: x: 4, y: 4 (y_hi: 2, y_lo: 2; y = y_hi * 2 + y_lo), z: 8, core: 2. Of those that a mesh axis runs over, the one named last changes fastest.
Arguments:
- phase: bfloat16 [64, 8, 128, 4096], P('grp', None, 'row', 'col'), may hold values from -6 to 6
- pseudo_inverse: bfloat16 [48, 64], replicated, may hold values from -0.75 to 0.75
- rotation: float32 [4, 3], replicated, may hold values from -4 to 4
- plate_id: int32 [1024, 4096], P(('grp', 'row'), 'col'), may hold values from 0 to 3
- coherent: int32 [1024, 4096], P(('grp', 'row'), 'col'), may hold values 0 or 1
Outputs:
- displacement: bfloat16 [48, 1024, 4096], P(None, ('grp', 'row'), 'col')
- grad_rows: float32 [1024, 4096], P(('grp', 'row'), 'col')
- grad_cols: float32 [1024, 4096], P(('grp', 'row'), 'col')
All inputs are finite; a program needn't handle non-finite values. No bound on the sum of `coherent` on one device may be relied on, other than what follows from the above.
Results may differ from a plain program's by a relative error of at most 0.001.
Values may be sent and summed in bfloat16 or wider, within the bound.
No kernel may reach another device: no remote copies, remote signals or barrier semaphores. Data moves between devices by JAX's collectives and lax.ppermute only.
A program may use at most 128 MiB of HBM per device.

v0:
```python
import jax
import jax.numpy as jnp
from jax import lax
from jax.sharding import PartitionSpec as P


def extended(block, sides, width):
    for axis, dim in sides:
        count = lax.axis_size(axis)
        forward = [(i, i + 1) for i in range(count - 1)]
        backward = [(target, source) for source, target in forward]
        low = lax.ppermute(
            lax.slice_in_dim(block, block.shape[dim] - width, None, axis=dim), axis, forward
        )
        high = lax.ppermute(lax.slice_in_dim(block, 0, width, axis=dim), axis, backward)
        block = jnp.concatenate([low, block, high], axis=dim)
    return block


def lever_field(rows, cols, total_rows, total_cols):
    lat = jnp.deg2rad(36.0 + 6.0 * (rows + 0.5) / total_rows)
    lon = jnp.deg2rad(26.0 + 19.0 * (cols + 0.5) / total_cols)
    px = jnp.cos(lat) * jnp.cos(lon)
    py = jnp.cos(lat) * jnp.sin(lon)
    pz = jnp.sin(lat) + 0.0 * lon
    sx, sy, sz = (0.38, -0.08, 0.92)
    return jnp.stack([py * sz - pz * sy, pz * sx - px * sz, px * sy - py * sx])


def on_device(phase, pseudo_inverse, rotation, plate_id, coherent):
    local_ifg = phase.shape[0]
    groups = phase.shape[1]
    tile_rows = plate_id.shape[0]
    tile_cols = plate_id.shape[1]
    epochs = pseudo_inverse.shape[0]
    own_cols = lax.dynamic_slice_in_dim(
        pseudo_inverse, lax.axis_index("grp") * local_ifg, local_ifg, 1
    )
    flat = phase.reshape(local_ifg, groups * tile_rows, tile_cols)
    summed = lax.psum_scatter(
        jnp.einsum("ei,irx->rex", own_cols, flat, preferred_element_type=jnp.float32),
        "grp",
        scatter_dimension=0,
        tiled=True,
    )
    series = jnp.transpose(summed, (1, 0, 2))
    displacement = series.astype(jnp.bfloat16)
    steps = jnp.arange(epochs, dtype=jnp.float32) - (epochs - 1) / 2.0
    slope = steps / jnp.sqrt(jnp.sum(steps * steps))
    rate = jnp.einsum("e,eyx->yx", slope, series, precision=lax.Precision.HIGHEST)
    tile_index = lax.axis_index("grp") * lax.axis_size("row") + lax.axis_index("row")
    total_rows = tile_rows * lax.axis_size("grp") * lax.axis_size("row")
    total_cols = tile_cols * lax.axis_size("col")
    rows = (tile_index * tile_rows).astype(jnp.float32) + jnp.arange(tile_rows, dtype=jnp.float32)[
        :, None
    ]
    cols = (lax.axis_index("col") * tile_cols).astype(jnp.float32) + jnp.arange(
        tile_cols, dtype=jnp.float32
    )[None, :]
    lever = lever_field(rows, cols, total_rows, total_cols)
    along = jnp.einsum("pk,kyx->pyx", rotation, lever, precision=lax.Precision.HIGHEST)
    plate_range = jnp.arange(rotation.shape[0], dtype=jnp.int32)[:, None, None]
    plate_rate = jnp.sum(jnp.where(plate_id[None] == plate_range, along, 0.0), axis=0)
    velocity = coherent.astype(jnp.float32) * rate - plate_rate
    reach = 16
    norm = jnp.sqrt(jnp.float32(reach * (reach + 1) * (2 * reach + 1) // 3))
    upright = extended(velocity, ((("grp", "row"), 0),), reach)
    sideways = extended(velocity, (("col", 1),), reach)
    grad_rows = jnp.zeros((tile_rows, tile_cols), jnp.float32)
    grad_cols = jnp.zeros((tile_rows, tile_cols), jnp.float32)
    for k in range(-reach, reach + 1):
        tap = k / norm
        grad_rows = grad_rows + tap * upright[reach + k : reach + k + tile_rows, :]
        grad_cols = grad_cols + tap * sideways[:, reach + k : reach + k + tile_cols]
    return (displacement, grad_rows, grad_cols)


def solution(mesh):
    return jax.shard_map(
        on_device,
        mesh=mesh,
        in_specs=(
            P("grp", None, "row", "col"),
            P(),
            P(),
            P(("grp", "row"), "col"),
            P(("grp", "row"), "col"),
        ),
        out_specs=(
            P(None, ("grp", "row"), "col"),
            P(("grp", "row"), "col"),
            P(("grp", "row"), "col"),
        ),
        check_vma=False,
    )
```

profile of v0, /device:TPU:96, one launch (start us, length us, event | category | flops | bytes accessed | tf_op | source)
XLA Modules:
  0.0 315.8 jit_solution(7524568718755876016)
XLA Ops:
  7.2 0.0 copy-start
  7.2 0.0 reduce-scatter.2.cloned.1.call-start
  7.2 1.5 copy-done
  8.8 10.9 %convolution_bitcast_fusion = f32[256,48,512]{2,1,0:T(8,128)} fusion(bf16[8,256,512]{2,1,0:T(8,128)(2,1)S(1)} %bitcast.27, bf16[48,64]{1,0:T(8,128)(2,1)} %param.6, s32[]{:T(128)S(6)} %select_n.7), kind=kOutput, calls=%fused_computation | convolution fusion | flops 100663296 | bytes 27269124 | tf_op jit(solution)/shard_map/ei,irx->rex/dot_general | solution.py:41
  19.7 0.0 copy-start.3
  19.7 0.0 copy-start.4
  19.7 0.0 reduce-scatter.2.cloned.1.call-update
  19.7 0.6 multiply_reduce_fusion
  21.0 0.1 fusion.207
  21.1 0.1 fusion.204
  21.1 0.1 fusion.201
  21.2 0.1 fusion.6
  21.3 0.0 copy-start.2
  21.3 0.0 copy-done.3
  21.3 0.0 copy-done.4
  21.3 0.8 fusion.4
  22.1 268.0 %reduce-scatter.2.cloned.1.call-done = f32[32,48,512]{2,1,0:T(8,128)} async-done(((f32[256,48,512]{2,1,0:T(8,128)}), f32[32,48,512]{2,1,0:T(8,128)}) %reduce-scatter.2.cloned.1.call-update) | async-done | bytes 3145744 | tf_op jit(solution)/shard_map/reduce_scatter | solution.py:40
  290.1 3.6 %fusion = f32[1,32,512]{2,0,1:T(1,128)S(1)} fusion(f32[32,48,512]{2,1,0:T(8,128)} %reduce-scatter.2.cloned.1.call-done, f32[]{:T(128)S(6)} %sqrt.3), kind=kOutput, calls=%fused_computation.1 | convolution fusion | flops 9437280 | bytes 3211268 | tf_op jit(solution)/shard_map/e,eyx->yx/dot_general | solution.py:50
  293.7 0.0 copy-done.2
  293.8 0.1 fusion.213
  293.8 2.4 collective-permute-start.3
  296.2 4.7 %collective-permute-start.2 = (f32[32,16]{1,0:T(8,128)S(1)}, f32[32,16]{1,0:T(8,128)S(1)}, u32[]{:S(2)}, u32[]{:S(2)}) collective-permute-start(f32[32,16]{1,0:T(8,128)S(1)} %get-tuple-element.11), channel_id=1, source_target_pairs={{0,1},{1,2},{2,3},{3,4},{4,5},{5,6},{6,7},{8,9},{9,10},{10,11},{11... | collective-permute-start | bytes 6152 | tf_op jit(solution)/shard_map/ppermute | solution.py:12
  300.9 1.3 collective-permute-start.1
  302.2 3.0 collective-permute-start
  305.2 0.0 copy-done.1
  305.2 0.2 bitcast_convert_fusion
  305.5 2.0 copy.14
  307.5 0.0 collective-permute-done.3
  307.5 0.0 collective-permute-done.2
  307.5 0.0 collective-permute-done.1
  307.5 0.0 collective-permute-done
  307.5 1.4 fusion.12
  (4 shorter events, 0.0 us)
Async XLA Ops:
  7.2 1.6 copy-start
  7.2 282.9 %reduce-scatter.2.cloned.1.call-start = ((), (), s32[]{:S(2)}) async-start(), calls=%async_computation.1 | async-start | bytes 28311552 | tf_op jit(solution)/shard_map/reduce_scatter | solution.py:40
  19.7 1.6 copy-start.3
  19.7 1.7 copy-start.4
  21.3 272.4 %copy-start.2 = (s32[32,512]{1,0:T(8,128)S(1)}, s32[32,512]{1,0:T(8,128)}, u32[]{:S(2)}) copy-start(s32[32,512]{1,0:T(8,128)} %param.9) | copy-start | bytes 196612
  290.1 15.1 %copy-start.1 = (f32[32,48,512]{2,1,0:T(8,128)S(1)}, f32[32,48,512]{2,1,0:T(8,128)}, u32[]{:S(2)}) copy-start(f32[32,48,512]{2,1,0:T(8,128)} %reduce-scatter.2.cloned.1.call-done) | copy-start | bytes 9437188
  293.8 13.7 %collective-permute-start.3 = (f32[32,16]{1,0:T(8,128)S(1)}, f32[32,16]{1,0:T(8,128)S(1)}, u32[]{:S(2)}, u32[]{:S(2)}) collective-permute-start(f32[32,16]{1,0:T(8,128)S(1)} %get-tuple-element.12), channel_id=1, source_target_pairs={{1,0},{2,1},{3,2},{4,3},{5,4},{6,5},{7,6},{9,8},{10,9},{11,10},{12... | collective-permute-start | bytes 6152 | tf_op jit(solution)/shard_map/ppermute | solution.py:15
  296.2 11.3 %collective-permute-start.2 = (f32[32,16]{1,0:T(8,128)S(1)}, f32[32,16]{1,0:T(8,128)S(1)}, u32[]{:S(2)}, u32[]{:S(2)}) collective-permute-start(f32[32,16]{1,0:T(8,128)S(1)} %get-tuple-element.11), channel_id=1, source_target_pairs={{0,1},{1,2},{2,3},{3,4},{4,5},{5,6},{6,7},{8,9},{9,10},{10,11},{11... | collective-permute-start | bytes 6152 | tf_op jit(solution)/shard_map/ppermute | solution.py:12
  300.9 6.6 %collective-permute-start.1 = (f32[16,512]{1,0:T(8,128)S(1)}, f32[16,512]{1,0:T(8,128)S(1)}, u32[]{:S(2)}, u32[]{:S(2)}) collective-permute-start(f32[16,512]{1,0:T(8,128)S(1)} %get-tuple-element.14), channel_id=1, source_target_pairs={{8,0},{16,8},{24,16},{32,24},{40,32},{48,40},{56,48},{64,56},{72,6... | collective-permute-start | bytes 98312 | tf_op jit(solution)/shard_map/ppermute | solution.py:15
  302.2 5.3 %collective-permute-start = (f32[16,512]{1,0:T(8,128)S(1)}, f32[16,512]{1,0:T(8,128)S(1)}, u32[]{:S(2)}, u32[]{:S(2)}) collective-permute-start(f32[16,512]{1,0:T(8,128)S(1)} %get-tuple-element.13), channel_id=1, source_target_pairs={{0,8},{8,16},{16,24},{24,32},{32,40},{40,48},{48,56},{56,64},{64,7... | collective-permute-start | bytes 98312 | tf_op jit(solution)/shard_map/ppermute | solution.py:12
Sparse Core Ops, SparseCore 0:
  19.8 270.2 reduce-scatter.1
where the time goes:
time: 317 us; the launch traced here: 316 us
  waiting for transfers between devices  268 us (85%)
  matrix products  15.3 us (5%)
  between operations  14.9 us (5%)
  starting transfers between devices  11.4 us (4%)
  local copies, waits for them, and re-layouts  3.64 us (1%)
    reduce_scatter x1, waiting for transfers between devices, on_device(): lax.psum_scatter(jnp.einsum('ei,irx->rex', own_cols, flat, preferred_elem...  268 us
    dot_general x1, matrix products, on_device(): jnp.einsum('ei,irx->rex', own_cols, flat, preferred_element_type=jnp.floa...  10.9 us
    ppermute x2, starting transfers between devices, extended(): lax.ppermute(lax.slice_in_dim(block, block.shape[dim] - width, None, axis...  7.71 us
  transfers between devices with their start and end apart: 5, of which 1 were waited for; matrix products, arithmetic and copies ran while one was open for 1% of the time, Pallas kernels for 0%

commit v1 on v0

v1 whole, which is shorter than its diff:
```python
import jax
import jax.numpy as jnp
from jax import lax
from jax.experimental import pallas as pl
from jax.experimental.pallas import tpu as pltpu
from jax.sharding import PartitionSpec as P

REACH = 16
SUB = 16
LANES = 128
F32 = jnp.float32
BF16 = jnp.bfloat16
VMEM_BYTES = 48 << 20

FLOWS = {
    "own": (0, 0),
    "D2": (2, 1),
    "Da": ("a", 1),
    "Db": ("b", 1),
    "X2": (2, 0),
    "Y2": (0, 1),
    "Xa": ("a", 0),
    "Xb": ("b", 0),
}
EMIT = ("Xa", "Da", "Y2", "X2", "Db", "Xb", "D2")


def along_x(step, x, core, pick):
    if step == "a":
        return pick(((x + core) & 1) == 0, 1, 3)
    if step == "b":
        return pick(((x + core) & 1) == 0, 3, 1)
    return step


def partner(flow, x, y, core, pick):
    step, turn = FLOWS[flow]
    return (((x + along_x(step, x, core, pick)) & 3) << 1) + ((y + turn) & 1)


def swap_pairs(flow):
    def choose(test, first, second):
        return first if test else second

    pairs = []
    for grp in range(8):
        for row in range(4):
            other = partner(flow, grp // 2, grp % 2, row % 2, choose)
            pairs.append((grp * 4 + row, other * 4 + row))
    return pairs


def row_pairs(tiles, first):
    pairs = []
    for low in range(first, tiles - 1, 2):
        pairs += [(low, low + 1), (low + 1, low)]
    return pairs


def prep_kernel(src_ref, rot_ref, pinv_ref, lat_ref, lon_ref, plate_ref, w_ref, rate_ref):
    epochs, ifg = pinv_ref.shape
    tall = epochs * SUB
    grow = lax.broadcasted_iota(jnp.int32, (tall, epochs), 0) // SUB
    pick = (grow == lax.broadcasted_iota(jnp.int32, (tall, epochs), 1)).astype(BF16)
    tall_inverse = jnp.dot(pick, pinv_ref[...], preferred_element_type=F32).astype(BF16)
    share = ifg // 8
    wide = share * SUB
    here = lax.broadcasted_iota(jnp.int32, (ifg, wide), 0)
    there = lax.broadcasted_iota(jnp.int32, (ifg, wide), 1) // SUB
    diagonal = (lax.broadcasted_iota(jnp.int32, (tall, wide), 0) % SUB) == (
        lax.broadcasted_iota(jnp.int32, (tall, wide), 1) % SUB
    )
    for k in range(8):
        spread = (here == there + src_ref[k] * share).astype(BF16)
        block = jnp.dot(tall_inverse, spread, preferred_element_type=F32)
        w_ref[:, k * wide : (k + 1) * wide] = jnp.where(diagonal, block, 0.0).astype(BF16)
    sx, sy, sz = (0.38, -0.08, 0.92)
    cos_lat, sin_lat = lat_ref[:, 0:1], lat_ref[:, 1:2]
    cos_lon, sin_lon = lon_ref[0:1, :], lon_ref[1:2, :]
    px = cos_lat * cos_lon
    py = cos_lat * sin_lon
    pz = sin_lat + 0.0 * sin_lon
    lever = (py * sz - pz * sy, pz * sx - px * sz, px * sy - py * sx)
    plate = plate_ref[...]
    total = jnp.zeros(plate.shape, F32)
    for p in range(rot_ref.shape[0]):
        along = rot_ref[p, 0] * lever[0] + rot_ref[p, 1] * lever[1] + rot_ref[p, 2] * lever[2]
        total = total + jnp.where(plate == p, along, 0.0)
    rate_ref[...] = total


def rate_kernel(src_ref, weight_ref, place_ref, *refs):
    blocks, (coherent_ref, plate_rate_ref), outs = refs[:8], refs[8:10], refs[10:]
    v_ref, one_ref, two_ref, left_ref, right_ref = outs
    share, rows, cols = blocks[0].shape
    rate = jnp.zeros((rows, cols), F32)
    for k, block in enumerate(blocks):
        for i in range(share):
            rate = rate + weight_ref[src_ref[k] * share + i] * block[i].astype(F32)
    v_ref[...] = coherent_ref[...].astype(F32) * rate - plate_rate_ref[...]
    core, column = place_ref[0], place_ref[1]
    top, low = v_ref[:REACH, :], v_ref[rows - REACH :, :]
    first, last = v_ref[:, :LANES], v_ref[:, cols - LANES :]
    one_ref[...] = jnp.where(core == 0, low, top)
    two_ref[...] = jnp.where(core == 0, top, low)
    left_ref[...] = jnp.where(column == 0, last, first)
    right_ref[...] = jnp.where(column == 0, first, last)


def product_kernel(w_ref, *refs):
    blocks, out_ref = refs[:-1], refs[-1]
    share, rows, cols = blocks[0].shape
    epochs = out_ref.shape[0]
    for t in range(rows // SUB):
        part = slice(t * SUB, (t + 1) * SUB)
        stack = jnp.concatenate([b[:, part, :].reshape(share * SUB, cols) for b in blocks], axis=0)
        series = jnp.dot(w_ref[...], stack, preferred_element_type=F32)
        out_ref[:, part, :] = series.astype(BF16).reshape(epochs, SUB, cols)


def three_parts(value):
    high = value.astype(BF16)
    rest = value - high.astype(F32)
    mid = rest.astype(BF16)
    low = (rest - mid.astype(F32)).astype(BF16)
    return high, mid, low


def banded(shape, axis, start):
    step = lax.broadcasted_iota(jnp.int32, shape, axis) - start
    step = step - lax.broadcasted_iota(jnp.int32, shape, 1 - axis)
    return jnp.where(jnp.abs(step) <= REACH, step, 0).astype(F32).astype(BF16)


def gradient_kernel(place_ref, v_ref, one_ref, two_ref, left_ref, right_ref, rows_ref, cols_ref):
    rows, cols = v_ref.shape
    scale = (REACH * (REACH + 1) * (2 * REACH + 1) // 3) ** -0.5
    core, column = place_ref[0], place_ref[1]
    v = v_ref[...]
    one, two = one_ref[...], two_ref[...]
    above = jnp.where(core == 0, two, one)
    below = jnp.where(core == 0, one, two)
    upright = jnp.concatenate([above, v, below], axis=0)
    taps = banded((rows, rows + 2 * REACH), 1, REACH)
    total = jnp.zeros((rows, cols), F32)
    for part in three_parts(upright):
        total = total + jnp.dot(taps, part, preferred_element_type=F32)
    rows_ref[...] = total * scale
    first, second = left_ref[...], right_ref[...]
    before = jnp.where(column == 0, second, first)
    after = jnp.where(column == 0, first, second)
    sideways = jnp.concatenate([before, v, after], axis=1)
    parts = jnp.concatenate(three_parts(sideways), axis=0)
    taps = banded((3 * LANES, LANES), 0, LANES)
    for c in range(0, cols, LANES):
        found = jnp.dot(parts[:, c : c + 3 * LANES], taps, preferred_element_type=F32)
        found = found[:rows] + found[rows : 2 * rows] + found[2 * rows :]
        cols_ref[:, c : c + LANES] = found * scale


SMEM = pl.BlockSpec(memory_space=pltpu.SMEM)
VMEM = pl.BlockSpec(memory_space=pltpu.VMEM)


def call(kernel, inputs, outputs, flops, moved, **more):
    return pl.pallas_call(
        kernel,
        in_specs=inputs,
        out_shape=outputs,
        cost_estimate=pl.CostEstimate(flops=flops, bytes_accessed=moved, transcendentals=0),
        compiler_params=pltpu.CompilerParams(vmem_limit_bytes=VMEM_BYTES),
        **more,
    )


def shape(*dims, dtype=F32):
    return jax.ShapeDtypeStruct(dims, dtype)


def on_device(phase, pseudo_inverse, rotation, plate_id, coherent):
    share, groups, rows, cols = phase.shape
    epochs, ifg = pseudo_inverse.shape
    grp, row, col = lax.axis_index("grp"), lax.axis_index("row"), lax.axis_index("col")
    x, y, core = grp >> 1, grp & 1, row & 1
    tiles = groups * lax.axis_size("row")
    total_rows, total_cols = tiles * rows, lax.axis_size("col") * cols

    names = ("own",) + EMIT
    sources = {name: partner(name, x, y, core, jnp.where) for name in names}
    blocks = {}
    for name in names:
        block = lax.dynamic_index_in_dim(phase, sources[name], 1, keepdims=False)
        if name != "own":
            block = lax.ppermute(block, ("grp", "row"), swap_pairs(name))
        blocks[name] = block
    src = jnp.stack([sources[name] for name in names]).astype(jnp.int32)
    held = [blocks[name] for name in names]

    steps = jnp.arange(epochs, dtype=F32) - (epochs - 1) / 2.0
    slope = steps / jnp.sqrt(jnp.sum(steps * steps))
    weight = jnp.sum(slope[:, None] * pseudo_inverse.astype(F32), axis=0)
    tile = (grp * lax.axis_size("row") + row) * rows
    lat = jnp.deg2rad(36.0 + 6.0 * (tile.astype(F32) + jnp.arange(rows, dtype=F32) + 0.5) / total_rows)
    lon = jnp.deg2rad(26.0 + 19.0 * ((col * cols).astype(F32) + jnp.arange(cols, dtype=F32) + 0.5) / total_cols)
    lat = jnp.stack([jnp.cos(lat), jnp.sin(lat)], axis=1)
    lon = jnp.stack([jnp.cos(lon), jnp.sin(lon)], axis=0)
    place = jnp.stack([core, col & 1]).astype(jnp.int32)

    tall, deep = epochs * SUB, ifg * SUB
    w, plate_rate = call(
        prep_kernel,
        [SMEM, SMEM, VMEM, VMEM, VMEM, VMEM],
        (shape(tall, deep, dtype=BF16), shape(rows, cols)),
        2 * tall * deep * ifg,
        2 * tall * deep,
    )(src, rotation, pseudo_inverse, lat, lon, plate_id)

    velocity, one, two, left, right = call(
        rate_kernel,
        [SMEM, SMEM, SMEM] + [VMEM] * 10,
        (shape(rows, cols), shape(REACH, cols), shape(REACH, cols), shape(rows, LANES), shape(rows, LANES)),
        2 * ifg * rows * cols,
        2 * ifg * rows * cols,
    )(src, weight, place, *held, coherent, plate_rate)

    one = lax.ppermute(one, ("grp", "row"), row_pairs(tiles, 0))
    two = lax.ppermute(two, ("grp", "row"), row_pairs(tiles, 1))
    left = lax.ppermute(left, "col", row_pairs(lax.axis_size("col"), 0))
    right = lax.ppermute(right, "col", row_pairs(lax.axis_size("col"), 1))

    cut = 3
    displacement = call(
        product_kernel,
        [pl.BlockSpec((tall // cut, deep), lambda e: (e, 0))]
        + [pl.BlockSpec((share, rows, cols), lambda e: (0, 0, 0))] * 8,
        shape(epochs, rows, cols, dtype=BF16),
        2 * epochs * ifg * rows * cols * SUB,
        2 * (ifg + epochs) * rows * cols,
        grid=(cut,),
        out_specs=pl.BlockSpec((epochs // cut, rows, cols), lambda e: (e, 0, 0)),
    )(w, *held)

    grad_rows, grad_cols = call(
        gradient_kernel,
        [SMEM] + [VMEM] * 5,
        (shape(rows, cols), shape(rows, cols)),
        2 * 200 * rows * cols,
        16 * rows * cols,
    )(place, velocity, one, two, left, right)
    return (displacement, grad_rows, grad_cols)


def solution(mesh):
    return jax.shard_map(
        on_device,
        mesh=mesh,
        in_specs=(
            P("grp", None, "row", "col"),
            P(),
            P(),
            P(("grp", "row"), "col"),
            P(("grp", "row"), "col"),
        ),
        out_specs=(
            P(None, ("grp", "row"), "col"),
            P(("grp", "row"), "col"),
            P(("grp", "row"), "col"),
        ),
        check_vma=False,
    )
```

time: 317 us -> 50.8 us (0.16)
  the two profiles are of different devices: /device:TPU:96 before, /device:TPU:102 now
where the time goes in v1:
time: 50.8 us; the launch traced here: 50.7 us
  starting transfers between devices  22.2 us (44%)
  waiting for transfers between devices  16.5 us (32%)
  Pallas kernels  6.81 us (13%)
  local copies, waits for them, and re-layouts  2.69 us (5%)
  between operations  1.46 us (3%)
  other arithmetic  0.98 us (2%)
    ppermute x7, waiting for transfers between devices, on_device(): block = lax.ppermute(block, ('grp', 'row'), swap_pairs(name))  16.3 us
    ppermute x7, starting transfers between devices, on_device(): block = lax.ppermute(block, ('grp', 'row'), swap_pairs(name))  12 us
    ppermute x1, starting transfers between devices, on_device(): right = lax.ppermute(right, 'col', row_pairs(lax.axis_size('col'), 1))  5.93 us
    ppermute x1, starting transfers between devices, on_device(): two = lax.ppermute(two, ('grp', 'row'), row_pairs(tiles, 1))  4.02 us
    pallas_call x1, Pallas kernels, on_device(): call(product_kernel, [pl.BlockSpec((tall // cut, deep), lambda e: (e, 0))...  3.03 us
    squeeze x1, local copies, waits for them, and re-layouts, on_device(): block = lax.dynamic_index_in_dim(phase, sources[name], 1, keepdims=False)  2.5 us
    pallas_call x1, Pallas kernels, on_device(): call(gradient_kernel, [SMEM] + [VMEM] * 5, (shape(rows, cols), shape(rows...  1.46 us
    pallas_call x1, Pallas kernels, on_device(): call(prep_kernel, [SMEM, SMEM, VMEM, VMEM, VMEM, VMEM], (shape(tall, deep...  1.34 us
  transfers between devices with their start and end apart: 11, of which 5 were waited for; matrix products, arithmetic and copies ran while one was open for 2% of the time, Pallas kernels for 9%

profile of v1, /device:TPU:102, one launch (start us, length us, event | category | flops | bytes accessed | tf_op | source)
XLA Modules:
  0.0 50.7 jit_solution(2206170781619749758)
XLA Ops:
  0.7 2.5 %dynamic-slice_bitcast_fusion = (bf16[8,32,512]{2,1,0:T(8,128)(2,1)S(1)}, bf16[8,32,512]{2,1,0:T(8,128)(2,1)S(1)}, bf16[8,32,512]{2,1,0:T(8,128)(2,1)}, bf16[8,3...) fusion(bf16[8,8,32,512]{3,2,1,0:T(8,128)(2,1)} %param.5, ...), kind=kLoop, calls=%fused_computation | loop fusion | bytes 4194336 | tf_op jit(solution)/shard_map/jit(dynamic_index_in_dim)/squeeze | solution.py:192
  3.2 4.0 %collective-permute-start.6 = (bf16[8,32,512]{2,1,0:T(8,128)(2,1)S(1)}, bf16[8,32,512]{2,1,0:T(8,128)(2,1)S(1)}, u32[]{:S(2)}, u32[]{:S(2)}) collective-permute-start(bf16[8,32,512]{2,1,0:T(8,128)(2,1)S(1)} %get-tuple-element.21), channel_id=1, source_target_pairs={{0,160},{8,168},{16,176},{24,184},{32,128},{40,136},{48,144},{56,1... | collective-permute-start | bytes 786440 | tf_op jit(solution)/shard_map/ppermute | solution.py:194
  7.2 1.9 %collective-permute-start.4 = (bf16[8,32,512]{2,1,0:T(8,128)(2,1)S(1)}, bf16[8,32,512]{2,1,0:T(8,128)(2,1)S(1)}, u32[]{:S(2)}, u32[]{:S(2)}) collective-permute-start(bf16[8,32,512]{2,1,0:T(8,128)(2,1)S(1)} %get-tuple-element.22), channel_id=1, source_target_pairs={{0,224},{8,104},{16,240},{24,120},{32,192},{40,72},{48,208},{56,88... | collective-permute-start | bytes 786440 | tf_op jit(solution)/shard_map/ppermute | solution.py:194
  9.1 0.3 collective-permute-start.3
  9.4 2.9 %collective-permute-start.2 = (bf16[8,32,512]{2,1,0:T(8,128)(2,1)S(1)}, bf16[8,32,512]{2,1,0:T(8,128)(2,1)S(1)}, u32[]{:S(2)}, u32[]{:S(2)}) collective-permute-start(bf16[8,32,512]{2,1,0:T(8,128)(2,1)S(1)} %get-tuple-element.24), channel_id=1, source_target_pairs={{0,32},{8,40},{16,48},{24,56},{32,0},{40,8},{48,16},{56,24},{64,96... | collective-permute-start | bytes 786440 | tf_op jit(solution)/shard_map/ppermute | solution.py:194
  12.3 1.8 %collective-permute-start.1 = (bf16[8,32,512]{2,1,0:T(8,128)(2,1)S(1)}, bf16[8,32,512]{2,1,0:T(8,128)(2,1)S(1)}, u32[]{:S(2)}, u32[]{:S(2)}) collective-permute-start(bf16[8,32,512]{2,1,0:T(8,128)(2,1)S(1)} %get-tuple-element.25), channel_id=1, source_target_pairs={{0,96},{8,232},{16,112},{24,248},{32,64},{40,200},{48,80},{56,216}... | collective-permute-start | bytes 786440 | tf_op jit(solution)/shard_map/ppermute | solution.py:194
  14.1 0.1 fusion.3
  14.1 0.6 %multiply_reduce_fusion.1 = f32[]{:T(128)} fusion(), kind=kLoop, calls=%fused_computation.15 | loop fusion | flops 143 | bytes 4 | tf_op jit(solution)/shard_map/reduce_sum | solution.py:200
  15.5 0.1 fusion
  15.6 2.2 %collective-permute-done.6.refs_7_ = bf16[8,32,512]{2,1,0:T(8,128)(2,1)S(1)} collective-permute-done((bf16[8,32,512]{2,1,0:T(8,128)(2,1)S(1)}, bf16[8,32,512]{2,1,0:T(8,128)(2,1)S(1)}, u32[]{:S(2)}, u32[]{:S(2)}) %collective-permute-start.6) | collective-permute-done | bytes 262176 | tf_op jit(solution)/shard_map/ppermute | solution.py:194
  17.8 1.1 %collective-permute-start = (bf16[8,32,512]{2,1,0:T(8,128)(2,1)S(1)}, bf16[8,32,512]{2,1,0:T(8,128)(2,1)S(1)}, u32[]{:S(2)}, u32[]{:S(2)}) collective-permute-start(bf16[8,32,512]{2,1,0:T(8,128)(2,1)S(1)} %get-tuple-element.26), channel_id=1, source_target_pairs={{0,64},{8,200},{16,80},{24,216},{32,96},{40,232},{48,112},{56,248}... | collective-permute-start | bytes 786440 | tf_op jit(solution)/shard_map/ppermute | solution.py:194
  18.9 8.2 %collective-permute-done.4.refs_5_ = bf16[8,32,512]{2,1,0:T(8,128)(2,1)S(1)} collective-permute-done((bf16[8,32,512]{2,1,0:T(8,128)(2,1)S(1)}, bf16[8,32,512]{2,1,0:T(8,128)(2,1)S(1)}, u32[]{:S(2)}, u32[]{:S(2)}) %collective-permute-start.4) | collective-permute-done | bytes 262176 | tf_op jit(solution)/shard_map/ppermute | solution.py:194
  27.1 0.0 collective-permute-start.5
  27.1 0.1 copy.8.lat_ref
  27.2 0.1 stack.54.src_ref
  27.3 1.3 %shard_map.76 = (bf16[768,1024]{1,0:T(8,128)(2,1)S(1)}, f32[32,512]{1,0:T(8,128)S(1)}) custom-call(s32[8]{0:T(128)S(1)} %stack.54.src_ref, f32[4,3]{1,0:T(4,128)S(1)} %copy-done.3, bf16[48,64]{1,0:T(8,128)(2,1)S(1)} %copy-done.1, f32[32,2]{1,0:T(8,128)S(1)} %copy.8.lat_ref, f32[2,512]{1,0:T(2,128)S(1)} %pad_maximum_fusion.lon_ref, s32[32,512]{1,0:T(8,128)S(1)} %copy-done.2), custom_call_target="tpu_custom_call" | custom-call | flops 100663296 | bytes 1572864 | tf_op jit(solution)/shard_map/pallas_call | solution.py:210
  28.6 0.1 pad_add_fusion.place_ref
  28.7 0.1 multiply_reduce_fusion.weight_ref
  28.8 0.0 collective-permute-done.3.refs_4_
  28.8 3.2 %collective-permute-done.2.refs_3_ = bf16[8,32,512]{2,1,0:T(8,128)(2,1)S(1)} collective-permute-done((bf16[8,32,512]{2,1,0:T(8,128)(2,1)S(1)}, bf16[8,32,512]{2,1,0:T(8,128)(2,1)S(1)}, u32[]{:S(2)}, u32[]{:S(2)}) %collective-permute-start.2) | collective-permute-done | bytes 262176 | tf_op jit(solution)/shard_map/ppermute | solution.py:194
  32.0 0.0 collective-permute-done.1.refs_2_
  32.0 0.0 collective-permute-done.refs_1_
  32.0 2.6 %collective-permute-done.5.refs_6_ = bf16[8,32,512]{2,1,0:T(8,128)(2,1)S(1)} collective-permute-done((bf16[8,32,512]{2,1,0:T(8,128)(2,1)S(1)}, bf16[8,32,512]{2,1,0:T(8,128)(2,1)S(1)}, u32[]{:S(2)}, u32[]{:S(2)}) %collective-permute-start.5) | collective-permute-done | bytes 262176 | tf_op jit(solution)/shard_map/ppermute | solution.py:194
  34.6 1.0 %shard_map.78 = (f32[32,512]{1,0:T(8,128)S(1)}, f32[16,512]{1,0:T(8,128)S(1)}, f32[16,512]{1,0:T(8,128)S(1)}, f32[32,128]{1,0:T(8,128)S(1)}, f32[32,128]{1,0:T(8,128)S(1)}) custom-call(s32[8]{0:T(128)S(1)} %stack.54.src_ref, f32[64]{0:T(128)S(1)} %multiply_reduce_fusion.weight_ref, s32[2]{0:T(128)S(1)} %pad_add_fusion.place_ref, ...), custom_call_target="tpu_custom_call" | custom-call | flops 2097152 | bytes 2097152 | tf_op jit(solution)/shard_map/pallas_call | solution.py:218
  35.6 0.2 collective-permute-start.9
  35.8 5.9 %collective-permute-start.10 = (f32[32,128]{1,0:T(8,128)S(1)}, f32[32,128]{1,0:T(8,128)S(1)}, u32[]{:S(2)}, u32[]{:S(2)}) collective-permute-start(f32[32,128]{1,0:T(8,128)S(1)} %get-tuple-element.18), channel_id=1, source_target_pairs={{1,2},{2,1},{3,4},{4,3},{5,6},{6,5},{9,10},{10,9},{11,12},{12,11},... | collective-permute-start | bytes 49160 | tf_op jit(solution)/shard_map/ppermute | solution.py:229
  41.8 0.1 collective-permute-start.7
  41.9 4.0 %collective-permute-start.8 = (f32[16,512]{1,0:T(8,128)S(1)}, f32[16,512]{1,0:T(8,128)S(1)}, u32[]{:S(2)}, u32[]{:S(2)}) collective-permute-start(f32[16,512]{1,0:T(8,128)S(1)} %get-tuple-element.16), channel_id=1, source_target_pairs={{8,16},{16,8},{24,32},{32,24},{40,48},{48,40},{56,64},{64,56},{72,... | collective-permute-start | bytes 98312 | tf_op jit(solution)/shard_map/ppermute | solution.py:227
  45.9 3.0 %shard_map.77 = bf16[48,32,512]{2,1,0:T(8,128)(2,1)} custom-call(bf16[768,1024]{1,0:T(8,128)(2,1)S(1)} %get-tuple-element.12.w_ref, bf16[8,32,512]{2,1,0:T(8,128)(2,1)S(1)} %get-tuple-element.27.refs_0_, bf16[8,32,512]{2,1,0:T(8,128)(2,1)S(1)} %collective-permute-done.refs_1_, bf16[8,32,512]{2,1,0:T(8,128)(2,1)S(1)} %collective-permute-done.1.refs_2_, ...), custom_call_target="tpu_custom_call" | custom-call | flops 1610612736 | bytes 3670016 | tf_op jit(solution)/shard_map/pallas_call | solution.py:232
  48.9 0.0 collective-permute-done.9.left_ref
  48.9 0.3 collective-permute-done.8.two_ref
  49.2 1.5 %shard_map.79 = (f32[32,512]{1,0:T(8,128)}, f32[32,512]{1,0:T(8,128)}) custom-call(s32[2]{0:T(128)S(1)} %pad_add_fusion.place_ref, f32[32,512]{1,0:T(8,128)S(1)} %get-tuple-element.14.v_ref, f32[16,512]{1,0:T(8,128)S(1)} %collective-permute-done.7.one_ref, f32[16,512]{1,0:T(8,128)S(1)} %collective-permute-done.8.two_ref, ...), custom_call_target="tpu_custom_call" | custom-call | flops 6553600 | bytes 262144 | tf_op jit(solution)/shard_map/pallas_call | solution.py:243
  (13 shorter events, 0.1 us)
Async XLA Ops:
  0.7 26.6 %copy-start.1 = (bf16[48,64]{1,0:T(8,128)(2,1)S(1)}, bf16[48,64]{1,0:T(8,128)(2,1)}, u32[]{:S(2)}) copy-start(bf16[48,64]{1,0:T(8,128)(2,1)} %pinv_ref.1) | copy-start | bytes 18436
  0.7 26.6 %copy-start.2 = (s32[32,512]{1,0:T(8,128)S(1)}, s32[32,512]{1,0:T(8,128)}, u32[]{:S(2)}) copy-start(s32[32,512]{1,0:T(8,128)} %plate_ref.1) | copy-start | bytes 196612
  0.7 26.6 %copy-start.3 = (f32[4,3]{1,0:T(4,128)S(1)}, f32[4,3]{1,0:T(4,128)}, u32[]{:S(2)}) copy-start(f32[4,3]{1,0:T(4,128)} %rot_ref.1) | copy-start | bytes 148
  0.7 33.9 %copy-start = (s32[32,512]{1,0:T(8,128)S(1)}, s32[32,512]{1,0:T(8,128)}, u32[]{:S(2)}) copy-start(s32[32,512]{1,0:T(8,128)} %refs_8_.1) | copy-start | bytes 196612
  3.2 14.6 %collective-permute-start.6 = (bf16[8,32,512]{2,1,0:T(8,128)(2,1)S(1)}, bf16[8,32,512]{2,1,0:T(8,128)(2,1)S(1)}, u32[]{:S(2)}, u32[]{:S(2)}) collective-permute-start(bf16[8,32,512]{2,1,0:T(8,128)(2,1)S(1)} %get-tuple-element.21), channel_id=1, source_target_pairs={{0,160},{8,168},{16,176},{24,184},{32,128},{40,136},{48,144},{56,1... | collective-permute-start | bytes 786440 | tf_op jit(solution)/shard_map/ppermute | solution.py:194
  7.2 19.8 %collective-permute-start.4 = (bf16[8,32,512]{2,1,0:T(8,128)(2,1)S(1)}, bf16[8,32,512]{2,1,0:T(8,128)(2,1)S(1)}, u32[]{:S(2)}, u32[]{:S(2)}) collective-permute-start(bf16[8,32,512]{2,1,0:T(8,128)(2,1)S(1)} %get-tuple-element.22), channel_id=1, source_target_pairs={{0,224},{8,104},{16,240},{24,120},{32,192},{40,72},{48,208},{56,88... | collective-permute-start | bytes 786440 | tf_op jit(solution)/shard_map/ppermute | solution.py:194
  9.1 19.7 %collective-permute-start.3 = (bf16[8,32,512]{2,1,0:T(8,128)(2,1)}, bf16[8,32,512]{2,1,0:T(8,128)(2,1)S(1)}, u32[]{:S(2)}, u32[]{:S(2)}) collective-permute-start(bf16[8,32,512]{2,1,0:T(8,128)(2,1)} %get-tuple-element.23), channel_id=1, source_target_pairs={{0,128},{8,136},{16,144},{24,152},{32,160},{40,168},{48,176},{56,1... | collective-permute-start | bytes 786440 | tf_op jit(solution)/shard_map/ppermute | solution.py:194
  9.4 22.6 %collective-permute-start.2 = (bf16[8,32,512]{2,1,0:T(8,128)(2,1)S(1)}, bf16[8,32,512]{2,1,0:T(8,128)(2,1)S(1)}, u32[]{:S(2)}, u32[]{:S(2)}) collective-permute-start(bf16[8,32,512]{2,1,0:T(8,128)(2,1)S(1)} %get-tuple-element.24), channel_id=1, source_target_pairs={{0,32},{8,40},{16,48},{24,56},{32,0},{40,8},{48,16},{56,24},{64,96... | collective-permute-start | bytes 786440 | tf_op jit(solution)/shard_map/ppermute | solution.py:194
  12.3 19.7 %collective-permute-start.1 = (bf16[8,32,512]{2,1,0:T(8,128)(2,1)S(1)}, bf16[8,32,512]{2,1,0:T(8,128)(2,1)S(1)}, u32[]{:S(2)}, u32[]{:S(2)}) collective-permute-start(bf16[8,32,512]{2,1,0:T(8,128)(2,1)S(1)} %get-tuple-element.25), channel_id=1, source_target_pairs={{0,96},{8,232},{16,112},{24,248},{32,64},{40,200},{48,80},{56,216}... | collective-permute-start | bytes 786440 | tf_op jit(solution)/shard_map/ppermute | solution.py:194
  17.8 14.2 %collective-permute-start = (bf16[8,32,512]{2,1,0:T(8,128)(2,1)S(1)}, bf16[8,32,512]{2,1,0:T(8,128)(2,1)S(1)}, u32[]{:S(2)}, u32[]{:S(2)}) collective-permute-start(bf16[8,32,512]{2,1,0:T(8,128)(2,1)S(1)} %get-tuple-element.26), channel_id=1, source_target_pairs={{0,64},{8,200},{16,80},{24,216},{32,96},{40,232},{48,112},{56,248}... | collective-permute-start | bytes 786440 | tf_op jit(solution)/shard_map/ppermute | solution.py:194
  27.1 7.6 %collective-permute-start.5 = (bf16[8,32,512]{2,1,0:T(8,128)(2,1)S(1)}, bf16[8,32,512]{2,1,0:T(8,128)(2,1)S(1)}, u32[]{:S(2)}, u32[]{:S(2)}) collective-permute-start(bf16[8,32,512]{2,1,0:T(8,128)(2,1)S(1)} %get-tuple-element.28), channel_id=1, source_target_pairs={{0,192},{8,72},{16,208},{24,88},{32,224},{40,104},{48,240},{56,120... | collective-permute-start | bytes 786440 | tf_op jit(solution)/shard_map/ppermute | solution.py:194
  35.6 13.3 %collective-permute-start.9 = (f32[32,128]{1,0:T(8,128)S(1)}, f32[32,128]{1,0:T(8,128)S(1)}, u32[]{:S(2)}, u32[]{:S(2)}) collective-permute-start(f32[32,128]{1,0:T(8,128)S(1)} %get-tuple-element.17), channel_id=1, source_target_pairs={{0,1},{1,0},{2,3},{3,2},{4,5},{5,4},{6,7},{7,6},{8,9},{9,8},{10,11... | collective-permute-start | bytes 49160 | tf_op jit(solution)/shard_map/ppermute | solution.py:228
  35.8 13.1 %collective-permute-start.10 = (f32[32,128]{1,0:T(8,128)S(1)}, f32[32,128]{1,0:T(8,128)S(1)}, u32[]{:S(2)}, u32[]{:S(2)}) collective-permute-start(f32[32,128]{1,0:T(8,128)S(1)} %get-tuple-element.18), channel_id=1, source_target_pairs={{1,2},{2,1},{3,4},{4,3},{5,6},{6,5},{9,10},{10,9},{11,12},{12,11},... | collective-permute-start | bytes 49160 | tf_op jit(solution)/shard_map/ppermute | solution.py:229
  41.8 7.2 %collective-permute-start.7 = (f32[16,512]{1,0:T(8,128)S(1)}, f32[16,512]{1,0:T(8,128)S(1)}, u32[]{:S(2)}, u32[]{:S(2)}) collective-permute-start(f32[16,512]{1,0:T(8,128)S(1)} %get-tuple-element.15), channel_id=1, source_target_pairs={{0,8},{8,0},{16,24},{24,16},{32,40},{40,32},{48,56},{56,48},{64,72... | collective-permute-start | bytes 98312 | tf_op jit(solution)/shard_map/ppermute | solution.py:226
  41.9 7.3 %collective-permute-start.8 = (f32[16,512]{1,0:T(8,128)S(1)}, f32[16,512]{1,0:T(8,128)S(1)}, u32[]{:S(2)}, u32[]{:S(2)}) collective-permute-start(f32[16,512]{1,0:T(8,128)S(1)} %get-tuple-element.16), channel_id=1, source_target_pairs={{8,16},{16,8},{24,32},{32,24},{40,48},{48,40},{56,64},{64,56},{72,... | collective-permute-start | bytes 98312 | tf_op jit(solution)/shard_map/ppermute | solution.py:227

commit v2 on v1

v2 whole, which is shorter than its diff:
```python
import math

import jax
import jax.numpy as jnp
from jax import lax
from jax.experimental import pallas as pl
from jax.experimental.pallas import tpu as pltpu
from jax.sharding import PartitionSpec as P

REACH = 16
SUB = 16
LANES = 128
F32 = jnp.float32
BF16 = jnp.bfloat16
VMEM_BYTES = 40 << 20
CUT = 16

FLOWS = {
    "own": (0, 0),
    "D2": (2, 1),
    "Da": ("a", 1),
    "Db": ("b", 1),
    "X2": (2, 0),
    "Y2": (0, 1),
    "Xa": ("a", 0),
    "Xb": ("b", 0),
}
EARLY = ("D2", "Db")
LATE = ("X2", "Y2", "Da", "Xa", "Xb")
ORDER = ("own",) + EARLY + LATE
STARTS = EARLY + LATE


def along_x(step, x, core, pick):
    if step == "a":
        return pick(((x + core) & 1) == 0, 1, 3)
    if step == "b":
        return pick(((x + core) & 1) == 0, 3, 1)
    return step


def partner(flow, x, y, core, pick):
    step, turn = FLOWS[flow]
    return (((x + along_x(step, x, core, pick)) & 3) << 1) + ((y + turn) & 1)


def swap_pairs(flow):
    def choose(test, first, second):
        return first if test else second

    pairs = []
    for grp in range(8):
        for row in range(4):
            other = partner(flow, grp // 2, grp % 2, row % 2, choose)
            pairs.append((grp * 4 + row, other * 4 + row))
    return pairs


def ring_pairs(count, first):
    pairs = []
    for low in range(first, count, 2):
        high = (low + 1) % count
        pairs += [(low, high), (high, low)]
    return pairs


def three_parts(value):
    high = value.astype(BF16)
    rest = value - high.astype(F32)
    mid = rest.astype(BF16)
    low = (rest - mid.astype(F32)).astype(BF16)
    return high, mid, low


def rate_weights(pinv_ref, weight_ref):
    epochs, ifg = pinv_ref.shape
    steps = lax.broadcasted_iota(jnp.int32, (epochs, LANES), 0).astype(F32) - (epochs - 1) / 2.0
    slope = steps * (epochs * (epochs * epochs - 1) / 12.0) ** -0.5
    total = jnp.zeros((ifg, LANES), F32)
    for part in three_parts(slope):
        total = total + lax.dot_general(
            pinv_ref[...], part, (((0,), (0,)), ((), ())), preferred_element_type=F32
        )
    weight_ref[...] = total


def prep_kernel(rot_ref, pinv_ref, plate_ref, w_ref, rate_ref, weight_ref):
    rate_weights(pinv_ref, weight_ref)
    epochs, ifg = pinv_ref.shape
    rows, cols = plate_ref.shape
    x, y, core = place_here()
    tall = epochs * SUB
    grow = lax.broadcasted_iota(jnp.int32, (tall, epochs), 0) // SUB
    pick = (grow == lax.broadcasted_iota(jnp.int32, (tall, epochs), 1)).astype(BF16)
    tall_inverse = jnp.dot(pick, pinv_ref[...], preferred_element_type=F32).astype(BF16)
    share = ifg // 8
    wide = share * SUB
    here = lax.broadcasted_iota(jnp.int32, (ifg, wide), 0)
    there = lax.broadcasted_iota(jnp.int32, (ifg, wide), 1) // SUB
    diagonal = (lax.broadcasted_iota(jnp.int32, (tall, wide), 0) % SUB) == (
        lax.broadcasted_iota(jnp.int32, (tall, wide), 1) % SUB
    )
    for k, name in enumerate(ORDER):
        source = partner(name, x, y, core, jnp.where)
        spread = (here == there + source * share).astype(BF16)
        block = jnp.dot(tall_inverse, spread, preferred_element_type=F32)
        w_ref[:, k * wide : (k + 1) * wide] = jnp.where(diagonal, block, 0.0).astype(BF16)
    tile = lax.axis_index("grp") * lax.axis_size("row") + lax.axis_index("row")
    total_rows = rows * lax.axis_size("grp") * lax.axis_size("row")
    total_cols = cols * lax.axis_size("col")
    down = lax.broadcasted_iota(jnp.int32, (rows, LANES), 0) + tile * rows
    over = lax.broadcasted_iota(jnp.int32, (8, cols), 1) + lax.axis_index("col") * cols
    lat = (36.0 + 6.0 * (down.astype(F32) + 0.5) / total_rows) * (math.pi / 180.0)
    lon = (26.0 + 19.0 * (over.astype(F32) + 0.5) / total_cols) * (math.pi / 180.0)
    cos_lat, sin_lat = jnp.cos(lat)[:, 0:1], jnp.sin(lat)[:, 0:1]
    cos_lon, sin_lon = jnp.cos(lon)[0:1, :], jnp.sin(lon)[0:1, :]
    sx, sy, sz = (0.38, -0.08, 0.92)
    px = cos_lat * cos_lon
    py = cos_lat * sin_lon
    pz = sin_lat + 0.0 * sin_lon
    lever = (py * sz - pz * sy, pz * sx - px * sz, px * sy - py * sx)
    plate = plate_ref[...]
    total = jnp.zeros(plate.shape, F32)
    for p in range(rot_ref.shape[0]):
        along = jnp.zeros(plate.shape, F32)
        for k in range(3):
            along = along + rot_ref[p : p + 1, k : k + 1] * lever[k]
        total = total + jnp.where(plate == p, along, 0.0)
    rate_ref[...] = total


def weighted(total, block, weight_ref, source):
    share, _, cols = block.shape
    for i in range(share):
        row = weight_ref[pl.ds(source * share + i, 1), :]
        total = total + jnp.concatenate([row] * (cols // LANES), axis=1) * block[i].astype(F32)
    return total


def place_here():
    grp, row = lax.axis_index("grp"), lax.axis_index("row")
    return grp >> 1, grp & 1, row & 1


def rate_kernel(weight_ref, *refs):
    outs = refs[-5:]
    v_ref, one_ref, two_ref, left_ref, right_ref = outs
    coherent_ref, plate_rate_ref = refs[-7:-5]
    blocks = refs[:-7]
    rows, cols = v_ref.shape
    rate = jnp.zeros((rows, cols), F32)
    x, y, core = place_here()
    for name, block in zip(ORDER, blocks):
        rate = weighted(rate, block, weight_ref, partner(name, x, y, core, jnp.where))
    v_ref[...] = coherent_ref[...].astype(F32) * rate - plate_rate_ref[...]
    column = lax.axis_index("col") & 1
    top, low = v_ref[:REACH, :], v_ref[rows - REACH :, :]
    first, last = v_ref[:, :LANES], v_ref[:, cols - LANES :]
    one_ref[...] = jnp.where(core == 0, low, top)
    two_ref[...] = jnp.where(core == 0, top, low)
    left_ref[...] = jnp.where(column == 0, last, first)
    right_ref[...] = jnp.where(column == 0, first, last)


def stacked(blocks, part):
    share, _, cols = blocks[0].shape
    return jnp.concatenate([b[:, part, :].reshape(share * SUB, cols) for b in blocks], axis=0)


def series_kernel(w_ref, *refs):
    blocks, out_ref = refs[:-1], refs[-1]
    epochs, rows, cols = out_ref.shape
    deep = len(blocks) * blocks[0].shape[0] * SUB
    for t in range(rows // SUB):
        part = slice(t * SUB, (t + 1) * SUB)
        stack = stacked(blocks, part)
        for e in range(0, epochs, CUT):
            found = jnp.dot(w_ref[e * SUB : (e + CUT) * SUB, :deep], stack, preferred_element_type=F32)
            out_ref[e : e + CUT, part, :] = found.reshape(CUT, SUB, cols)


def displacement_kernel(w_ref, series_ref, *refs):
    blocks, (out_ref, held_ref, sem) = refs[:-3], refs[-3:]
    epochs, rows, cols = held_ref.shape
    deep = len(blocks) * blocks[0].shape[0] * SUB
    start = w_ref.shape[1] - deep
    parts = [slice(t * SUB, (t + 1) * SUB) for t in range(rows // SUB)]
    stacks = [stacked(blocks, part) for part in parts]
    copies = []
    for n, e in enumerate(range(0, epochs, CUT)):
        for part, stack in zip(parts, stacks):
            found = jnp.dot(w_ref[e * SUB : (e + CUT) * SUB, start:], stack, preferred_element_type=F32)
            found = found.reshape(CUT, SUB, cols) + series_ref[e : e + CUT, part, :]
            held_ref[e : e + CUT, part, :] = found.astype(BF16)
        copies.append(pltpu.make_async_copy(held_ref.at[e : e + CUT], out_ref.at[e : e + CUT], sem.at[n]))
        copies[-1].start()
    for copy in copies:
        copy.wait()


def banded(shape, axis, start):
    step = lax.broadcasted_iota(jnp.int32, shape, axis) - start
    step = step - lax.broadcasted_iota(jnp.int32, shape, 1 - axis)
    return jnp.where(jnp.abs(step) <= REACH, step, 0).astype(F32).astype(BF16)


def gradient_kernel(v_ref, right_ref, two_ref, left_ref, one_ref, rows_ref, cols_ref):
    rows, cols = v_ref.shape
    scale = (REACH * (REACH + 1) * (2 * REACH + 1) // 3) ** -0.5
    tile = lax.axis_index("grp") * lax.axis_size("row") + lax.axis_index("row")
    tiles = lax.axis_size("grp") * lax.axis_size("row")
    place, columns = lax.axis_index("col"), lax.axis_size("col")
    core, column = tile & 1, place & 1
    v = v_ref[...]
    one, two = one_ref[...], two_ref[...]
    above = jnp.where(tile == 0, 0.0, jnp.where(core == 0, two, one))
    below = jnp.where(tile == tiles - 1, 0.0, jnp.where(core == 0, one, two))
    upright = jnp.concatenate([above, v, below], axis=0)
    taps = banded((rows, rows + 2 * REACH), 1, REACH)
    total = jnp.zeros((rows, cols), F32)
    for part in three_parts(upright):
        total = total + jnp.dot(taps, part, preferred_element_type=F32)
    rows_ref[...] = total * scale
    first, second = left_ref[...], right_ref[...]
    before = jnp.where(place == 0, 0.0, jnp.where(column == 0, second, first))
    after = jnp.where(place == columns - 1, 0.0, jnp.where(column == 0, first, second))
    sideways = jnp.concatenate([before, v, after], axis=1)
    parts = jnp.concatenate(three_parts(sideways), axis=0)
    taps = banded((3 * LANES, LANES), 0, LANES)
    for c in range(0, cols, LANES):
        found = jnp.dot(parts[:, c : c + 3 * LANES], taps, preferred_element_type=F32)
        found = found[:rows] + found[rows : 2 * rows] + found[2 * rows :]
        cols_ref[:, c : c + LANES] = found * scale


VMEM = pl.BlockSpec(memory_space=pltpu.VMEM)


def call(kernel, inputs, outputs, flops, moved, limit=VMEM_BYTES, **more):
    return pl.pallas_call(
        kernel,
        in_specs=inputs,
        out_shape=outputs,
        cost_estimate=pl.CostEstimate(flops=flops, bytes_accessed=moved, transcendentals=0),
        compiler_params=pltpu.CompilerParams(vmem_limit_bytes=limit),
        **more,
    )


def shape(*dims, dtype=F32):
    return jax.ShapeDtypeStruct(dims, dtype)


def on_device(phase, pseudo_inverse, rotation, plate_id, coherent):
    share, groups, rows, cols = phase.shape
    epochs, ifg = pseudo_inverse.shape
    tiles = groups * lax.axis_size("row")
    both = ("grp", "row")
    tall, deep = epochs * SUB, ifg * SUB
    x, y, core = place_here()
    def cut(name):
        return lax.dynamic_index_in_dim(phase, partner(name, x, y, core, jnp.where), 1, keepdims=False)

    sent = {name: cut(name) for name in STARTS}
    got = {name: lax.ppermute(sent[name], both, swap_pairs(name)) for name in STARTS}
    later = (got[STARTS[0]], phase, pseudo_inverse, rotation, plate_id, coherent)
    got[STARTS[0]], phase, pseudo_inverse, rotation, plate_id, coherent = lax.optimization_barrier(later)
    early = [cut("own")] + [got[name] for name in EARLY]
    late = [got[name] for name in LATE]

    w, plate_rate, weight = call(
        prep_kernel,
        [VMEM, VMEM, VMEM],
        (shape(tall, deep, dtype=BF16), shape(rows, cols), shape(ifg, LANES)),
        2 * tall * deep * ifg,
        2 * tall * deep,
    )(rotation, pseudo_inverse, plate_id)

    series = call(
        series_kernel,
        [VMEM] * (1 + len(early)),
        shape(epochs, rows, cols),
        2 * epochs * ifg * rows * cols * SUB,
        2 * ifg * rows * cols,
    )(w, *early)
    series, plate_rate = lax.optimization_barrier((series, plate_rate))

    velocity, one, two, left, right = call(
        rate_kernel,
        [VMEM] * (3 + len(ORDER)),
        (shape(rows, cols), shape(REACH, cols), shape(REACH, cols), shape(rows, LANES), shape(rows, LANES)),
        2 * ifg * rows * cols,
        2 * ifg * rows * cols,
    )(weight, *early, *late, coherent, plate_rate)

    right = lax.ppermute(right, "col", ring_pairs(lax.axis_size("col"), 1))
    two = lax.ppermute(two, both, ring_pairs(tiles, 1))
    left = lax.ppermute(left, "col", ring_pairs(lax.axis_size("col"), 0))
    one = lax.ppermute(one, both, ring_pairs(tiles, 0))

    displacement = call(
        displacement_kernel,
        [VMEM] * (2 + len(late)),
        shape(epochs, rows, cols, dtype=BF16),
        epochs * ifg * rows * cols * SUB,
        2 * epochs * rows * cols,
        out_specs=pl.BlockSpec(memory_space=pl.ANY),
        scratch_shapes=[
            pltpu.VMEM((epochs, rows, cols), BF16),
            pltpu.SemaphoreType.DMA((epochs // CUT,)),
        ],
    )(w, series, *late)

    grad_rows, grad_cols = call(
        gradient_kernel,
        [VMEM] * 5,
        (shape(rows, cols), shape(rows, cols)),
        2 * 200 * rows * cols,
        16 * rows * cols,
    )(velocity, right, two, left, one)
    return (displacement, grad_rows, grad_cols)


def solution(mesh):
    return jax.shard_map(
        on_device,
        mesh=mesh,
        in_specs=(
            P("grp", None, "row", "col"),
            P(),
            P(),
            P(("grp", "row"), "col"),
            P(("grp", "row"), "col"),
        ),
        out_specs=(
            P(None, ("grp", "row"), "col"),
            P(("grp", "row"), "col"),
            P(("grp", "row"), "col"),
        ),
        check_vma=False,
    )
```

time: 50.8 us -> 48.7 us (0.959)
  the two profiles are of different devices: /device:TPU:102 before, /device:TPU:32 now
where the time goes in v2:
time: 48.7 us; the launch traced here: 48.5 us
  starting transfers between devices  30.5 us (63%)
  waiting for transfers between devices  9.18 us (19%)
  Pallas kernels  5.45 us (11%)
  local copies, waits for them, and re-layouts  2.64 us (5%)
  between operations  0.79 us (2%)
    ppermute x7, starting transfers between devices, on_device(): lax.ppermute(sent[name], both, swap_pairs(name))  18.7 us
    ppermute x7, waiting for transfers between devices, on_device(): lax.ppermute(sent[name], both, swap_pairs(name))  9.17 us
    ppermute x1, starting transfers between devices, on_device(): two = lax.ppermute(two, both, ring_pairs(tiles, 1))  5.72 us
    ppermute x1, starting transfers between devices, on_device(): left = lax.ppermute(left, 'col', ring_pairs(lax.axis_size('col'), 0))  4.05 us
    squeeze x2, local copies, waits for them, and re-layouts, cut(): lax.dynamic_index_in_dim(phase, partner(name, x, y, core, jnp.where), 1,...  2.62 us
    pallas_call x1, Pallas kernels, on_device(): call(displacement_kernel, [VMEM] * (2 + len(late)), shape(epochs, rows, c...  2.21 us
    ppermute x1, starting transfers between devices, on_device(): right = lax.ppermute(right, 'col', ring_pairs(lax.axis_size('col'), 1))  1.92 us
  transfers between devices with their start and end apart: 11, of which 5 were waited for; matrix products, arithmetic and copies ran while one was open for 2% of the time, Pallas kernels for 8%

profile of v2, /device:TPU:32, one launch (start us, length us, event | category | flops | bytes accessed | tf_op | source)
XLA Modules:
  0.0 48.5 jit_solution(7044148077530555139)
XLA Ops:
  0.6 0.0 copy-start.2
  0.7 1.6 %dynamic-slice_bitcast_fusion = (bf16[8,32,512]{2,1,0:T(8,128)(2,1)S(1)}, bf16[8,32,512]{2,1,0:T(8,128)(2,1)S(1)}, bf16[8,32,512]{2,1,0:T(8,128)(2,1)S(1)}, bf16...) fusion(bf16[8,8,32,512]{3,2,1,0:T(8,128)(2,1)} %param.5, ...), kind=kLoop, calls=%fused_computation | loop fusion | bytes 3670044 | tf_op jit(solution)/shard_map/jit(dynamic_index_in_dim)/squeeze | solution.py:262
  2.3 5.7 %collective-permute-start = (bf16[8,32,512]{2,1,0:T(8,128)(2,1)S(1)}, bf16[8,32,512]{2,1,0:T(8,128)(2,1)S(1)}, u32[]{:S(2)}, u32[]{:S(2)}) collective-permute-start(bf16[8,32,512]{2,1,0:T(8,128)(2,1)S(1)} %get-tuple-element.44), channel_id=1, source_target_pairs={{0,160},{8,168},{16,176},{24,184},{32,128},{40,136},{48,144},{56,1... | collective-permute-start | bytes 786440 | tf_op jit(solution)/shard_map/ppermute | solution.py:265
  8.1 0.9 %collective-permute-start.1 = (bf16[8,32,512]{2,1,0:T(8,128)(2,1)S(1)}, bf16[8,32,512]{2,1,0:T(8,128)(2,1)S(1)}, u32[]{:S(2)}, u32[]{:S(2)}) collective-permute-start(bf16[8,32,512]{2,1,0:T(8,128)(2,1)S(1)} %get-tuple-element.43), channel_id=1, source_target_pairs={{0,224},{8,104},{16,240},{24,120},{32,192},{40,72},{48,208},{56,88... | collective-permute-start | bytes 786440 | tf_op jit(solution)/shard_map/ppermute | solution.py:265
  9.0 1.5 %collective-permute-start.2 = (bf16[8,32,512]{2,1,0:T(8,128)(2,1)S(1)}, bf16[8,32,512]{2,1,0:T(8,128)(2,1)S(1)}, u32[]{:S(2)}, u32[]{:S(2)}) collective-permute-start(bf16[8,32,512]{2,1,0:T(8,128)(2,1)S(1)} %get-tuple-element.42), channel_id=1, source_target_pairs={{0,128},{8,136},{16,144},{24,152},{32,160},{40,168},{48,176},{56,1... | collective-permute-start | bytes 786440 | tf_op jit(solution)/shard_map/ppermute | solution.py:265
  10.5 3.2 %collective-permute-start.3 = (bf16[8,32,512]{2,1,0:T(8,128)(2,1)S(1)}, bf16[8,32,512]{2,1,0:T(8,128)(2,1)S(1)}, u32[]{:S(2)}, u32[]{:S(2)}) collective-permute-start(bf16[8,32,512]{2,1,0:T(8,128)(2,1)S(1)} %get-tuple-element.41), channel_id=1, source_target_pairs={{0,32},{8,40},{16,48},{24,56},{32,0},{40,8},{48,16},{56,24},{64,96... | collective-permute-start | bytes 786440 | tf_op jit(solution)/shard_map/ppermute | solution.py:265
  13.7 1.2 %collective-permute-start.4 = (bf16[8,32,512]{2,1,0:T(8,128)(2,1)S(1)}, bf16[8,32,512]{2,1,0:T(8,128)(2,1)S(1)}, u32[]{:S(2)}, u32[]{:S(2)}) collective-permute-start(bf16[8,32,512]{2,1,0:T(8,128)(2,1)S(1)} %get-tuple-element.40), channel_id=1, source_target_pairs={{0,96},{8,232},{16,112},{24,248},{32,64},{40,200},{48,80},{56,216}... | collective-permute-start | bytes 786440 | tf_op jit(solution)/shard_map/ppermute | solution.py:265
  14.9 0.9 %collective-permute-done.refs_1_ = bf16[8,32,512]{2,1,0:T(8,128)(2,1)S(1)} collective-permute-done((bf16[8,32,512]{2,1,0:T(8,128)(2,1)S(1)}, bf16[8,32,512]{2,1,0:T(8,128)(2,1)S(1)}, u32[]{:S(2)}, u32[]{:S(2)}) %collective-permute-start) | collective-permute-done | bytes 262176 | tf_op jit(solution)/shard_map/ppermute | solution.py:265
  15.8 2.5 %collective-permute-start.5 = (bf16[8,32,512]{2,1,0:T(8,128)(2,1)S(1)}, bf16[8,32,512]{2,1,0:T(8,128)(2,1)S(1)}, u32[]{:S(2)}, u32[]{:S(2)}) collective-permute-start(bf16[8,32,512]{2,1,0:T(8,128)(2,1)S(1)} %get-tuple-element.45), channel_id=1, source_target_pairs={{0,64},{8,200},{16,80},{24,216},{32,96},{40,232},{48,112},{56,248}... | collective-permute-start | bytes 786440 | tf_op jit(solution)/shard_map/ppermute | solution.py:265
  18.2 0.9 %shard_map.76 = (bf16[768,1024]{1,0:T(8,128)(2,1)S(1)}, f32[32,512]{1,0:T(8,128)S(1)}, f32[64,128]{1,0:T(8,128)S(1)}) custom-call(f32[4,3]{1,0:T(4,128)S(1)} %copy-done.3, bf16[48,64]{1,0:T(8,128)(2,1)S(1)} %copy-done.2, s32[32,512]{1,0:T(8,128)S(1)} %copy-done.1), custom_call_target="tpu_custom_call" | custom-call | flops 100663296 | bytes 1572864 | tf_op jit(solution)/shard_map/pallas_call | solution.py:271
  19.2 5.9 %collective-permute-done.1.refs_2_ = bf16[8,32,512]{2,1,0:T(8,128)(2,1)S(1)} collective-permute-done((bf16[8,32,512]{2,1,0:T(8,128)(2,1)S(1)}, bf16[8,32,512]{2,1,0:T(8,128)(2,1)S(1)}, u32[]{:S(2)}, u32[]{:S(2)}) %collective-permute-start.1) | collective-permute-done | bytes 262176 | tf_op jit(solution)/shard_map/ppermute | solution.py:265
  25.1 3.6 %collective-permute-start.6 = (bf16[8,32,512]{2,1,0:T(8,128)(2,1)S(1)}, bf16[8,32,512]{2,1,0:T(8,128)(2,1)S(1)}, u32[]{:S(2)}, u32[]{:S(2)}) collective-permute-start(bf16[8,32,512]{2,1,0:T(8,128)(2,1)S(1)} %get-tuple-element.39), channel_id=1, source_target_pairs={{0,192},{8,72},{16,208},{24,88},{32,224},{40,104},{48,240},{56,120... | collective-permute-start | bytes 786440 | tf_op jit(solution)/shard_map/ppermute | solution.py:265
  28.8 1.0 %dynamic-slice_bitcast_fusion.6.refs_0_ = bf16[8,32,512]{2,1,0:T(8,128)(2,1)S(1)} fusion(bf16[8,8,32,512]{3,2,1,0:T(8,128)(2,1)} %param.5, s32[]{:T(128)S(6)} %select_n.35), kind=kLoop, calls=%fused_computation.6 | loop fusion | bytes 524292 | tf_op jit(solution)/shard_map/jit(dynamic_index_in_dim)/squeeze | solution.py:262
  29.7 0.0 copy-start
  29.7 1.0 %shard_map.77.series_ref = f32[48,32,512]{2,1,0:T(8,128)S(1)} custom-call(bf16[768,1024]{1,0:T(8,128)(2,1)S(1)} %get-tuple-element.24.w_ref, bf16[8,32,512]{2,1,0:T(8,128)(2,1)S(1)} %dynamic-slice_bitcast_fusion.6.refs_0_, bf16[8,32,512]{2,1,0:T(8,128)(2,1)S(1)} %collective-permute-done.refs_1_, bf16[8,32,512]{2,1,0:T(8,128)(2,1)S(1)} %collective-permute-done.1.refs_2_), custom_call_target="tpu_custom_call" | custom-call | flops 1610612736 | bytes 2097152 | tf_op jit(solution)/shard_map/pallas_call | solution.py:279
  30.7 0.0 collective-permute-done.2.refs_0_.refs_3_
  30.7 0.6 %collective-permute-done.3.refs_1_.refs_4_ = bf16[8,32,512]{2,1,0:T(8,128)(2,1)S(1)} collective-permute-done((bf16[8,32,512]{2,1,0:T(8,128)(2,1)S(1)}, bf16[8,32,512]{2,1,0:T(8,128)(2,1)S(1)}, u32[]{:S(2)}, u32[]{:S(2)}) %collective-permute-start.3) | collective-permute-done | bytes 262176 | tf_op jit(solution)/shard_map/ppermute | solution.py:265
  31.3 0.0 collective-permute-done.4.refs_2_.refs_5_
  31.3 0.5 %collective-permute-done.5.refs_3_.refs_6_ = bf16[8,32,512]{2,1,0:T(8,128)(2,1)S(1)} collective-permute-done((bf16[8,32,512]{2,1,0:T(8,128)(2,1)S(1)}, bf16[8,32,512]{2,1,0:T(8,128)(2,1)S(1)}, u32[]{:S(2)}, u32[]{:S(2)}) %collective-permute-start.5) | collective-permute-done | bytes 262176 | tf_op jit(solution)/shard_map/ppermute | solution.py:265
  31.8 1.3 %collective-permute-done.6.refs_4_.refs_7_ = bf16[8,32,512]{2,1,0:T(8,128)(2,1)S(1)} collective-permute-done((bf16[8,32,512]{2,1,0:T(8,128)(2,1)S(1)}, bf16[8,32,512]{2,1,0:T(8,128)(2,1)S(1)}, u32[]{:S(2)}, u32[]{:S(2)}) %collective-permute-start.6) | collective-permute-done | bytes 262176 | tf_op jit(solution)/shard_map/ppermute | solution.py:265
  33.1 0.0 copy-done
  33.1 0.4 shard_map.79
  33.5 0.1 collective-permute-start.10
  33.6 5.7 %collective-permute-start.8 = (f32[16,512]{1,0:T(8,128)S(1)}, f32[16,512]{1,0:T(8,128)S(1)}, u32[]{:S(2)}, u32[]{:S(2)}) collective-permute-start(f32[16,512]{1,0:T(8,128)S(1)} %get-tuple-element.34), channel_id=1, source_target_pairs={{8,16},{16,8},{24,32},{32,24},{40,48},{48,40},{56,64},{64,56},{72,... | collective-permute-start | bytes 98312 | tf_op jit(solution)/shard_map/ppermute | solution.py:297
  39.4 1.9 %collective-permute-start.7 = (f32[32,128]{1,0:T(8,128)S(1)}, f32[32,128]{1,0:T(8,128)S(1)}, u32[]{:S(2)}, u32[]{:S(2)}) collective-permute-start(f32[32,128]{1,0:T(8,128)S(1)} %get-tuple-element.33), channel_id=1, source_target_pairs={{1,2},{2,1},{3,4},{4,3},{5,6},{6,5},{7,0},{0,7},{9,10},{10,9},{11,... | collective-permute-start | bytes 49160 | tf_op jit(solution)/shard_map/ppermute | solution.py:296
  41.3 4.0 %collective-permute-start.9 = (f32[32,128]{1,0:T(8,128)S(1)}, f32[32,128]{1,0:T(8,128)S(1)}, u32[]{:S(2)}, u32[]{:S(2)}) collective-permute-start(f32[32,128]{1,0:T(8,128)S(1)} %get-tuple-element.35), channel_id=1, source_target_pairs={{0,1},{1,0},{2,3},{3,2},{4,5},{5,4},{6,7},{7,6},{8,9},{9,8},{10,11... | collective-permute-start | bytes 49160 | tf_op jit(solution)/shard_map/ppermute | solution.py:298
  45.3 2.2 %shard_map.78 = bf16[48,32,512]{2,1,0:T(8,128)(2,1)} custom-call(bf16[768,1024]{1,0:T(8,128)(2,1)S(1)} %get-tuple-element.24.w_ref, f32[48,32,512]{2,1,0:T(8,128)S(1)} %shard_map.77.series_ref, bf16[8,32,512]{2,1,0:T(8,128)(2,1)S(1)} %collective-permute-done.2.refs_0_.refs_3_, bf16[8,32,512]{2,1,0:T(8,128)(2,1)S(1)} %collective-permute-done.3.refs_1_.refs_4_, ...), custom_call_target="tpu_custom_call" | custom-call | flops 805306368 | bytes 1572864 | tf_op jit(solution)/shard_map/pallas_call | solution.py:301
  47.5 0.0 collective-permute-done.7.right_ref
  47.6 0.0 collective-permute-done.9.left_ref
  47.6 0.0 collective-permute-done.10.one_ref
  47.6 0.0 collective-permute-done.8.two_ref
  47.6 0.9 %shard_map.80 = (f32[32,512]{1,0:T(8,128)}, f32[32,512]{1,0:T(8,128)}) custom-call(f32[32,512]{1,0:T(8,128)S(1)} %get-tuple-element.32.v_ref, f32[32,128]{1,0:T(8,128)S(1)} %collective-permute-done.7.right_ref, f32[16,512]{1,0:T(8,128)S(1)} %collective-permute-done.8.two_ref, f32[32,128]{1,0:T(8,128)S(1)} %collective-permute-done.9.left_ref, ...), custom_call_target="tpu_custom_call" | custom-call | flops 6553600 | bytes 262144 | tf_op jit(solution)/shard_map/pallas_call | solution.py:314
  (5 shorter events, 0.0 us)
Async XLA Ops:
  0.6 17.6 %copy-start.2 = (bf16[48,64]{1,0:T(8,128)(2,1)S(1)}, bf16[48,64]{1,0:T(8,128)(2,1)}, u32[]{:S(2)}) copy-start(bf16[48,64]{1,0:T(8,128)(2,1)} %pinv_ref) | copy-start | bytes 18436
  0.6 17.6 %copy-start.3 = (f32[4,3]{1,0:T(4,128)S(1)}, f32[4,3]{1,0:T(4,128)}, u32[]{:S(2)}) copy-start(f32[4,3]{1,0:T(4,128)} %rot_ref) | copy-start | bytes 148
  0.7 17.6 %copy-start.1 = (s32[32,512]{1,0:T(8,128)S(1)}, s32[32,512]{1,0:T(8,128)}, u32[]{:S(2)}) copy-start(s32[32,512]{1,0:T(8,128)} %plate_ref) | copy-start | bytes 196612
  2.3 13.4 %collective-permute-start = (bf16[8,32,512]{2,1,0:T(8,128)(2,1)S(1)}, bf16[8,32,512]{2,1,0:T(8,128)(2,1)S(1)}, u32[]{:S(2)}, u32[]{:S(2)}) collective-permute-start(bf16[8,32,512]{2,1,0:T(8,128)(2,1)S(1)} %get-tuple-element.44), channel_id=1, source_target_pairs={{0,160},{8,168},{16,176},{24,184},{32,128},{40,136},{48,144},{56,1... | collective-permute-start | bytes 786440 | tf_op jit(solution)/shard_map/ppermute | solution.py:265
  8.1 17.0 %collective-permute-start.1 = (bf16[8,32,512]{2,1,0:T(8,128)(2,1)S(1)}, bf16[8,32,512]{2,1,0:T(8,128)(2,1)S(1)}, u32[]{:S(2)}, u32[]{:S(2)}) collective-permute-start(bf16[8,32,512]{2,1,0:T(8,128)(2,1)S(1)} %get-tuple-element.43), channel_id=1, source_target_pairs={{0,224},{8,104},{16,240},{24,120},{32,192},{40,72},{48,208},{56,88... | collective-permute-start | bytes 786440 | tf_op jit(solution)/shard_map/ppermute | solution.py:265
  9.0 21.7 %collective-permute-start.2 = (bf16[8,32,512]{2,1,0:T(8,128)(2,1)S(1)}, bf16[8,32,512]{2,1,0:T(8,128)(2,1)S(1)}, u32[]{:S(2)}, u32[]{:S(2)}) collective-permute-start(bf16[8,32,512]{2,1,0:T(8,128)(2,1)S(1)} %get-tuple-element.42), channel_id=1, source_target_pairs={{0,128},{8,136},{16,144},{24,152},{32,160},{40,168},{48,176},{56,1... | collective-permute-start | bytes 786440 | tf_op jit(solution)/shard_map/ppermute | solution.py:265
  10.5 20.8 %collective-permute-start.3 = (bf16[8,32,512]{2,1,0:T(8,128)(2,1)S(1)}, bf16[8,32,512]{2,1,0:T(8,128)(2,1)S(1)}, u32[]{:S(2)}, u32[]{:S(2)}) collective-permute-start(bf16[8,32,512]{2,1,0:T(8,128)(2,1)S(1)} %get-tuple-element.41), channel_id=1, source_target_pairs={{0,32},{8,40},{16,48},{24,56},{32,0},{40,8},{48,16},{56,24},{64,96... | collective-permute-start | bytes 786440 | tf_op jit(solution)/shard_map/ppermute | solution.py:265
  13.7 17.6 %collective-permute-start.4 = (bf16[8,32,512]{2,1,0:T(8,128)(2,1)S(1)}, bf16[8,32,512]{2,1,0:T(8,128)(2,1)S(1)}, u32[]{:S(2)}, u32[]{:S(2)}) collective-permute-start(bf16[8,32,512]{2,1,0:T(8,128)(2,1)S(1)} %get-tuple-element.40), channel_id=1, source_target_pairs={{0,96},{8,232},{16,112},{24,248},{32,64},{40,200},{48,80},{56,216}... | collective-permute-start | bytes 786440 | tf_op jit(solution)/shard_map/ppermute | solution.py:265
  15.8 16.0 %collective-permute-start.5 = (bf16[8,32,512]{2,1,0:T(8,128)(2,1)S(1)}, bf16[8,32,512]{2,1,0:T(8,128)(2,1)S(1)}, u32[]{:S(2)}, u32[]{:S(2)}) collective-permute-start(bf16[8,32,512]{2,1,0:T(8,128)(2,1)S(1)} %get-tuple-element.45), channel_id=1, source_target_pairs={{0,64},{8,200},{16,80},{24,216},{32,96},{40,232},{48,112},{56,248}... | collective-permute-start | bytes 786440 | tf_op jit(solution)/shard_map/ppermute | solution.py:265
  25.1 8.0 %collective-permute-start.6 = (bf16[8,32,512]{2,1,0:T(8,128)(2,1)S(1)}, bf16[8,32,512]{2,1,0:T(8,128)(2,1)S(1)}, u32[]{:S(2)}, u32[]{:S(2)}) collective-permute-start(bf16[8,32,512]{2,1,0:T(8,128)(2,1)S(1)} %get-tuple-element.39), channel_id=1, source_target_pairs={{0,192},{8,72},{16,208},{24,88},{32,224},{40,104},{48,240},{56,120... | collective-permute-start | bytes 786440 | tf_op jit(solution)/shard_map/ppermute | solution.py:265
  29.7 3.4 %copy-start = (s32[32,512]{1,0:T(8,128)S(1)}, s32[32,512]{1,0:T(8,128)}, u32[]{:S(2)}) copy-start(s32[32,512]{1,0:T(8,128)} %refs_8_) | copy-start | bytes 196612
  33.5 14.0 %collective-permute-start.10 = (f32[16,512]{1,0:T(8,128)S(1)}, f32[16,512]{1,0:T(8,128)S(1)}, u32[]{:S(2)}, u32[]{:S(2)}) collective-permute-start(f32[16,512]{1,0:T(8,128)S(1)} %get-tuple-element.36), channel_id=1, source_target_pairs={{0,8},{8,0},{16,24},{24,16},{32,40},{40,32},{48,56},{56,48},{64,72... | collective-permute-start | bytes 98312 | tf_op jit(solution)/shard_map/ppermute | solution.py:299
  33.6 13.9 %collective-permute-start.8 = (f32[16,512]{1,0:T(8,128)S(1)}, f32[16,512]{1,0:T(8,128)S(1)}, u32[]{:S(2)}, u32[]{:S(2)}) collective-permute-start(f32[16,512]{1,0:T(8,128)S(1)} %get-tuple-element.34), channel_id=1, source_target_pairs={{8,16},{16,8},{24,32},{32,24},{40,48},{48,40},{56,64},{64,56},{72,... | collective-permute-start | bytes 98312 | tf_op jit(solution)/shard_map/ppermute | solution.py:297
  39.4 8.2 %collective-permute-start.7 = (f32[32,128]{1,0:T(8,128)S(1)}, f32[32,128]{1,0:T(8,128)S(1)}, u32[]{:S(2)}, u32[]{:S(2)}) collective-permute-start(f32[32,128]{1,0:T(8,128)S(1)} %get-tuple-element.33), channel_id=1, source_target_pairs={{1,2},{2,1},{3,4},{4,3},{5,6},{6,5},{7,0},{0,7},{9,10},{10,9},{11,... | collective-permute-start | bytes 49160 | tf_op jit(solution)/shard_map/ppermute | solution.py:296
  41.3 6.3 %collective-permute-start.9 = (f32[32,128]{1,0:T(8,128)S(1)}, f32[32,128]{1,0:T(8,128)S(1)}, u32[]{:S(2)}, u32[]{:S(2)}) collective-permute-start(f32[32,128]{1,0:T(8,128)S(1)} %get-tuple-element.35), channel_id=1, source_target_pairs={{0,1},{1,0},{2,3},{3,2},{4,5},{5,4},{6,7},{7,6},{8,9},{9,8},{10,11... | collective-permute-start | bytes 49160 | tf_op jit(solution)/shard_map/ppermute | solution.py:298

commit v3 on v2

--- a/solution.py
+++ b/solution.py
@@ -13,6 +13,7 @@
 F32 = jnp.float32
 BF16 = jnp.bfloat16
 VMEM_BYTES = 40 << 20
+WIDE = 72
 CUT = 16
 
 FLOWS = {
@@ -25,10 +26,10 @@
     "Xa": ("a", 0),
     "Xb": ("b", 0),
 }
-EARLY = ("D2", "Db")
-LATE = ("X2", "Y2", "Da", "Xa", "Xb")
+EARLY = ("D2", "Db", "X2", "Xa")
+LATE = ("Y2", "Da", "Xb")
 ORDER = ("own",) + EARLY + LATE
-STARTS = EARLY + LATE
+STARTS = ("D2", "Db", "X2", "Y2", "Da", "Xa", "Xb")
 
 
 def along_x(step, x, core, pick):
@@ -56,11 +57,18 @@
     return pairs
 
 
-def ring_pairs(count, first):
+def neighbour_pairs(tiles, columns, along, first):
     pairs = []
-    for low in range(first, count, 2):
-        high = (low + 1) % count
-        pairs += [(low, high), (high, low)]
+    for tile in range(tiles):
+        for column in range(columns):
+            count = (tiles, columns)[along]
+            here = (tile, column)[along]
+            other = here + 1 if here % 2 == first else here - 1
+            if 0 <= other < count:
+                there = (other, column) if along == 0 else (tile, other)
+            else:
+                there = (tile, column ^ 1) if along == 0 else (tile ^ 1, column)
+            pairs.append((tile * columns + column, there[0] * columns + there[1]))
     return pairs
 
 
@@ -142,24 +150,28 @@
     return grp >> 1, grp & 1, row & 1
 
 
-def rate_kernel(weight_ref, *refs):
-    outs = refs[-5:]
-    v_ref, one_ref, two_ref, left_ref, right_ref = outs
+def rates(total, weight_ref, names, blocks):
+    x, y, core = place_here()
+    for name, block in zip(names, blocks):
+        total = weighted(total, block, weight_ref, partner(name, x, y, core, jnp.where))
+    return total
+
+
+def rate_kernel(weight_ref, part_ref, *refs):
+    v_ref, one_ref, two_ref, left_ref, right_ref = refs[-5:]
     coherent_ref, plate_rate_ref = refs[-7:-5]
-    blocks = refs[:-7]
     rows, cols = v_ref.shape
-    rate = jnp.zeros((rows, cols), F32)
-    x, y, core = place_here()
-    for name, block in zip(ORDER, blocks):
-        rate = weighted(rate, block, weight_ref, partner(name, x, y, core, jnp.where))
+    rate = rates(part_ref[...], weight_ref, LATE, refs[:-7])
     v_ref[...] = coherent_ref[...].astype(F32) * rate - plate_rate_ref[...]
+    core = place_here()[2]
     column = lax.axis_index("col") & 1
     top, low = v_ref[:REACH, :], v_ref[rows - REACH :, :]
     first, last = v_ref[:, :LANES], v_ref[:, cols - LANES :]
     one_ref[...] = jnp.where(core == 0, low, top)
     two_ref[...] = jnp.where(core == 0, top, low)
     left_ref[...] = jnp.where(column == 0, last, first)
-    right_ref[...] = jnp.where(column == 0, first, last)
+    right_ref[:rows, :] = jnp.where(column == 0, first, last)
+    right_ref[rows:, :] = jnp.zeros((WIDE - rows, LANES), F32)
 
 
 def stacked(blocks, part):
@@ -167,8 +179,8 @@
     return jnp.concatenate([b[:, part, :].reshape(share * SUB, cols) for b in blocks], axis=0)
 
 
-def series_kernel(w_ref, *refs):
-    blocks, out_ref = refs[:-1], refs[-1]
+def series_kernel(w_ref, weight_ref, *refs):
+    blocks, out_ref, rate_ref = refs[:-2], refs[-2], refs[-1]
     epochs, rows, cols = out_ref.shape
     deep = len(blocks) * blocks[0].shape[0] * SUB
     for t in range(rows // SUB):
@@ -177,6 +189,7 @@
         for e in range(0, epochs, CUT):
             found = jnp.dot(w_ref[e * SUB : (e + CUT) * SUB, :deep], stack, preferred_element_type=F32)
             out_ref[e : e + CUT, part, :] = found.reshape(CUT, SUB, cols)
+    rate_ref[...] = rates(jnp.zeros((rows, cols), F32), weight_ref, ("own",) + EARLY, blocks)
 
 
 def displacement_kernel(w_ref, series_ref, *refs):
@@ -204,7 +217,7 @@
     return jnp.where(jnp.abs(step) <= REACH, step, 0).astype(F32).astype(BF16)
 
 
-def gradient_kernel(v_ref, right_ref, two_ref, left_ref, one_ref, rows_ref, cols_ref):
+def gradient_kernel(v_ref, right_ref, two_ref, one_ref, left_ref, rows_ref, cols_ref):
     rows, cols = v_ref.shape
     scale = (REACH * (REACH + 1) * (2 * REACH + 1) // 3) ** -0.5
     tile = lax.axis_index("grp") * lax.axis_size("row") + lax.axis_index("row")
@@ -221,7 +234,7 @@
     for part in three_parts(upright):
         total = total + jnp.dot(taps, part, preferred_element_type=F32)
     rows_ref[...] = total * scale
-    first, second = left_ref[...], right_ref[...]
+    first, second = left_ref[...], right_ref[:rows, :]
     before = jnp.where(place == 0, 0.0, jnp.where(column == 0, second, first))
     after = jnp.where(place == columns - 1, 0.0, jnp.where(column == 0, first, second))
     sideways = jnp.concatenate([before, v, after], axis=1)
@@ -276,28 +289,29 @@
         2 * tall * deep,
     )(rotation, pseudo_inverse, plate_id)
 
-    series = call(
+    series, rate = call(
         series_kernel,
-        [VMEM] * (1 + len(early)),
-        shape(epochs, rows, cols),
+        [VMEM] * (2 + len(early)),
+        (shape(epochs, rows, cols), shape(rows, cols)),
         2 * epochs * ifg * rows * cols * SUB,
         2 * ifg * rows * cols,
-    )(w, *early)
+    )(w, weight, *early)
     series, plate_rate = lax.optimization_barrier((series, plate_rate))
 
     velocity, one, two, left, right = call(
         rate_kernel,
-        [VMEM] * (3 + len(ORDER)),
-        (shape(rows, cols), shape(REACH, cols), shape(REACH, cols), shape(rows, LANES), shape(rows, LANES)),
+        [VMEM] * (4 + len(late)),
+        (shape(rows, cols), shape(REACH, cols), shape(REACH, cols), shape(rows, LANES), shape(WIDE, LANES)),
         2 * ifg * rows * cols,
         2 * ifg * rows * cols,
-    )(weight, *early, *late, coherent, plate_rate)
-
-    right = lax.ppermute(right, "col", ring_pairs(lax.axis_size("col"), 1))
-    two = lax.ppermute(two, both, ring_pairs(tiles, 1))
-    left = lax.ppermute(left, "col", ring_pairs(lax.axis_size("col"), 0))
-    one = lax.ppermute(one, both, ring_pairs(tiles, 0))
-
+    )(weight, rate, *late, coherent, plate_rate)
+
+    columns = lax.axis_size("col")
+    everywhere = ("grp", "row", "col")
+    right = lax.ppermute(right, everywhere, neighbour_pairs(tiles, columns, 1, 1))
+    one = lax.ppermute(one, everywhere, neighbour_pairs(tiles, columns, 0, 0))
+    two = lax.ppermute(two, everywhere, neighbour_pairs(tiles, columns, 0, 1))
+    left = lax.ppermute(left, everywhere, neighbour_pairs(tiles, columns, 1, 0))
     displacement = call(
         displacement_kernel,
         [VMEM] * (2 + len(late)),
@@ -317,7 +331,7 @@
         (shape(rows, cols), shape(rows, cols)),
         2 * 200 * rows * cols,
         16 * rows * cols,
-    )(velocity, right, two, left, one)
+    )(velocity, right, two, one, left)
     return (displacement, grad_rows, grad_cols)
 
 

time: 48.7 us -> 43.9 us (0.901)
  the two profiles are of different devices: /device:TPU:32 before, /device:TPU:96 now
where the time goes in v3:
time: 43.9 us; the launch traced here: 43.2 us
  starting transfers between devices  25.2 us (57%)
  waiting for transfers between devices  9.28 us (21%)
  Pallas kernels  5.34 us (12%)
  local copies, waits for them, and re-layouts  2.64 us (6%)
  between operations  0.77 us (2%)
    ppermute x7, starting transfers between devices, on_device(): lax.ppermute(sent[name], both, swap_pairs(name))  20 us
    ppermute x7, waiting for transfers between devices, on_device(): lax.ppermute(sent[name], both, swap_pairs(name))  8 us
    ppermute x1, starting transfers between devices, on_device(): lax.ppermute(right, everywhere, neighbour_pairs(tiles, columns, 1, 1))  3.22 us
    squeeze x2, local copies, waits for them, and re-layouts, cut(): lax.dynamic_index_in_dim(phase, partner(name, x, y, core, jnp.where), 1,...  2.62 us
    pallas_call x1, Pallas kernels, on_device(): call(displacement_kernel, [VMEM] * (2 + len(late)), shape(epochs, rows, c...  1.8 us
    pallas_call x1, Pallas kernels, on_device(): call(series_kernel, [VMEM] * (2 + len(early)), (shape(epochs, rows, cols)...  1.53 us
    ppermute x1, starting transfers between devices, on_device(): one = lax.ppermute(one, everywhere, neighbour_pairs(tiles, columns, 0, 0))  1.36 us
    ppermute x1, waiting for transfers between devices, on_device(): left = lax.ppermute(left, everywhere, neighbour_pairs(tiles, columns, 1, 0))  1.27 us
  transfers between devices with their start and end apart: 11, of which 5 were waited for; matrix products, arithmetic and copies ran while one was open for 2% of the time, Pallas kernels for 10%

profile of v3, /device:TPU:96, one launch (start us, length us, event | category | flops | bytes accessed | tf_op | source)
XLA Modules:
  0.0 43.2 jit_solution(10421505720951314493)
XLA Ops:
  0.6 0.0 copy-start.2
  0.6 0.0 copy-start.3
  0.7 1.6 %dynamic-slice_bitcast_fusion = (bf16[8,32,512]{2,1,0:T(8,128)(2,1)S(1)}, bf16[8,32,512]{2,1,0:T(8,128)(2,1)S(1)}, bf16[8,32,512]{2,1,0:T(8,128)(2,1)S(1)}, bf16...) fusion(bf16[8,8,32,512]{3,2,1,0:T(8,128)(2,1)} %param.5, ...), kind=kLoop, calls=%fused_computation | loop fusion | bytes 3670044 | tf_op jit(solution)/shard_map/jit(dynamic_index_in_dim)/squeeze | solution.py:275
  2.3 5.7 %collective-permute-start = (bf16[8,32,512]{2,1,0:T(8,128)(2,1)S(1)}, bf16[8,32,512]{2,1,0:T(8,128)(2,1)S(1)}, u32[]{:S(2)}, u32[]{:S(2)}) collective-permute-start(bf16[8,32,512]{2,1,0:T(8,128)(2,1)S(1)} %get-tuple-element.48), channel_id=1, source_target_pairs={{0,160},{8,168},{16,176},{24,184},{32,128},{40,136},{48,144},{56,1... | collective-permute-start | bytes 786440 | tf_op jit(solution)/shard_map/ppermute | solution.py:278
  8.1 0.9 %collective-permute-start.1 = (bf16[8,32,512]{2,1,0:T(8,128)(2,1)S(1)}, bf16[8,32,512]{2,1,0:T(8,128)(2,1)S(1)}, u32[]{:S(2)}, u32[]{:S(2)}) collective-permute-start(bf16[8,32,512]{2,1,0:T(8,128)(2,1)S(1)} %get-tuple-element.47), channel_id=1, source_target_pairs={{0,224},{8,104},{16,240},{24,120},{32,192},{40,72},{48,208},{56,88... | collective-permute-start | bytes 786440 | tf_op jit(solution)/shard_map/ppermute | solution.py:278
  9.0 1.5 %collective-permute-start.2 = (bf16[8,32,512]{2,1,0:T(8,128)(2,1)S(1)}, bf16[8,32,512]{2,1,0:T(8,128)(2,1)S(1)}, u32[]{:S(2)}, u32[]{:S(2)}) collective-permute-start(bf16[8,32,512]{2,1,0:T(8,128)(2,1)S(1)} %get-tuple-element.46), channel_id=1, source_target_pairs={{0,128},{8,136},{16,144},{24,152},{32,160},{40,168},{48,176},{56,1... | collective-permute-start | bytes 786440 | tf_op jit(solution)/shard_map/ppermute | solution.py:278
  10.5 1.4 %collective-permute-start.3 = (bf16[8,32,512]{2,1,0:T(8,128)(2,1)S(1)}, bf16[8,32,512]{2,1,0:T(8,128)(2,1)S(1)}, u32[]{:S(2)}, u32[]{:S(2)}) collective-permute-start(bf16[8,32,512]{2,1,0:T(8,128)(2,1)S(1)} %get-tuple-element.45), channel_id=1, source_target_pairs={{0,64},{8,200},{16,80},{24,216},{32,96},{40,232},{48,112},{56,248}... | collective-permute-start | bytes 786440 | tf_op jit(solution)/shard_map/ppermute | solution.py:278
  12.0 3.2 %collective-permute-start.4 = (bf16[8,32,512]{2,1,0:T(8,128)(2,1)S(1)}, bf16[8,32,512]{2,1,0:T(8,128)(2,1)S(1)}, u32[]{:S(2)}, u32[]{:S(2)}) collective-permute-start(bf16[8,32,512]{2,1,0:T(8,128)(2,1)S(1)} %get-tuple-element.44), channel_id=1, source_target_pairs={{0,32},{8,40},{16,48},{24,56},{32,0},{40,8},{48,16},{56,24},{64,96... | collective-permute-start | bytes 786440 | tf_op jit(solution)/shard_map/ppermute | solution.py:278
  15.2 0.6 %collective-permute-done.refs_1_ = bf16[8,32,512]{2,1,0:T(8,128)(2,1)S(1)} collective-permute-done((bf16[8,32,512]{2,1,0:T(8,128)(2,1)S(1)}, bf16[8,32,512]{2,1,0:T(8,128)(2,1)S(1)}, u32[]{:S(2)}, u32[]{:S(2)}) %collective-permute-start) | collective-permute-done | bytes 262176 | tf_op jit(solution)/shard_map/ppermute | solution.py:278
  15.7 4.7 %collective-permute-start.5 = (bf16[8,32,512]{2,1,0:T(8,128)(2,1)S(1)}, bf16[8,32,512]{2,1,0:T(8,128)(2,1)S(1)}, u32[]{:S(2)}, u32[]{:S(2)}) collective-permute-start(bf16[8,32,512]{2,1,0:T(8,128)(2,1)S(1)} %get-tuple-element.49), channel_id=1, source_target_pairs={{0,96},{8,232},{16,112},{24,248},{32,64},{40,200},{48,80},{56,216}... | collective-permute-start | bytes 786440 | tf_op jit(solution)/shard_map/ppermute | solution.py:278
  20.4 0.9 %shard_map.76 = (bf16[768,1024]{1,0:T(8,128)(2,1)S(1)}, f32[32,512]{1,0:T(8,128)S(1)}, f32[64,128]{1,0:T(8,128)S(1)}) custom-call(f32[4,3]{1,0:T(4,128)S(1)} %copy-done.3, bf16[48,64]{1,0:T(8,128)(2,1)S(1)} %copy-done.2, s32[32,512]{1,0:T(8,128)S(1)} %copy-done.1), custom_call_target="tpu_custom_call" | custom-call | flops 100663296 | bytes 1572864 | tf_op jit(solution)/shard_map/pallas_call | solution.py:284
  21.3 4.9 %collective-permute-done.1.refs_2_ = bf16[8,32,512]{2,1,0:T(8,128)(2,1)S(1)} collective-permute-done((bf16[8,32,512]{2,1,0:T(8,128)(2,1)S(1)}, bf16[8,32,512]{2,1,0:T(8,128)(2,1)S(1)}, u32[]{:S(2)}, u32[]{:S(2)}) %collective-permute-start.1) | collective-permute-done | bytes 262176 | tf_op jit(solution)/shard_map/ppermute | solution.py:278
  26.2 2.5 %collective-permute-start.6 = (bf16[8,32,512]{2,1,0:T(8,128)(2,1)S(1)}, bf16[8,32,512]{2,1,0:T(8,128)(2,1)S(1)}, u32[]{:S(2)}, u32[]{:S(2)}) collective-permute-start(bf16[8,32,512]{2,1,0:T(8,128)(2,1)S(1)} %get-tuple-element.43), channel_id=1, source_target_pairs={{0,192},{8,72},{16,208},{24,88},{32,224},{40,104},{48,240},{56,120... | collective-permute-start | bytes 786440 | tf_op jit(solution)/shard_map/ppermute | solution.py:278
  28.7 1.0 %dynamic-slice_bitcast_fusion.6.refs_0_ = bf16[8,32,512]{2,1,0:T(8,128)(2,1)S(1)} fusion(bf16[8,8,32,512]{3,2,1,0:T(8,128)(2,1)} %param.5, s32[]{:T(128)S(6)} %select_n.35), kind=kLoop, calls=%fused_computation.6 | loop fusion | bytes 524292 | tf_op jit(solution)/shard_map/jit(dynamic_index_in_dim)/squeeze | solution.py:275
  29.7 0.0 collective-permute-done.2.refs_3_
  29.7 0.0 collective-permute-done.3.refs_4_
  29.7 0.0 copy-start
  29.7 1.5 %shard_map.77 = (f32[48,32,512]{2,1,0:T(8,128)S(1)}, f32[32,512]{1,0:T(8,128)S(1)}) custom-call(bf16[768,1024]{1,0:T(8,128)(2,1)S(1)} %get-tuple-element.26.w_ref, f32[64,128]{1,0:T(8,128)S(1)} %get-tuple-element.27.weight_ref, bf16[8,32,512]{2,1,0:T(8,128)(2,1)S(1)} %dynamic-slice_bitcast_fusion.6.refs_0_, ...), custom_call_target="tpu_custom_call" | custom-call | flops 1610612736 | bytes 2097152 | tf_op jit(solution)/shard_map/pallas_call | solution.py:292
  31.2 0.0 collective-permute-done.4.refs_0_
  31.2 1.0 %collective-permute-done.5.refs_1_ = bf16[8,32,512]{2,1,0:T(8,128)(2,1)S(1)} collective-permute-done((bf16[8,32,512]{2,1,0:T(8,128)(2,1)S(1)}, bf16[8,32,512]{2,1,0:T(8,128)(2,1)S(1)}, u32[]{:S(2)}, u32[]{:S(2)}) %collective-permute-start.5) | collective-permute-done | bytes 262176 | tf_op jit(solution)/shard_map/ppermute | solution.py:278
  32.3 1.5 %collective-permute-done.6.refs_2_ = bf16[8,32,512]{2,1,0:T(8,128)(2,1)S(1)} collective-permute-done((bf16[8,32,512]{2,1,0:T(8,128)(2,1)S(1)}, bf16[8,32,512]{2,1,0:T(8,128)(2,1)S(1)}, u32[]{:S(2)}, u32[]{:S(2)}) %collective-permute-start.6) | collective-permute-done | bytes 262176 | tf_op jit(solution)/shard_map/ppermute | solution.py:278
  33.8 0.2 shard_map.79
  34.0 3.2 %collective-permute-start.7 = (f32[72,128]{1,0:T(8,128)S(1)}, f32[72,128]{1,0:T(8,128)S(1)}, u32[]{:S(2)}, u32[]{:S(2)}) collective-permute-start(f32[72,128]{1,0:T(8,128)S(1)} %get-tuple-element.37), channel_id=1, source_target_pairs={{0,8},{1,2},{2,1},{3,4},{4,3},{5,6},{6,5},{7,15},{8,0},{9,10},{10,... | collective-permute-start | bytes 110600 | tf_op jit(solution)/shard_map/ppermute | solution.py:311
  37.2 0.0 collective-permute-start.8
  37.2 1.4 %collective-permute-start.9 = (f32[16,512]{1,0:T(8,128)S(1)}, f32[16,512]{1,0:T(8,128)S(1)}, u32[]{:S(2)}, u32[]{:S(2)}) collective-permute-start(f32[16,512]{1,0:T(8,128)S(1)} %get-tuple-element.39), channel_id=1, source_target_pairs={{0,8},{1,9},{2,10},{3,11},{4,12},{5,13},{6,14},{7,15},{8,0},{9,1},... | collective-permute-start | bytes 98312 | tf_op jit(solution)/shard_map/ppermute | solution.py:312
  38.6 0.7 %collective-permute-start.10 = (f32[32,128]{1,0:T(8,128)S(1)}, f32[32,128]{1,0:T(8,128)S(1)}, u32[]{:S(2)}, u32[]{:S(2)}) collective-permute-start(f32[32,128]{1,0:T(8,128)S(1)} %get-tuple-element.40), channel_id=1, source_target_pairs={{0,1},{1,0},{2,3},{3,2},{4,5},{5,4},{6,7},{7,6},{8,9},{9,8},{10,11... | collective-permute-start | bytes 49160 | tf_op jit(solution)/shard_map/ppermute | solution.py:314
  39.2 1.8 %shard_map.78 = bf16[48,32,512]{2,1,0:T(8,128)(2,1)} custom-call(bf16[768,1024]{1,0:T(8,128)(2,1)S(1)} %get-tuple-element.26.w_ref, f32[48,32,512]{2,1,0:T(8,128)S(1)} %get-tuple-element.32.series_ref, bf16[8,32,512]{2,1,0:T(8,128)(2,1)S(1)} %collective-permute-done.4.refs_0_, bf16[8,32,512]{2,1,0:T(8,128)(2,1)S(1)} %collective-permute-done.5.refs_1_, ...), custom_call_target="tpu_custom_call" | custom-call | flops 805306368 | bytes 1572864 | tf_op jit(solution)/shard_map/pallas_call | solution.py:315
  41.0 1.3 %collective-permute-done.10.left_ref = f32[32,128]{1,0:T(8,128)S(1)} collective-permute-done((f32[32,128]{1,0:T(8,128)S(1)}, f32[32,128]{1,0:T(8,128)S(1)}, u32[]{:S(2)}, u32[]{:S(2)}) %collective-permute-start.10) | collective-permute-done | bytes 16416 | tf_op jit(solution)/shard_map/ppermute | solution.py:314
  42.3 0.0 collective-permute-done.8.two_ref
  42.3 0.0 collective-permute-done.9.one_ref
  42.3 0.0 collective-permute-done.7.right_ref
  42.3 0.9 %shard_map.80 = (f32[32,512]{1,0:T(8,128)}, f32[32,512]{1,0:T(8,128)}) custom-call(f32[32,512]{1,0:T(8,128)S(1)} %get-tuple-element.36.v_ref, f32[72,128]{1,0:T(8,128)S(1)} %collective-permute-done.7.right_ref, f32[16,512]{1,0:T(8,128)S(1)} %collective-permute-done.8.two_ref, f32[16,512]{1,0:T(8,128)S(1)} %collective-permute-done.9.one_ref, ...), custom_call_target="tpu_custom_call" | custom-call | flops 6553600 | bytes 262144 | tf_op jit(solution)/shard_map/pallas_call | solution.py:328
  (5 shorter events, 0.0 us)
Async XLA Ops:
  0.6 19.8 %copy-start.2 = (bf16[48,64]{1,0:T(8,128)(2,1)S(1)}, bf16[48,64]{1,0:T(8,128)(2,1)}, u32[]{:S(2)}) copy-start(bf16[48,64]{1,0:T(8,128)(2,1)} %pinv_ref) | copy-start | bytes 18436
  0.6 19.7 %copy-start.3 = (f32[4,3]{1,0:T(4,128)S(1)}, f32[4,3]{1,0:T(4,128)}, u32[]{:S(2)}) copy-start(f32[4,3]{1,0:T(4,128)} %rot_ref) | copy-start | bytes 148
  0.7 19.7 %copy-start.1 = (s32[32,512]{1,0:T(8,128)S(1)}, s32[32,512]{1,0:T(8,128)}, u32[]{:S(2)}) copy-start(s32[32,512]{1,0:T(8,128)} %plate_ref) | copy-start | bytes 196612
  2.3 13.4 %collective-permute-start = (bf16[8,32,512]{2,1,0:T(8,128)(2,1)S(1)}, bf16[8,32,512]{2,1,0:T(8,128)(2,1)S(1)}, u32[]{:S(2)}, u32[]{:S(2)}) collective-permute-start(bf16[8,32,512]{2,1,0:T(8,128)(2,1)S(1)} %get-tuple-element.48), channel_id=1, source_target_pairs={{0,160},{8,168},{16,176},{24,184},{32,128},{40,136},{48,144},{56,1... | collective-permute-start | bytes 786440 | tf_op jit(solution)/shard_map/ppermute | solution.py:278
  8.1 18.1 %collective-permute-start.1 = (bf16[8,32,512]{2,1,0:T(8,128)(2,1)S(1)}, bf16[8,32,512]{2,1,0:T(8,128)(2,1)S(1)}, u32[]{:S(2)}, u32[]{:S(2)}) collective-permute-start(bf16[8,32,512]{2,1,0:T(8,128)(2,1)S(1)} %get-tuple-element.47), channel_id=1, source_target_pairs={{0,224},{8,104},{16,240},{24,120},{32,192},{40,72},{48,208},{56,88... | collective-permute-start | bytes 786440 | tf_op jit(solution)/shard_map/ppermute | solution.py:278
  9.0 20.7 %collective-permute-start.2 = (bf16[8,32,512]{2,1,0:T(8,128)(2,1)S(1)}, bf16[8,32,512]{2,1,0:T(8,128)(2,1)S(1)}, u32[]{:S(2)}, u32[]{:S(2)}) collective-permute-start(bf16[8,32,512]{2,1,0:T(8,128)(2,1)S(1)} %get-tuple-element.46), channel_id=1, source_target_pairs={{0,128},{8,136},{16,144},{24,152},{32,160},{40,168},{48,176},{56,1... | collective-permute-start | bytes 786440 | tf_op jit(solution)/shard_map/ppermute | solution.py:278
  10.5 19.1 %collective-permute-start.3 = (bf16[8,32,512]{2,1,0:T(8,128)(2,1)S(1)}, bf16[8,32,512]{2,1,0:T(8,128)(2,1)S(1)}, u32[]{:S(2)}, u32[]{:S(2)}) collective-permute-start(bf16[8,32,512]{2,1,0:T(8,128)(2,1)S(1)} %get-tuple-element.45), channel_id=1, source_target_pairs={{0,64},{8,200},{16,80},{24,216},{32,96},{40,232},{48,112},{56,248}... | collective-permute-start | bytes 786440 | tf_op jit(solution)/shard_map/ppermute | solution.py:278
  12.0 19.3 %collective-permute-start.4 = (bf16[8,32,512]{2,1,0:T(8,128)(2,1)S(1)}, bf16[8,32,512]{2,1,0:T(8,128)(2,1)S(1)}, u32[]{:S(2)}, u32[]{:S(2)}) collective-permute-start(bf16[8,32,512]{2,1,0:T(8,128)(2,1)S(1)} %get-tuple-element.44), channel_id=1, source_target_pairs={{0,32},{8,40},{16,48},{24,56},{32,0},{40,8},{48,16},{56,24},{64,96... | collective-permute-start | bytes 786440 | tf_op jit(solution)/shard_map/ppermute | solution.py:278
  15.7 16.6 %collective-permute-start.5 = (bf16[8,32,512]{2,1,0:T(8,128)(2,1)S(1)}, bf16[8,32,512]{2,1,0:T(8,128)(2,1)S(1)}, u32[]{:S(2)}, u32[]{:S(2)}) collective-permute-start(bf16[8,32,512]{2,1,0:T(8,128)(2,1)S(1)} %get-tuple-element.49), channel_id=1, source_target_pairs={{0,96},{8,232},{16,112},{24,248},{32,64},{40,200},{48,80},{56,216}... | collective-permute-start | bytes 786440 | tf_op jit(solution)/shard_map/ppermute | solution.py:278
  26.2 7.6 %collective-permute-start.6 = (bf16[8,32,512]{2,1,0:T(8,128)(2,1)S(1)}, bf16[8,32,512]{2,1,0:T(8,128)(2,1)S(1)}, u32[]{:S(2)}, u32[]{:S(2)}) collective-permute-start(bf16[8,32,512]{2,1,0:T(8,128)(2,1)S(1)} %get-tuple-element.43), channel_id=1, source_target_pairs={{0,192},{8,72},{16,208},{24,88},{32,224},{40,104},{48,240},{56,120... | collective-permute-start | bytes 786440 | tf_op jit(solution)/shard_map/ppermute | solution.py:278
  29.7 4.1 %copy-start = (s32[32,512]{1,0:T(8,128)S(1)}, s32[32,512]{1,0:T(8,128)}, u32[]{:S(2)}) copy-start(s32[32,512]{1,0:T(8,128)} %refs_3_) | copy-start | bytes 196612
  34.0 8.3 %collective-permute-start.7 = (f32[72,128]{1,0:T(8,128)S(1)}, f32[72,128]{1,0:T(8,128)S(1)}, u32[]{:S(2)}, u32[]{:S(2)}) collective-permute-start(f32[72,128]{1,0:T(8,128)S(1)} %get-tuple-element.37), channel_id=1, source_target_pairs={{0,8},{1,2},{2,1},{3,4},{4,3},{5,6},{6,5},{7,15},{8,0},{9,10},{10,... | collective-permute-start | bytes 110600 | tf_op jit(solution)/shard_map/ppermute | solution.py:311
  37.2 5.1 %collective-permute-start.8 = (f32[16,512]{1,0:T(8,128)S(1)}, f32[16,512]{1,0:T(8,128)S(1)}, u32[]{:S(2)}, u32[]{:S(2)}) collective-permute-start(f32[16,512]{1,0:T(8,128)S(1)} %get-tuple-element.38), channel_id=1, source_target_pairs={{0,1},{1,0},{2,3},{3,2},{4,5},{5,4},{6,7},{7,6},{8,16},{9,17},{10,... | collective-permute-start | bytes 98312 | tf_op jit(solution)/shard_map/ppermute | solution.py:313
  37.2 5.1 %collective-permute-start.9 = (f32[16,512]{1,0:T(8,128)S(1)}, f32[16,512]{1,0:T(8,128)S(1)}, u32[]{:S(2)}, u32[]{:S(2)}) collective-permute-start(f32[16,512]{1,0:T(8,128)S(1)} %get-tuple-element.39), channel_id=1, source_target_pairs={{0,8},{1,9},{2,10},{3,11},{4,12},{5,13},{6,14},{7,15},{8,0},{9,1},... | collective-permute-start | bytes 98312 | tf_op jit(solution)/shard_map/ppermute | solution.py:312
  38.6 3.7 %collective-permute-start.10 = (f32[32,128]{1,0:T(8,128)S(1)}, f32[32,128]{1,0:T(8,128)S(1)}, u32[]{:S(2)}, u32[]{:S(2)}) collective-permute-start(f32[32,128]{1,0:T(8,128)S(1)} %get-tuple-element.40), channel_id=1, source_target_pairs={{0,1},{1,0},{2,3},{3,2},{4,5},{5,4},{6,7},{7,6},{8,9},{9,8},{10,11... | collective-permute-start | bytes 49160 | tf_op jit(solution)/shard_map/ppermute | solution.py:314

commit v4 on v3

--- a/solution.py
+++ b/solution.py
@@ -13,7 +13,7 @@
 F32 = jnp.float32
 BF16 = jnp.bfloat16
 VMEM_BYTES = 40 << 20
-WIDE = 72
+EXTRA = 8
 CUT = 16
 
 FLOWS = {
@@ -26,10 +26,10 @@
     "Xa": ("a", 0),
     "Xb": ("b", 0),
 }
-EARLY = ("D2", "Db", "X2", "Xa")
-LATE = ("Y2", "Da", "Xb")
+EARLY = ("D2", "Xa", "Db", "X2")
+LATE = ("Da", "Y2", "Xb")
 ORDER = ("own",) + EARLY + LATE
-STARTS = ("D2", "Db", "X2", "Y2", "Da", "Xa", "Xb")
+STARTS = EARLY + LATE
 
 
 def along_x(step, x, core, pick):
@@ -169,9 +169,9 @@
     first, last = v_ref[:, :LANES], v_ref[:, cols - LANES :]
     one_ref[...] = jnp.where(core == 0, low, top)
     two_ref[...] = jnp.where(core == 0, top, low)
-    left_ref[...] = jnp.where(column == 0, last, first)
+    left_ref[:rows, :] = jnp.where(column == 0, last, first)
+    left_ref[rows:, :] = jnp.zeros((EXTRA, LANES), F32)
     right_ref[:rows, :] = jnp.where(column == 0, first, last)
-    right_ref[rows:, :] = jnp.zeros((WIDE - rows, LANES), F32)
 
 
 def stacked(blocks, part):
@@ -234,7 +234,7 @@
     for part in three_parts(upright):
         total = total + jnp.dot(taps, part, preferred_element_type=F32)
     rows_ref[...] = total * scale
-    first, second = left_ref[...], right_ref[:rows, :]
+    first, second = left_ref[:rows, :], right_ref[:rows, :]
     before = jnp.where(place == 0, 0.0, jnp.where(column == 0, second, first))
     after = jnp.where(place == columns - 1, 0.0, jnp.where(column == 0, first, second))
     sideways = jnp.concatenate([before, v, after], axis=1)
@@ -301,7 +301,7 @@
     velocity, one, two, left, right = call(
         rate_kernel,
         [VMEM] * (4 + len(late)),
-        (shape(rows, cols), shape(REACH, cols), shape(REACH, cols), shape(rows, LANES), shape(WIDE, LANES)),
+        (shape(rows, cols), shape(REACH, cols), shape(REACH, cols), shape(rows + EXTRA, LANES), shape(rows, LANES)),
         2 * ifg * rows * cols,
         2 * ifg * rows * cols,
     )(weight, rate, *late, coherent, plate_rate)

time: 43.9 us -> 41.3 us (0.941)
  waiting for transfers between devices: 9.28 us -> 6.36 us
    ppermute x7, waiting for transfers between devices: 8 us -> 6.35 us  [on_device(): lax.ppermute(sent[name], both, swap_pairs(name))]
    ppermute x1, waiting for transfers between devices: 1.27 us -> 0.01 us  [on_device(): left = lax.ppermute(left, everywhere, neighbour_pairs(tiles, columns, 1, 0))]
    ppermute x1, starting transfers between devices: 3.22 us -> 3.81 us  [on_device(): lax.ppermute(right, everywhere, neighbour_pairs(tiles, columns, 1, 1))]
    ppermute x7, starting transfers between devices: 20 us -> 19.5 us  [on_device(): lax.ppermute(sent[name], both, swap_pairs(name))]
  transfers between devices with their start and end apart: 11 -> 11, of which waited for: 5 -> 4; matrix products, arithmetic and copies ran while one was open for 2% -> 2% of each run, Pallas kernels for 10% -> 10%
where the time goes in v4:
time: 41.3 us; the launch traced here: 40.5 us
  starting transfers between devices  25.4 us (62%)
  waiting for transfers between devices  6.36 us (15%)
  Pallas kernels  5.34 us (13%)
  local copies, waits for them, and re-layouts  2.63 us (6%)
  between operations  0.77 us (2%)
    ppermute x7, starting transfers between devices, on_device(): lax.ppermute(sent[name], both, swap_pairs(name))  19.5 us
    ppermute x7, waiting for transfers between devices, on_device(): lax.ppermute(sent[name], both, swap_pairs(name))  6.35 us
    ppermute x1, starting transfers between devices, on_device(): lax.ppermute(right, everywhere, neighbour_pairs(tiles, columns, 1, 1))  3.81 us
    squeeze x2, local copies, waits for them, and re-layouts, cut(): lax.dynamic_index_in_dim(phase, partner(name, x, y, core, jnp.where), 1,...  2.62 us
    pallas_call x1, Pallas kernels, on_device(): call(displacement_kernel, [VMEM] * (2 + len(late)), shape(epochs, rows, c...  1.8 us
    ppermute x1, starting transfers between devices, on_device(): one = lax.ppermute(one, everywhere, neighbour_pairs(tiles, columns, 0, 0))  1.58 us
    pallas_call x1, Pallas kernels, on_device(): call(series_kernel, [VMEM] * (2 + len(early)), (shape(epochs, rows, cols)...  1.53 us
    pallas_call x1, Pallas kernels, on_device(): call(gradient_kernel, [VMEM] * 5, (shape(rows, cols), shape(rows, cols)),...  0.93 us
  transfers between devices with their start and end apart: 11, of which 4 were waited for; matrix products, arithmetic and copies ran while one was open for 2% of the time, Pallas kernels for 10%

profile of v4, /device:TPU:96, one launch (start us, length us, event | category | flops | bytes accessed | tf_op | source)
XLA Modules:
  0.0 40.5 jit_solution(5508261875826507615)
XLA Ops:
  0.6 0.0 copy-start.2
  0.6 0.0 copy-start.3
  0.7 0.0 copy-start.1
  0.7 1.6 %dynamic-slice_bitcast_fusion = (bf16[8,32,512]{2,1,0:T(8,128)(2,1)S(1)}, bf16[8,32,512]{2,1,0:T(8,128)(2,1)S(1)}, bf16[8,32,512]{2,1,0:T(8,128)(2,1)S(1)}, bf16...) fusion(bf16[8,8,32,512]{3,2,1,0:T(8,128)(2,1)} %param.5, ...), kind=kLoop, calls=%fused_computation | loop fusion | bytes 3670044 | tf_op jit(solution)/shard_map/jit(dynamic_index_in_dim)/squeeze | solution.py:275
  2.3 5.7 %collective-permute-start = (bf16[8,32,512]{2,1,0:T(8,128)(2,1)S(1)}, bf16[8,32,512]{2,1,0:T(8,128)(2,1)S(1)}, u32[]{:S(2)}, u32[]{:S(2)}) collective-permute-start(bf16[8,32,512]{2,1,0:T(8,128)(2,1)S(1)} %get-tuple-element.48), channel_id=1, source_target_pairs={{0,160},{8,168},{16,176},{24,184},{32,128},{40,136},{48,144},{56,1... | collective-permute-start | bytes 786440 | tf_op jit(solution)/shard_map/ppermute | solution.py:278
  8.1 0.6 %collective-permute-start.1 = (bf16[8,32,512]{2,1,0:T(8,128)(2,1)S(1)}, bf16[8,32,512]{2,1,0:T(8,128)(2,1)S(1)}, u32[]{:S(2)}, u32[]{:S(2)}) collective-permute-start(bf16[8,32,512]{2,1,0:T(8,128)(2,1)S(1)} %get-tuple-element.47), channel_id=1, source_target_pairs={{0,64},{8,200},{16,80},{24,216},{32,96},{40,232},{48,112},{56,248}... | collective-permute-start | bytes 786440 | tf_op jit(solution)/shard_map/ppermute | solution.py:278
  8.7 0.3 collective-permute-start.2
  9.0 3.0 %collective-permute-start.3 = (bf16[8,32,512]{2,1,0:T(8,128)(2,1)S(1)}, bf16[8,32,512]{2,1,0:T(8,128)(2,1)S(1)}, u32[]{:S(2)}, u32[]{:S(2)}) collective-permute-start(bf16[8,32,512]{2,1,0:T(8,128)(2,1)S(1)} %get-tuple-element.45), channel_id=1, source_target_pairs={{0,128},{8,136},{16,144},{24,152},{32,160},{40,168},{48,176},{56,1... | collective-permute-start | bytes 786440 | tf_op jit(solution)/shard_map/ppermute | solution.py:278
  12.0 3.2 %collective-permute-start.4 = (bf16[8,32,512]{2,1,0:T(8,128)(2,1)S(1)}, bf16[8,32,512]{2,1,0:T(8,128)(2,1)S(1)}, u32[]{:S(2)}, u32[]{:S(2)}) collective-permute-start(bf16[8,32,512]{2,1,0:T(8,128)(2,1)S(1)} %get-tuple-element.44), channel_id=1, source_target_pairs={{0,96},{8,232},{16,112},{24,248},{32,64},{40,200},{48,80},{56,216}... | collective-permute-start | bytes 786440 | tf_op jit(solution)/shard_map/ppermute | solution.py:278
  15.2 0.0 collective-permute-done.refs_1_
  15.2 4.1 %collective-permute-start.5 = (bf16[8,32,512]{2,1,0:T(8,128)(2,1)S(1)}, bf16[8,32,512]{2,1,0:T(8,128)(2,1)S(1)}, u32[]{:S(2)}, u32[]{:S(2)}) collective-permute-start(bf16[8,32,512]{2,1,0:T(8,128)(2,1)S(1)} %get-tuple-element.49), channel_id=1, source_target_pairs={{0,32},{8,40},{16,48},{24,56},{32,0},{40,8},{48,16},{56,24},{64,96... | collective-permute-start | bytes 786440 | tf_op jit(solution)/shard_map/ppermute | solution.py:278
  19.3 0.9 %shard_map.76 = (bf16[768,1024]{1,0:T(8,128)(2,1)S(1)}, f32[32,512]{1,0:T(8,128)S(1)}, f32[64,128]{1,0:T(8,128)S(1)}) custom-call(f32[4,3]{1,0:T(4,128)S(1)} %copy-done.3, bf16[48,64]{1,0:T(8,128)(2,1)S(1)} %copy-done.2, s32[32,512]{1,0:T(8,128)S(1)} %copy-done.1), custom_call_target="tpu_custom_call" | custom-call | flops 100663296 | bytes 1572864 | tf_op jit(solution)/shard_map/pallas_call | solution.py:284
  20.3 1.2 %collective-permute-done.1.refs_2_ = bf16[8,32,512]{2,1,0:T(8,128)(2,1)S(1)} collective-permute-done((bf16[8,32,512]{2,1,0:T(8,128)(2,1)S(1)}, bf16[8,32,512]{2,1,0:T(8,128)(2,1)S(1)}, u32[]{:S(2)}, u32[]{:S(2)}) %collective-permute-start.1) | collective-permute-done | bytes 262176 | tf_op jit(solution)/shard_map/ppermute | solution.py:278
  21.5 2.5 %collective-permute-start.6 = (bf16[8,32,512]{2,1,0:T(8,128)(2,1)S(1)}, bf16[8,32,512]{2,1,0:T(8,128)(2,1)S(1)}, u32[]{:S(2)}, u32[]{:S(2)}) collective-permute-start(bf16[8,32,512]{2,1,0:T(8,128)(2,1)S(1)} %get-tuple-element.43), channel_id=1, source_target_pairs={{0,192},{8,72},{16,208},{24,88},{32,224},{40,104},{48,240},{56,120... | collective-permute-start | bytes 786440 | tf_op jit(solution)/shard_map/ppermute | solution.py:278
  24.0 1.0 %dynamic-slice_bitcast_fusion.6.refs_0_ = bf16[8,32,512]{2,1,0:T(8,128)(2,1)S(1)} fusion(bf16[8,8,32,512]{3,2,1,0:T(8,128)(2,1)} %param.5, s32[]{:T(128)S(6)} %select_n.35), kind=kLoop, calls=%fused_computation.6 | loop fusion | bytes 524292 | tf_op jit(solution)/shard_map/jit(dynamic_index_in_dim)/squeeze | solution.py:275
  25.0 2.5 %collective-permute-done.2.refs_3_ = bf16[8,32,512]{2,1,0:T(8,128)(2,1)S(1)} collective-permute-done((bf16[8,32,512]{2,1,0:T(8,128)(2,1)S(1)}, bf16[8,32,512]{2,1,0:T(8,128)(2,1)S(1)}, u32[]{:S(2)}, u32[]{:S(2)}) %collective-permute-start.2) | collective-permute-done | bytes 262176 | tf_op jit(solution)/shard_map/ppermute | solution.py:278
  27.5 0.0 collective-permute-done.3.refs_4_
  27.5 1.5 %shard_map.77 = (f32[48,32,512]{2,1,0:T(8,128)S(1)}, f32[32,512]{1,0:T(8,128)S(1)}) custom-call(bf16[768,1024]{1,0:T(8,128)(2,1)S(1)} %get-tuple-element.26.w_ref, f32[64,128]{1,0:T(8,128)S(1)} %get-tuple-element.27.weight_ref, bf16[8,32,512]{2,1,0:T(8,128)(2,1)S(1)} %dynamic-slice_bitcast_fusion.6.refs_0_, ...), custom_call_target="tpu_custom_call" | custom-call | flops 1610612736 | bytes 2097152 | tf_op jit(solution)/shard_map/pallas_call | solution.py:292
  29.0 2.4 %collective-permute-done.4.refs_0_ = bf16[8,32,512]{2,1,0:T(8,128)(2,1)S(1)} collective-permute-done((bf16[8,32,512]{2,1,0:T(8,128)(2,1)S(1)}, bf16[8,32,512]{2,1,0:T(8,128)(2,1)S(1)}, u32[]{:S(2)}, u32[]{:S(2)}) %collective-permute-start.4) | collective-permute-done | bytes 262176 | tf_op jit(solution)/shard_map/ppermute | solution.py:278
  31.4 0.2 collective-permute-done.5.refs_1_
  31.6 0.0 collective-permute-done.6.refs_2_
  31.6 0.2 shard_map.79
  31.8 0.2 collective-permute-start.8
  32.0 1.6 %collective-permute-start.9 = (f32[16,512]{1,0:T(8,128)S(1)}, f32[16,512]{1,0:T(8,128)S(1)}, u32[]{:S(2)}, u32[]{:S(2)}) collective-permute-start(f32[16,512]{1,0:T(8,128)S(1)} %get-tuple-element.39), channel_id=1, source_target_pairs={{0,8},{1,9},{2,10},{3,11},{4,12},{5,13},{6,14},{7,15},{8,0},{9,1},... | collective-permute-start | bytes 98312 | tf_op jit(solution)/shard_map/ppermute | solution.py:312
  33.6 0.3 collective-permute-start.10
  33.9 3.8 %collective-permute-start.7 = (f32[32,128]{1,0:T(8,128)S(1)}, f32[32,128]{1,0:T(8,128)S(1)}, u32[]{:S(2)}, u32[]{:S(2)}) collective-permute-start(f32[32,128]{1,0:T(8,128)S(1)} %get-tuple-element.37), channel_id=1, source_target_pairs={{0,8},{1,2},{2,1},{3,4},{4,3},{5,6},{6,5},{7,15},{8,0},{9,10},{10,... | collective-permute-start | bytes 49160 | tf_op jit(solution)/shard_map/ppermute | solution.py:311
  37.7 1.8 %shard_map.78 = bf16[48,32,512]{2,1,0:T(8,128)(2,1)} custom-call(bf16[768,1024]{1,0:T(8,128)(2,1)S(1)} %get-tuple-element.26.w_ref, f32[48,32,512]{2,1,0:T(8,128)S(1)} %get-tuple-element.32.series_ref, bf16[8,32,512]{2,1,0:T(8,128)(2,1)S(1)} %collective-permute-done.4.refs_0_, bf16[8,32,512]{2,1,0:T(8,128)(2,1)S(1)} %collective-permute-done.5.refs_1_, ...), custom_call_target="tpu_custom_call" | custom-call | flops 805306368 | bytes 1572864 | tf_op jit(solution)/shard_map/pallas_call | solution.py:315
  39.5 0.0 collective-permute-done.7.right_ref
  39.5 0.0 collective-permute-done.10.left_ref
  39.5 0.0 collective-permute-done.8.two_ref
  39.6 0.0 collective-permute-done.9.one_ref
  39.6 0.9 %shard_map.80 = (f32[32,512]{1,0:T(8,128)}, f32[32,512]{1,0:T(8,128)}) custom-call(f32[32,512]{1,0:T(8,128)S(1)} %get-tuple-element.36.v_ref, f32[32,128]{1,0:T(8,128)S(1)} %collective-permute-done.7.right_ref, f32[16,512]{1,0:T(8,128)S(1)} %collective-permute-done.8.two_ref, f32[16,512]{1,0:T(8,128)S(1)} %collective-permute-done.9.one_ref, ...), custom_call_target="tpu_custom_call" | custom-call | flops 6553600 | bytes 262144 | tf_op jit(solution)/shard_map/pallas_call | solution.py:328
  (5 shorter events, 0.0 us)
Async XLA Ops:
  0.6 18.7 %copy-start.2 = (bf16[48,64]{1,0:T(8,128)(2,1)S(1)}, bf16[48,64]{1,0:T(8,128)(2,1)}, u32[]{:S(2)}) copy-start(bf16[48,64]{1,0:T(8,128)(2,1)} %pinv_ref) | copy-start | bytes 18436
  0.6 18.7 %copy-start.3 = (f32[4,3]{1,0:T(4,128)S(1)}, f32[4,3]{1,0:T(4,128)}, u32[]{:S(2)}) copy-start(f32[4,3]{1,0:T(4,128)} %rot_ref) | copy-start | bytes 148
  0.7 18.7 %copy-start.1 = (s32[32,512]{1,0:T(8,128)S(1)}, s32[32,512]{1,0:T(8,128)}, u32[]{:S(2)}) copy-start(s32[32,512]{1,0:T(8,128)} %plate_ref) | copy-start | bytes 196612
  2.3 12.8 %collective-permute-start = (bf16[8,32,512]{2,1,0:T(8,128)(2,1)S(1)}, bf16[8,32,512]{2,1,0:T(8,128)(2,1)S(1)}, u32[]{:S(2)}, u32[]{:S(2)}) collective-permute-start(bf16[8,32,512]{2,1,0:T(8,128)(2,1)S(1)} %get-tuple-element.48), channel_id=1, source_target_pairs={{0,160},{8,168},{16,176},{24,184},{32,128},{40,136},{48,144},{56,1... | collective-permute-start | bytes 786440 | tf_op jit(solution)/shard_map/ppermute | solution.py:278
  8.1 13.4 %collective-permute-start.1 = (bf16[8,32,512]{2,1,0:T(8,128)(2,1)S(1)}, bf16[8,32,512]{2,1,0:T(8,128)(2,1)S(1)}, u32[]{:S(2)}, u32[]{:S(2)}) collective-permute-start(bf16[8,32,512]{2,1,0:T(8,128)(2,1)S(1)} %get-tuple-element.47), channel_id=1, source_target_pairs={{0,64},{8,200},{16,80},{24,216},{32,96},{40,232},{48,112},{56,248}... | collective-permute-start | bytes 786440 | tf_op jit(solution)/shard_map/ppermute | solution.py:278
  8.7 18.8 %collective-permute-start.2 = (bf16[8,32,512]{2,1,0:T(8,128)(2,1)S(1)}, bf16[8,32,512]{2,1,0:T(8,128)(2,1)S(1)}, u32[]{:S(2)}, u32[]{:S(2)}) collective-permute-start(bf16[8,32,512]{2,1,0:T(8,128)(2,1)S(1)} %get-tuple-element.46), channel_id=1, source_target_pairs={{0,224},{8,104},{16,240},{24,120},{32,192},{40,72},{48,208},{56,88... | collective-permute-start | bytes 786440 | tf_op jit(solution)/shard_map/ppermute | solution.py:278
  9.0 18.5 %collective-permute-start.3 = (bf16[8,32,512]{2,1,0:T(8,128)(2,1)S(1)}, bf16[8,32,512]{2,1,0:T(8,128)(2,1)S(1)}, u32[]{:S(2)}, u32[]{:S(2)}) collective-permute-start(bf16[8,32,512]{2,1,0:T(8,128)(2,1)S(1)} %get-tuple-element.45), channel_id=1, source_target_pairs={{0,128},{8,136},{16,144},{24,152},{32,160},{40,168},{48,176},{56,1... | collective-permute-start | bytes 786440 | tf_op jit(solution)/shard_map/ppermute | solution.py:278
  12.0 19.5 %collective-permute-start.4 = (bf16[8,32,512]{2,1,0:T(8,128)(2,1)S(1)}, bf16[8,32,512]{2,1,0:T(8,128)(2,1)S(1)}, u32[]{:S(2)}, u32[]{:S(2)}) collective-permute-start(bf16[8,32,512]{2,1,0:T(8,128)(2,1)S(1)} %get-tuple-element.44), channel_id=1, source_target_pairs={{0,96},{8,232},{16,112},{24,248},{32,64},{40,200},{48,80},{56,216}... | collective-permute-start | bytes 786440 | tf_op jit(solution)/shard_map/ppermute | solution.py:278
  15.2 16.4 %collective-permute-start.5 = (bf16[8,32,512]{2,1,0:T(8,128)(2,1)S(1)}, bf16[8,32,512]{2,1,0:T(8,128)(2,1)S(1)}, u32[]{:S(2)}, u32[]{:S(2)}) collective-permute-start(bf16[8,32,512]{2,1,0:T(8,128)(2,1)S(1)} %get-tuple-element.49), channel_id=1, source_target_pairs={{0,32},{8,40},{16,48},{24,56},{32,0},{40,8},{48,16},{56,24},{64,96... | collective-permute-start | bytes 786440 | tf_op jit(solution)/shard_map/ppermute | solution.py:278
  21.5 10.1 %collective-permute-start.6 = (bf16[8,32,512]{2,1,0:T(8,128)(2,1)S(1)}, bf16[8,32,512]{2,1,0:T(8,128)(2,1)S(1)}, u32[]{:S(2)}, u32[]{:S(2)}) collective-permute-start(bf16[8,32,512]{2,1,0:T(8,128)(2,1)S(1)} %get-tuple-element.43), channel_id=1, source_target_pairs={{0,192},{8,72},{16,208},{24,88},{32,224},{40,104},{48,240},{56,120... | collective-permute-start | bytes 786440 | tf_op jit(solution)/shard_map/ppermute | solution.py:278
  27.5 4.1 %copy-start = (s32[32,512]{1,0:T(8,128)S(1)}, s32[32,512]{1,0:T(8,128)}, u32[]{:S(2)}) copy-start(s32[32,512]{1,0:T(8,128)} %refs_3_) | copy-start | bytes 196612
  31.8 7.8 %collective-permute-start.8 = (f32[16,512]{1,0:T(8,128)S(1)}, f32[16,512]{1,0:T(8,128)S(1)}, u32[]{:S(2)}, u32[]{:S(2)}) collective-permute-start(f32[16,512]{1,0:T(8,128)S(1)} %get-tuple-element.38), channel_id=1, source_target_pairs={{0,1},{1,0},{2,3},{3,2},{4,5},{5,4},{6,7},{7,6},{8,16},{9,17},{10,... | collective-permute-start | bytes 98312 | tf_op jit(solution)/shard_map/ppermute | solution.py:313
  32.0 7.6 %collective-permute-start.9 = (f32[16,512]{1,0:T(8,128)S(1)}, f32[16,512]{1,0:T(8,128)S(1)}, u32[]{:S(2)}, u32[]{:S(2)}) collective-permute-start(f32[16,512]{1,0:T(8,128)S(1)} %get-tuple-element.39), channel_id=1, source_target_pairs={{0,8},{1,9},{2,10},{3,11},{4,12},{5,13},{6,14},{7,15},{8,0},{9,1},... | collective-permute-start | bytes 98312 | tf_op jit(solution)/shard_map/ppermute | solution.py:312
  33.6 6.0 %collective-permute-start.10 = (f32[40,128]{1,0:T(8,128)S(1)}, f32[40,128]{1,0:T(8,128)S(1)}, u32[]{:S(2)}, u32[]{:S(2)}) collective-permute-start(f32[40,128]{1,0:T(8,128)S(1)} %get-tuple-element.40), channel_id=1, source_target_pairs={{0,1},{1,0},{2,3},{3,2},{4,5},{5,4},{6,7},{7,6},{8,9},{9,8},{10,11... | collective-permute-start | bytes 61448 | tf_op jit(solution)/shard_map/ppermute | solution.py:314
  33.9 5.6 %collective-permute-start.7 = (f32[32,128]{1,0:T(8,128)S(1)}, f32[32,128]{1,0:T(8,128)S(1)}, u32[]{:S(2)}, u32[]{:S(2)}) collective-permute-start(f32[32,128]{1,0:T(8,128)S(1)} %get-tuple-element.37), channel_id=1, source_target_pairs={{0,8},{1,2},{2,1},{3,4},{4,3},{5,6},{6,5},{7,15},{8,0},{9,10},{10,... | collective-permute-start | bytes 49160 | tf_op jit(solution)/shard_map/ppermute | solution.py:311

commit v5 on v4

--- a/solution.py
+++ b/solution.py
@@ -271,13 +271,17 @@
     both = ("grp", "row")
     tall, deep = epochs * SUB, ifg * SUB
     x, y, core = place_here()
+
     def cut(name):
         return lax.dynamic_index_in_dim(phase, partner(name, x, y, core, jnp.where), 1, keepdims=False)
 
-    sent = {name: cut(name) for name in STARTS}
-    got = {name: lax.ppermute(sent[name], both, swap_pairs(name)) for name in STARTS}
+    def send(names):
+        return {name: lax.ppermute(cut(name), both, swap_pairs(name)) for name in names}
+
+    got = send(EARLY + LATE[:1])
     later = (got[STARTS[0]], phase, pseudo_inverse, rotation, plate_id, coherent)
     got[STARTS[0]], phase, pseudo_inverse, rotation, plate_id, coherent = lax.optimization_barrier(later)
+    got.update(send(LATE[1:]))
     early = [cut("own")] + [got[name] for name in EARLY]
     late = [got[name] for name in LATE]
 

time: 41.3 us -> 41.1 us (level)
  waiting for transfers between devices: 6.36 us -> 5.84 us
    ppermute x7, waiting for transfers between devices: 6.35 us -> 5.83 us  [send(): lax.ppermute(cut(name), both, swap_pairs(name))]
  transfers between devices with their start and end apart: 11 -> 11, of which waited for: 4 -> 4; matrix products, arithmetic and copies ran while one was open for 2% -> 3% of each run, Pallas kernels for 10% -> 11%
where the time goes in v5:
time: 41.1 us; the launch traced here: 40.3 us
  starting transfers between devices  25.7 us (63%)
  waiting for transfers between devices  5.84 us (14%)
  Pallas kernels  5.34 us (13%)
  local copies, waits for them, and re-layouts  2.63 us (6%)
  between operations  0.77 us (2%)
    ppermute x7, starting transfers between devices, send(): lax.ppermute(cut(name), both, swap_pairs(name))  19.8 us
    ppermute x7, waiting for transfers between devices, send(): lax.ppermute(cut(name), both, swap_pairs(name))  5.83 us
    ppermute x1, starting transfers between devices, on_device(): lax.ppermute(right, everywhere, neighbour_pairs(tiles, columns, 1, 1))  3.79 us
    squeeze x2, local copies, waits for them, and re-layouts, cut(): lax.dynamic_index_in_dim(phase, partner(name, x, y, core, jnp.where), 1,...  2.61 us
    pallas_call x1, Pallas kernels, on_device(): call(displacement_kernel, [VMEM] * (2 + len(late)), shape(epochs, rows, c...  1.8 us
    ppermute x1, starting transfers between devices, on_device(): one = lax.ppermute(one, everywhere, neighbour_pairs(tiles, columns, 0, 0))  1.56 us
    pallas_call x1, Pallas kernels, on_device(): call(series_kernel, [VMEM] * (2 + len(early)), (shape(epochs, rows, cols)...  1.53 us
    pallas_call x1, Pallas kernels, on_device(): call(gradient_kernel, [VMEM] * 5, (shape(rows, cols), shape(rows, cols)),...  0.93 us
  transfers between devices with their start and end apart: 11, of which 4 were waited for; matrix products, arithmetic and copies ran while one was open for 3% of the time, Pallas kernels for 11%

profile of v5, /device:TPU:96, one launch (start us, length us, event | category | flops | bytes accessed | tf_op | source)
XLA Modules:
  0.0 40.3 jit_solution(294793116574786865)
XLA Ops:
  0.7 0.0 copy-start.1
  0.7 0.0 copy-start.2
  0.7 0.0 copy-start.3
  0.7 1.4 %dynamic-slice_bitcast_fusion.2 = (bf16[8,32,512]{2,1,0:T(8,128)(2,1)S(1)}, bf16[8,32,512]{2,1,0:T(8,128)(2,1)S(1)}, bf16[8,32,512]{2,1,0:T(8,128)(2,1)S(1)}, bf...) fusion(bf16[8,8,32,512]{3,2,1,0:T(8,128)(2,1)} %param.5, s32[]{:T(128)S(6)} %select_n.41, s32[]{:T(128)S(6)} %select_n.39, ...), kind=kLoop, calls=%fused_computation.2 | loop fusion | bytes 2621460 | tf_op jit(solution)/shard_map/jit(dynamic_index_in_dim)/squeeze | solution.py:276
  2.1 5.7 %collective-permute-start = (bf16[8,32,512]{2,1,0:T(8,128)(2,1)S(1)}, bf16[8,32,512]{2,1,0:T(8,128)(2,1)S(1)}, u32[]{:S(2)}, u32[]{:S(2)}) collective-permute-start(bf16[8,32,512]{2,1,0:T(8,128)(2,1)S(1)} %get-tuple-element.49), channel_id=1, source_target_pairs={{0,160},{8,168},{16,176},{24,184},{32,128},{40,136},{48,144},{56,1... | collective-permute-start | bytes 786440 | tf_op jit(solution)/shard_map/ppermute | solution.py:279
  7.9 0.6 %collective-permute-start.1 = (bf16[8,32,512]{2,1,0:T(8,128)(2,1)S(1)}, bf16[8,32,512]{2,1,0:T(8,128)(2,1)S(1)}, u32[]{:S(2)}, u32[]{:S(2)}) collective-permute-start(bf16[8,32,512]{2,1,0:T(8,128)(2,1)S(1)} %get-tuple-element.48), channel_id=1, source_target_pairs={{0,64},{8,200},{16,80},{24,216},{32,96},{40,232},{48,112},{56,248}... | collective-permute-start | bytes 786440 | tf_op jit(solution)/shard_map/ppermute | solution.py:279
  8.5 0.3 collective-permute-start.2
  8.8 3.0 %collective-permute-start.3 = (bf16[8,32,512]{2,1,0:T(8,128)(2,1)S(1)}, bf16[8,32,512]{2,1,0:T(8,128)(2,1)S(1)}, u32[]{:S(2)}, u32[]{:S(2)}) collective-permute-start(bf16[8,32,512]{2,1,0:T(8,128)(2,1)S(1)} %get-tuple-element.50), channel_id=1, source_target_pairs={{0,128},{8,136},{16,144},{24,152},{32,160},{40,168},{48,176},{56,1... | collective-permute-start | bytes 786440 | tf_op jit(solution)/shard_map/ppermute | solution.py:279
  11.7 3.2 %collective-permute-start.4 = (bf16[8,32,512]{2,1,0:T(8,128)(2,1)S(1)}, bf16[8,32,512]{2,1,0:T(8,128)(2,1)S(1)}, u32[]{:S(2)}, u32[]{:S(2)}) collective-permute-start(bf16[8,32,512]{2,1,0:T(8,128)(2,1)S(1)} %get-tuple-element.46), channel_id=1, source_target_pairs={{0,96},{8,232},{16,112},{24,248},{32,64},{40,200},{48,80},{56,216}... | collective-permute-start | bytes 786440 | tf_op jit(solution)/shard_map/ppermute | solution.py:279
  15.0 0.0 collective-permute-done.refs_1_
  15.0 1.2 %dynamic-slice_bitcast_fusion = (bf16[8,32,512]{2,1,0:T(8,128)(2,1)S(1)}, bf16[8,32,512]{2,1,0:T(8,128)(2,1)S(1)}, bf16[8,32,512]{2,1,0:T(8,128)(2,1)S(1)}) fusion(bf16[8,8,32,512]{3,2,1,0:T(8,128)(2,1)} %param.5, s32[]{:T(128)S(6)} %select_n.43, s32[]{:T(128)S(6)} %select_n.42, s32[]{:T(128)S(6)} %select_n.35), kind=kLoop, calls=%fused_computation | loop fusion | bytes 1572876 | tf_op jit(solution)/shard_map/jit(dynamic_index_in_dim)/squeeze | solution.py:276
  16.2 4.2 %collective-permute-start.5 = (bf16[8,32,512]{2,1,0:T(8,128)(2,1)S(1)}, bf16[8,32,512]{2,1,0:T(8,128)(2,1)S(1)}, u32[]{:S(2)}, u32[]{:S(2)}) collective-permute-start(bf16[8,32,512]{2,1,0:T(8,128)(2,1)S(1)} %get-tuple-element.44), channel_id=1, source_target_pairs={{0,32},{8,40},{16,48},{24,56},{32,0},{40,8},{48,16},{56,24},{64,96... | collective-permute-start | bytes 786440 | tf_op jit(solution)/shard_map/ppermute | solution.py:279
  20.4 0.9 %collective-permute-done.1.refs_2_ = bf16[8,32,512]{2,1,0:T(8,128)(2,1)S(1)} collective-permute-done((bf16[8,32,512]{2,1,0:T(8,128)(2,1)S(1)}, bf16[8,32,512]{2,1,0:T(8,128)(2,1)S(1)}, u32[]{:S(2)}, u32[]{:S(2)}) %collective-permute-start.1) | collective-permute-done | bytes 262176 | tf_op jit(solution)/shard_map/ppermute | solution.py:279
  21.3 2.7 %collective-permute-start.6 = (bf16[8,32,512]{2,1,0:T(8,128)(2,1)S(1)}, bf16[8,32,512]{2,1,0:T(8,128)(2,1)S(1)}, u32[]{:S(2)}, u32[]{:S(2)}) collective-permute-start(bf16[8,32,512]{2,1,0:T(8,128)(2,1)S(1)} %get-tuple-element.43), channel_id=1, source_target_pairs={{0,192},{8,72},{16,208},{24,88},{32,224},{40,104},{48,240},{56,120... | collective-permute-start | bytes 786440 | tf_op jit(solution)/shard_map/ppermute | solution.py:279
  24.0 0.9 %shard_map.76 = (bf16[768,1024]{1,0:T(8,128)(2,1)S(1)}, f32[32,512]{1,0:T(8,128)S(1)}, f32[64,128]{1,0:T(8,128)S(1)}) custom-call(f32[4,3]{1,0:T(4,128)S(1)} %copy-done.3, bf16[48,64]{1,0:T(8,128)(2,1)S(1)} %copy-done.2, s32[32,512]{1,0:T(8,128)S(1)} %copy-done.1), custom_call_target="tpu_custom_call" | custom-call | flops 100663296 | bytes 1572864 | tf_op jit(solution)/shard_map/pallas_call | solution.py:288
  25.0 2.3 %collective-permute-done.2.refs_3_ = bf16[8,32,512]{2,1,0:T(8,128)(2,1)S(1)} collective-permute-done((bf16[8,32,512]{2,1,0:T(8,128)(2,1)S(1)}, bf16[8,32,512]{2,1,0:T(8,128)(2,1)S(1)}, u32[]{:S(2)}, u32[]{:S(2)}) %collective-permute-start.2) | collective-permute-done | bytes 262176 | tf_op jit(solution)/shard_map/ppermute | solution.py:279
  27.2 0.0 collective-permute-done.3.refs_4_
  27.2 1.5 %shard_map.77 = (f32[48,32,512]{2,1,0:T(8,128)S(1)}, f32[32,512]{1,0:T(8,128)S(1)}) custom-call(bf16[768,1024]{1,0:T(8,128)(2,1)S(1)} %get-tuple-element.26.w_ref, f32[64,128]{1,0:T(8,128)S(1)} %get-tuple-element.27.weight_ref, bf16[8,32,512]{2,1,0:T(8,128)(2,1)S(1)} %get-tuple-element.45.refs_0_, bf16[8,32,512]{2,1,0:T(8,128)(2,1)S(1)} %collective-permute-done.refs_1_, ...), custom_call_target="tpu_custom_call" | custom-call | flops 1610612736 | bytes 2097152 | tf_op jit(solution)/shard_map/pallas_call | solution.py:296
  28.8 2.4 %collective-permute-done.4.refs_0_ = bf16[8,32,512]{2,1,0:T(8,128)(2,1)S(1)} collective-permute-done((bf16[8,32,512]{2,1,0:T(8,128)(2,1)S(1)}, bf16[8,32,512]{2,1,0:T(8,128)(2,1)S(1)}, u32[]{:S(2)}, u32[]{:S(2)}) %collective-permute-start.4) | collective-permute-done | bytes 262176 | tf_op jit(solution)/shard_map/ppermute | solution.py:279
  31.2 0.2 collective-permute-done.5.refs_1_
  31.4 0.0 collective-permute-done.6.refs_2_
  31.4 0.2 shard_map.79
  31.6 0.2 collective-permute-start.8
  31.8 1.6 %collective-permute-start.9 = (f32[16,512]{1,0:T(8,128)S(1)}, f32[16,512]{1,0:T(8,128)S(1)}, u32[]{:S(2)}, u32[]{:S(2)}) collective-permute-start(f32[16,512]{1,0:T(8,128)S(1)} %get-tuple-element.39), channel_id=1, source_target_pairs={{0,8},{1,9},{2,10},{3,11},{4,12},{5,13},{6,14},{7,15},{8,0},{9,1},... | collective-permute-start | bytes 98312 | tf_op jit(solution)/shard_map/ppermute | solution.py:316
  33.4 0.4 collective-permute-start.10
  33.7 3.8 %collective-permute-start.7 = (f32[32,128]{1,0:T(8,128)S(1)}, f32[32,128]{1,0:T(8,128)S(1)}, u32[]{:S(2)}, u32[]{:S(2)}) collective-permute-start(f32[32,128]{1,0:T(8,128)S(1)} %get-tuple-element.37), channel_id=1, source_target_pairs={{0,8},{1,2},{2,1},{3,4},{4,3},{5,6},{6,5},{7,15},{8,0},{9,10},{10,... | collective-permute-start | bytes 49160 | tf_op jit(solution)/shard_map/ppermute | solution.py:315
  37.5 1.8 %shard_map.78 = bf16[48,32,512]{2,1,0:T(8,128)(2,1)} custom-call(bf16[768,1024]{1,0:T(8,128)(2,1)S(1)} %get-tuple-element.26.w_ref, f32[48,32,512]{2,1,0:T(8,128)S(1)} %get-tuple-element.32.series_ref, bf16[8,32,512]{2,1,0:T(8,128)(2,1)S(1)} %collective-permute-done.4.refs_0_, bf16[8,32,512]{2,1,0:T(8,128)(2,1)S(1)} %collective-permute-done.5.refs_1_, ...), custom_call_target="tpu_custom_call" | custom-call | flops 805306368 | bytes 1572864 | tf_op jit(solution)/shard_map/pallas_call | solution.py:319
  39.3 0.0 collective-permute-done.7.right_ref
  39.3 0.0 collective-permute-done.10.left_ref
  39.3 0.0 collective-permute-done.8.two_ref
  39.3 0.0 collective-permute-done.9.one_ref
  39.3 0.9 %shard_map.80 = (f32[32,512]{1,0:T(8,128)}, f32[32,512]{1,0:T(8,128)}) custom-call(f32[32,512]{1,0:T(8,128)S(1)} %get-tuple-element.36.v_ref, f32[32,128]{1,0:T(8,128)S(1)} %collective-permute-done.7.right_ref, f32[16,512]{1,0:T(8,128)S(1)} %collective-permute-done.8.two_ref, f32[16,512]{1,0:T(8,128)S(1)} %collective-permute-done.9.one_ref, ...), custom_call_target="tpu_custom_call" | custom-call | flops 6553600 | bytes 262144 | tf_op jit(solution)/shard_map/pallas_call | solution.py:332
  (5 shorter events, 0.0 us)
Async XLA Ops:
  0.7 23.4 %copy-start.1 = (s32[32,512]{1,0:T(8,128)S(1)}, s32[32,512]{1,0:T(8,128)}, u32[]{:S(2)}) copy-start(s32[32,512]{1,0:T(8,128)} %plate_ref) | copy-start | bytes 196612
  0.7 23.4 %copy-start.2 = (bf16[48,64]{1,0:T(8,128)(2,1)S(1)}, bf16[48,64]{1,0:T(8,128)(2,1)}, u32[]{:S(2)}) copy-start(bf16[48,64]{1,0:T(8,128)(2,1)} %pinv_ref) | copy-start | bytes 18436
  0.7 23.4 %copy-start.3 = (f32[4,3]{1,0:T(4,128)S(1)}, f32[4,3]{1,0:T(4,128)}, u32[]{:S(2)}) copy-start(f32[4,3]{1,0:T(4,128)} %rot_ref) | copy-start | bytes 148
  2.1 12.8 %collective-permute-start = (bf16[8,32,512]{2,1,0:T(8,128)(2,1)S(1)}, bf16[8,32,512]{2,1,0:T(8,128)(2,1)S(1)}, u32[]{:S(2)}, u32[]{:S(2)}) collective-permute-start(bf16[8,32,512]{2,1,0:T(8,128)(2,1)S(1)} %get-tuple-element.49), channel_id=1, source_target_pairs={{0,160},{8,168},{16,176},{24,184},{32,128},{40,136},{48,144},{56,1... | collective-permute-start | bytes 786440 | tf_op jit(solution)/shard_map/ppermute | solution.py:279
  7.9 13.4 %collective-permute-start.1 = (bf16[8,32,512]{2,1,0:T(8,128)(2,1)S(1)}, bf16[8,32,512]{2,1,0:T(8,128)(2,1)S(1)}, u32[]{:S(2)}, u32[]{:S(2)}) collective-permute-start(bf16[8,32,512]{2,1,0:T(8,128)(2,1)S(1)} %get-tuple-element.48), channel_id=1, source_target_pairs={{0,64},{8,200},{16,80},{24,216},{32,96},{40,232},{48,112},{56,248}... | collective-permute-start | bytes 786440 | tf_op jit(solution)/shard_map/ppermute | solution.py:279
  8.5 18.8 %collective-permute-start.2 = (bf16[8,32,512]{2,1,0:T(8,128)(2,1)S(1)}, bf16[8,32,512]{2,1,0:T(8,128)(2,1)S(1)}, u32[]{:S(2)}, u32[]{:S(2)}) collective-permute-start(bf16[8,32,512]{2,1,0:T(8,128)(2,1)S(1)} %get-tuple-element.47), channel_id=1, source_target_pairs={{0,224},{8,104},{16,240},{24,120},{32,192},{40,72},{48,208},{56,88... | collective-permute-start | bytes 786440 | tf_op jit(solution)/shard_map/ppermute | solution.py:279
  8.8 18.5 %collective-permute-start.3 = (bf16[8,32,512]{2,1,0:T(8,128)(2,1)S(1)}, bf16[8,32,512]{2,1,0:T(8,128)(2,1)S(1)}, u32[]{:S(2)}, u32[]{:S(2)}) collective-permute-start(bf16[8,32,512]{2,1,0:T(8,128)(2,1)S(1)} %get-tuple-element.50), channel_id=1, source_target_pairs={{0,128},{8,136},{16,144},{24,152},{32,160},{40,168},{48,176},{56,1... | collective-permute-start | bytes 786440 | tf_op jit(solution)/shard_map/ppermute | solution.py:279
  11.7 19.5 %collective-permute-start.4 = (bf16[8,32,512]{2,1,0:T(8,128)(2,1)S(1)}, bf16[8,32,512]{2,1,0:T(8,128)(2,1)S(1)}, u32[]{:S(2)}, u32[]{:S(2)}) collective-permute-start(bf16[8,32,512]{2,1,0:T(8,128)(2,1)S(1)} %get-tuple-element.46), channel_id=1, source_target_pairs={{0,96},{8,232},{16,112},{24,248},{32,64},{40,200},{48,80},{56,216}... | collective-permute-start | bytes 786440 | tf_op jit(solution)/shard_map/ppermute | solution.py:279
  16.2 15.3 %collective-permute-start.5 = (bf16[8,32,512]{2,1,0:T(8,128)(2,1)S(1)}, bf16[8,32,512]{2,1,0:T(8,128)(2,1)S(1)}, u32[]{:S(2)}, u32[]{:S(2)}) collective-permute-start(bf16[8,32,512]{2,1,0:T(8,128)(2,1)S(1)} %get-tuple-element.44), channel_id=1, source_target_pairs={{0,32},{8,40},{16,48},{24,56},{32,0},{40,8},{48,16},{56,24},{64,96... | collective-permute-start | bytes 786440 | tf_op jit(solution)/shard_map/ppermute | solution.py:279
  21.3 10.1 %collective-permute-start.6 = (bf16[8,32,512]{2,1,0:T(8,128)(2,1)S(1)}, bf16[8,32,512]{2,1,0:T(8,128)(2,1)S(1)}, u32[]{:S(2)}, u32[]{:S(2)}) collective-permute-start(bf16[8,32,512]{2,1,0:T(8,128)(2,1)S(1)} %get-tuple-element.43), channel_id=1, source_target_pairs={{0,192},{8,72},{16,208},{24,88},{32,224},{40,104},{48,240},{56,120... | collective-permute-start | bytes 786440 | tf_op jit(solution)/shard_map/ppermute | solution.py:279
  27.2 4.2 %copy-start = (s32[32,512]{1,0:T(8,128)S(1)}, s32[32,512]{1,0:T(8,128)}, u32[]{:S(2)}) copy-start(s32[32,512]{1,0:T(8,128)} %refs_3_) | copy-start | bytes 196612
  31.6 7.7 %collective-permute-start.8 = (f32[16,512]{1,0:T(8,128)S(1)}, f32[16,512]{1,0:T(8,128)S(1)}, u32[]{:S(2)}, u32[]{:S(2)}) collective-permute-start(f32[16,512]{1,0:T(8,128)S(1)} %get-tuple-element.38), channel_id=1, source_target_pairs={{0,1},{1,0},{2,3},{3,2},{4,5},{5,4},{6,7},{7,6},{8,16},{9,17},{10,... | collective-permute-start | bytes 98312 | tf_op jit(solution)/shard_map/ppermute | solution.py:317
  31.8 7.5 %collective-permute-start.9 = (f32[16,512]{1,0:T(8,128)S(1)}, f32[16,512]{1,0:T(8,128)S(1)}, u32[]{:S(2)}, u32[]{:S(2)}) collective-permute-start(f32[16,512]{1,0:T(8,128)S(1)} %get-tuple-element.39), channel_id=1, source_target_pairs={{0,8},{1,9},{2,10},{3,11},{4,12},{5,13},{6,14},{7,15},{8,0},{9,1},... | collective-permute-start | bytes 98312 | tf_op jit(solution)/shard_map/ppermute | solution.py:316
  33.4 6.0 %collective-permute-start.10 = (f32[40,128]{1,0:T(8,128)S(1)}, f32[40,128]{1,0:T(8,128)S(1)}, u32[]{:S(2)}, u32[]{:S(2)}) collective-permute-start(f32[40,128]{1,0:T(8,128)S(1)} %get-tuple-element.40), channel_id=1, source_target_pairs={{0,1},{1,0},{2,3},{3,2},{4,5},{5,4},{6,7},{7,6},{8,9},{9,8},{10,11... | collective-permute-start | bytes 61448 | tf_op jit(solution)/shard_map/ppermute | solution.py:318
  33.7 5.6 %collective-permute-start.7 = (f32[32,128]{1,0:T(8,128)S(1)}, f32[32,128]{1,0:T(8,128)S(1)}, u32[]{:S(2)}, u32[]{:S(2)}) collective-permute-start(f32[32,128]{1,0:T(8,128)S(1)} %get-tuple-element.37), channel_id=1, source_target_pairs={{0,8},{1,2},{2,1},{3,4},{4,3},{5,6},{6,5},{7,15},{8,0},{9,10},{10,... | collective-permute-start | bytes 49160 | tf_op jit(solution)/shard_map/ppermute | solution.py:315

commit v6 on v5

--- a/solution.py
+++ b/solution.py
@@ -26,8 +26,8 @@
     "Xa": ("a", 0),
     "Xb": ("b", 0),
 }
-EARLY = ("D2", "Xa", "Db", "X2")
-LATE = ("Da", "Y2", "Xb")
+EARLY = ("D2", "Xb", "Da", "X2")
+LATE = ("Db", "Y2", "Xa")
 ORDER = ("own",) + EARLY + LATE
 STARTS = EARLY + LATE
 

time: 41.1 us -> 40.8 us (level); the launches traced: 40.3 us -> 40.6 us
  waiting for transfers between devices: 5.84 us -> 8.5 us
  starting transfers between devices: 25.7 us -> 23.4 us
    ppermute x7, waiting for transfers between devices: 5.83 us -> 8.49 us  [send(): lax.ppermute(cut(name), both, swap_pairs(name))]
    ppermute x7, starting transfers between devices: 19.8 us -> 18 us  [send(): lax.ppermute(cut(name), both, swap_pairs(name))]
    ppermute x1, starting transfers between devices: 3.79 us -> 3.29 us  [on_device(): lax.ppermute(right, everywhere, neighbour_pairs(tiles, columns, 1, 1))]
    ppermute x1, starting transfers between devices: 0.36 us -> 0.86 us  [on_device(): left = lax.ppermute(left, everywhere, neighbour_pairs(tiles, columns, 1, 0))]
    ppermute x1, starting transfers between devices: 1.56 us -> 1.06 us  [on_device(): one = lax.ppermute(one, everywhere, neighbour_pairs(tiles, columns, 0, 0))]
  transfers between devices with their start and end apart: 11 -> 11, of which waited for: 4 -> 4; matrix products, arithmetic and copies ran while one was open for 3% -> 3% of each run, Pallas kernels for 11% -> 10%
where the time goes in v6:
time: 40.8 us; the launch traced here: 40.6 us
  starting transfers between devices  23.4 us (57%)
  waiting for transfers between devices  8.5 us (21%)
  Pallas kernels  5.34 us (13%)
  local copies, waits for them, and re-layouts  2.63 us (6%)
  between operations  0.78 us (2%)
    ppermute x7, starting transfers between devices, send(): lax.ppermute(cut(name), both, swap_pairs(name))  18 us
    ppermute x7, waiting for transfers between devices, send(): lax.ppermute(cut(name), both, swap_pairs(name))  8.49 us
    ppermute x1, starting transfers between devices, on_device(): lax.ppermute(right, everywhere, neighbour_pairs(tiles, columns, 1, 1))  3.29 us
    squeeze x2, local copies, waits for them, and re-layouts, cut(): lax.dynamic_index_in_dim(phase, partner(name, x, y, core, jnp.where), 1,...  2.61 us
    pallas_call x1, Pallas kernels, on_device(): call(displacement_kernel, [VMEM] * (2 + len(late)), shape(epochs, rows, c...  1.8 us
    pallas_call x1, Pallas kernels, on_device(): call(series_kernel, [VMEM] * (2 + len(early)), (shape(epochs, rows, cols)...  1.52 us
    ppermute x1, starting transfers between devices, on_device(): one = lax.ppermute(one, everywhere, neighbour_pairs(tiles, columns, 0, 0))  1.06 us
    pallas_call x1, Pallas kernels, on_device(): call(gradient_kernel, [VMEM] * 5, (shape(rows, cols), shape(rows, cols)),...  0.92 us
  transfers between devices with their start and end apart: 11, of which 4 were waited for; matrix products, arithmetic and copies ran while one was open for 3% of the time, Pallas kernels for 10%

profile of v6, /device:TPU:96, one launch (start us, length us, event | category | flops | bytes accessed | tf_op | source)
XLA Modules:
  0.0 40.6 jit_solution(17719885705324508093)
XLA Ops:
  0.7 0.0 copy-start.1
  0.7 0.0 copy-start.2
  0.7 1.4 %dynamic-slice_bitcast_fusion.2 = (bf16[8,32,512]{2,1,0:T(8,128)(2,1)S(1)}, bf16[8,32,512]{2,1,0:T(8,128)(2,1)S(1)}, bf16[8,32,512]{2,1,0:T(8,128)(2,1)S(1)}, bf...) fusion(bf16[8,8,32,512]{3,2,1,0:T(8,128)(2,1)} %param.5, s32[]{:T(128)S(6)} %select_n.41, s32[]{:T(128)S(6)} %select_n.39, ...), kind=kLoop, calls=%fused_computation.2 | loop fusion | bytes 2621460 | tf_op jit(solution)/shard_map/jit(dynamic_index_in_dim)/squeeze | solution.py:276
  2.1 5.7 %collective-permute-start = (bf16[8,32,512]{2,1,0:T(8,128)(2,1)S(1)}, bf16[8,32,512]{2,1,0:T(8,128)(2,1)S(1)}, u32[]{:S(2)}, u32[]{:S(2)}) collective-permute-start(bf16[8,32,512]{2,1,0:T(8,128)(2,1)S(1)} %get-tuple-element.49), channel_id=1, source_target_pairs={{0,160},{8,168},{16,176},{24,184},{32,128},{40,136},{48,144},{56,1... | collective-permute-start | bytes 786440 | tf_op jit(solution)/shard_map/ppermute | solution.py:279
  7.9 1.1 %collective-permute-start.1 = (bf16[8,32,512]{2,1,0:T(8,128)(2,1)S(1)}, bf16[8,32,512]{2,1,0:T(8,128)(2,1)S(1)}, u32[]{:S(2)}, u32[]{:S(2)}) collective-permute-start(bf16[8,32,512]{2,1,0:T(8,128)(2,1)S(1)} %get-tuple-element.48), channel_id=1, source_target_pairs={{0,192},{8,72},{16,208},{24,88},{32,224},{40,104},{48,240},{56,120... | collective-permute-start | bytes 786440 | tf_op jit(solution)/shard_map/ppermute | solution.py:279
  9.0 0.0 collective-permute-start.2
  9.0 3.3 %collective-permute-start.3 = (bf16[8,32,512]{2,1,0:T(8,128)(2,1)S(1)}, bf16[8,32,512]{2,1,0:T(8,128)(2,1)S(1)}, u32[]{:S(2)}, u32[]{:S(2)}) collective-permute-start(bf16[8,32,512]{2,1,0:T(8,128)(2,1)S(1)} %get-tuple-element.50), channel_id=1, source_target_pairs={{0,128},{8,136},{16,144},{24,152},{32,160},{40,168},{48,176},{56,1... | collective-permute-start | bytes 786440 | tf_op jit(solution)/shard_map/ppermute | solution.py:279
  12.3 3.8 %collective-permute-start.4 = (bf16[8,32,512]{2,1,0:T(8,128)(2,1)S(1)}, bf16[8,32,512]{2,1,0:T(8,128)(2,1)S(1)}, u32[]{:S(2)}, u32[]{:S(2)}) collective-permute-start(bf16[8,32,512]{2,1,0:T(8,128)(2,1)S(1)} %get-tuple-element.46), channel_id=1, source_target_pairs={{0,224},{8,104},{16,240},{24,120},{32,192},{40,72},{48,208},{56,88... | collective-permute-start | bytes 786440 | tf_op jit(solution)/shard_map/ppermute | solution.py:279
  16.1 0.0 collective-permute-done.refs_1_
  16.1 1.2 %dynamic-slice_bitcast_fusion = (bf16[8,32,512]{2,1,0:T(8,128)(2,1)S(1)}, bf16[8,32,512]{2,1,0:T(8,128)(2,1)S(1)}, bf16[8,32,512]{2,1,0:T(8,128)(2,1)S(1)}) fusion(bf16[8,8,32,512]{3,2,1,0:T(8,128)(2,1)} %param.5, s32[]{:T(128)S(6)} %select_n.43, s32[]{:T(128)S(6)} %select_n.42, s32[]{:T(128)S(6)} %select_n.35), kind=kLoop, calls=%fused_computation | loop fusion | bytes 1572876 | tf_op jit(solution)/shard_map/jit(dynamic_index_in_dim)/squeeze | solution.py:276
  17.3 2.5 %collective-permute-start.5 = (bf16[8,32,512]{2,1,0:T(8,128)(2,1)S(1)}, bf16[8,32,512]{2,1,0:T(8,128)(2,1)S(1)}, u32[]{:S(2)}, u32[]{:S(2)}) collective-permute-start(bf16[8,32,512]{2,1,0:T(8,128)(2,1)S(1)} %get-tuple-element.44), channel_id=1, source_target_pairs={{0,32},{8,40},{16,48},{24,56},{32,0},{40,8},{48,16},{56,24},{64,96... | collective-permute-start | bytes 786440 | tf_op jit(solution)/shard_map/ppermute | solution.py:279
  19.8 1.3 %collective-permute-done.1.refs_2_ = bf16[8,32,512]{2,1,0:T(8,128)(2,1)S(1)} collective-permute-done((bf16[8,32,512]{2,1,0:T(8,128)(2,1)S(1)}, bf16[8,32,512]{2,1,0:T(8,128)(2,1)S(1)}, u32[]{:S(2)}, u32[]{:S(2)}) %collective-permute-start.1) | collective-permute-done | bytes 262176 | tf_op jit(solution)/shard_map/ppermute | solution.py:279
  21.1 1.5 %collective-permute-start.6 = (bf16[8,32,512]{2,1,0:T(8,128)(2,1)S(1)}, bf16[8,32,512]{2,1,0:T(8,128)(2,1)S(1)}, u32[]{:S(2)}, u32[]{:S(2)}) collective-permute-start(bf16[8,32,512]{2,1,0:T(8,128)(2,1)S(1)} %get-tuple-element.43), channel_id=1, source_target_pairs={{0,64},{8,200},{16,80},{24,216},{32,96},{40,232},{48,112},{56,248}... | collective-permute-start | bytes 786440 | tf_op jit(solution)/shard_map/ppermute | solution.py:279
  22.6 0.0 copy-done.3
  22.6 0.9 %shard_map.76 = (bf16[768,1024]{1,0:T(8,128)(2,1)S(1)}, f32[32,512]{1,0:T(8,128)S(1)}, f32[64,128]{1,0:T(8,128)S(1)}) custom-call(f32[4,3]{1,0:T(4,128)S(1)} %copy-done.3, bf16[48,64]{1,0:T(8,128)(2,1)S(1)} %copy-done.2, s32[32,512]{1,0:T(8,128)S(1)} %copy-done.1), custom_call_target="tpu_custom_call" | custom-call | flops 100663296 | bytes 1572864 | tf_op jit(solution)/shard_map/pallas_call | solution.py:288
  23.5 0.0 collective-permute-done.2.refs_3_
  23.6 3.3 %collective-permute-done.3.refs_4_ = bf16[8,32,512]{2,1,0:T(8,128)(2,1)S(1)} collective-permute-done((bf16[8,32,512]{2,1,0:T(8,128)(2,1)S(1)}, bf16[8,32,512]{2,1,0:T(8,128)(2,1)S(1)}, u32[]{:S(2)}, u32[]{:S(2)}) %collective-permute-start.3) | collective-permute-done | bytes 262176 | tf_op jit(solution)/shard_map/ppermute | solution.py:279
  26.9 1.5 %shard_map.77 = (f32[48,32,512]{2,1,0:T(8,128)S(1)}, f32[32,512]{1,0:T(8,128)S(1)}) custom-call(bf16[768,1024]{1,0:T(8,128)(2,1)S(1)} %get-tuple-element.26.w_ref, f32[64,128]{1,0:T(8,128)S(1)} %get-tuple-element.27.weight_ref, bf16[8,32,512]{2,1,0:T(8,128)(2,1)S(1)} %get-tuple-element.45.refs_0_, bf16[8,32,512]{2,1,0:T(8,128)(2,1)S(1)} %collective-permute-done.refs_1_, ...), custom_call_target="tpu_custom_call" | custom-call | flops 1610612736 | bytes 2097152 | tf_op jit(solution)/shard_map/pallas_call | solution.py:296
  28.4 2.1 %collective-permute-done.4.refs_0_ = bf16[8,32,512]{2,1,0:T(8,128)(2,1)S(1)} collective-permute-done((bf16[8,32,512]{2,1,0:T(8,128)(2,1)S(1)}, bf16[8,32,512]{2,1,0:T(8,128)(2,1)S(1)}, u32[]{:S(2)}, u32[]{:S(2)}) %collective-permute-start.4) | collective-permute-done | bytes 262176 | tf_op jit(solution)/shard_map/ppermute | solution.py:279
  30.5 1.8 %collective-permute-done.5.refs_1_ = bf16[8,32,512]{2,1,0:T(8,128)(2,1)S(1)} collective-permute-done((bf16[8,32,512]{2,1,0:T(8,128)(2,1)S(1)}, bf16[8,32,512]{2,1,0:T(8,128)(2,1)S(1)}, u32[]{:S(2)}, u32[]{:S(2)}) %collective-permute-start.5) | collective-permute-done | bytes 262176 | tf_op jit(solution)/shard_map/ppermute | solution.py:279
  32.3 0.0 collective-permute-done.6.refs_2_
  32.3 0.2 shard_map.79
  32.5 0.2 collective-permute-start.8
  32.7 1.1 %collective-permute-start.9 = (f32[16,512]{1,0:T(8,128)S(1)}, f32[16,512]{1,0:T(8,128)S(1)}, u32[]{:S(2)}, u32[]{:S(2)}) collective-permute-start(f32[16,512]{1,0:T(8,128)S(1)} %get-tuple-element.39), channel_id=1, source_target_pairs={{0,8},{1,9},{2,10},{3,11},{4,12},{5,13},{6,14},{7,15},{8,0},{9,1},... | collective-permute-start | bytes 98312 | tf_op jit(solution)/shard_map/ppermute | solution.py:316
  33.7 0.9 %collective-permute-start.10 = (f32[40,128]{1,0:T(8,128)S(1)}, f32[40,128]{1,0:T(8,128)S(1)}, u32[]{:S(2)}, u32[]{:S(2)}) collective-permute-start(f32[40,128]{1,0:T(8,128)S(1)} %get-tuple-element.40), channel_id=1, source_target_pairs={{0,1},{1,0},{2,3},{3,2},{4,5},{5,4},{6,7},{7,6},{8,9},{9,8},{10,11... | collective-permute-start | bytes 61448 | tf_op jit(solution)/shard_map/ppermute | solution.py:318
  34.6 3.3 %collective-permute-start.7 = (f32[32,128]{1,0:T(8,128)S(1)}, f32[32,128]{1,0:T(8,128)S(1)}, u32[]{:S(2)}, u32[]{:S(2)}) collective-permute-start(f32[32,128]{1,0:T(8,128)S(1)} %get-tuple-element.37), channel_id=1, source_target_pairs={{0,8},{1,2},{2,1},{3,4},{4,3},{5,6},{6,5},{7,15},{8,0},{9,10},{10,... | collective-permute-start | bytes 49160 | tf_op jit(solution)/shard_map/ppermute | solution.py:315
  37.9 1.8 %shard_map.78 = bf16[48,32,512]{2,1,0:T(8,128)(2,1)} custom-call(bf16[768,1024]{1,0:T(8,128)(2,1)S(1)} %get-tuple-element.26.w_ref, f32[48,32,512]{2,1,0:T(8,128)S(1)} %get-tuple-element.32.series_ref, bf16[8,32,512]{2,1,0:T(8,128)(2,1)S(1)} %collective-permute-done.4.refs_0_, bf16[8,32,512]{2,1,0:T(8,128)(2,1)S(1)} %collective-permute-done.5.refs_1_, ...), custom_call_target="tpu_custom_call" | custom-call | flops 805306368 | bytes 1572864 | tf_op jit(solution)/shard_map/pallas_call | solution.py:319
  39.7 0.0 collective-permute-done.7.right_ref
  39.7 0.0 collective-permute-done.10.left_ref
  39.7 0.0 collective-permute-done.8.two_ref
  39.7 0.0 collective-permute-done.9.one_ref
  39.7 0.9 %shard_map.80 = (f32[32,512]{1,0:T(8,128)}, f32[32,512]{1,0:T(8,128)}) custom-call(f32[32,512]{1,0:T(8,128)S(1)} %get-tuple-element.36.v_ref, f32[32,128]{1,0:T(8,128)S(1)} %collective-permute-done.7.right_ref, f32[16,512]{1,0:T(8,128)S(1)} %collective-permute-done.8.two_ref, f32[16,512]{1,0:T(8,128)S(1)} %collective-permute-done.9.one_ref, ...), custom_call_target="tpu_custom_call" | custom-call | flops 6553600 | bytes 262144 | tf_op jit(solution)/shard_map/pallas_call | solution.py:332
  (5 shorter events, 0.0 us)
Async XLA Ops:
  0.7 22.0 %copy-start.1 = (s32[32,512]{1,0:T(8,128)S(1)}, s32[32,512]{1,0:T(8,128)}, u32[]{:S(2)}) copy-start(s32[32,512]{1,0:T(8,128)} %plate_ref) | copy-start | bytes 196612
  0.7 21.9 %copy-start.2 = (bf16[48,64]{1,0:T(8,128)(2,1)S(1)}, bf16[48,64]{1,0:T(8,128)(2,1)}, u32[]{:S(2)}) copy-start(bf16[48,64]{1,0:T(8,128)(2,1)} %pinv_ref) | copy-start | bytes 18436
  0.7 21.9 %copy-start.3 = (f32[4,3]{1,0:T(4,128)S(1)}, f32[4,3]{1,0:T(4,128)}, u32[]{:S(2)}) copy-start(f32[4,3]{1,0:T(4,128)} %rot_ref) | copy-start | bytes 148
  2.1 14.0 %collective-permute-start = (bf16[8,32,512]{2,1,0:T(8,128)(2,1)S(1)}, bf16[8,32,512]{2,1,0:T(8,128)(2,1)S(1)}, u32[]{:S(2)}, u32[]{:S(2)}) collective-permute-start(bf16[8,32,512]{2,1,0:T(8,128)(2,1)S(1)} %get-tuple-element.49), channel_id=1, source_target_pairs={{0,160},{8,168},{16,176},{24,184},{32,128},{40,136},{48,144},{56,1... | collective-permute-start | bytes 786440 | tf_op jit(solution)/shard_map/ppermute | solution.py:279
  7.9 13.2 %collective-permute-start.1 = (bf16[8,32,512]{2,1,0:T(8,128)(2,1)S(1)}, bf16[8,32,512]{2,1,0:T(8,128)(2,1)S(1)}, u32[]{:S(2)}, u32[]{:S(2)}) collective-permute-start(bf16[8,32,512]{2,1,0:T(8,128)(2,1)S(1)} %get-tuple-element.48), channel_id=1, source_target_pairs={{0,192},{8,72},{16,208},{24,88},{32,224},{40,104},{48,240},{56,120... | collective-permute-start | bytes 786440 | tf_op jit(solution)/shard_map/ppermute | solution.py:279
  9.0 14.5 %collective-permute-start.2 = (bf16[8,32,512]{2,1,0:T(8,128)(2,1)S(1)}, bf16[8,32,512]{2,1,0:T(8,128)(2,1)S(1)}, u32[]{:S(2)}, u32[]{:S(2)}) collective-permute-start(bf16[8,32,512]{2,1,0:T(8,128)(2,1)S(1)} %get-tuple-element.47), channel_id=1, source_target_pairs={{0,96},{8,232},{16,112},{24,248},{32,64},{40,200},{48,80},{56,216}... | collective-permute-start | bytes 786440 | tf_op jit(solution)/shard_map/ppermute | solution.py:279
  9.0 17.9 %collective-permute-start.3 = (bf16[8,32,512]{2,1,0:T(8,128)(2,1)S(1)}, bf16[8,32,512]{2,1,0:T(8,128)(2,1)S(1)}, u32[]{:S(2)}, u32[]{:S(2)}) collective-permute-start(bf16[8,32,512]{2,1,0:T(8,128)(2,1)S(1)} %get-tuple-element.50), channel_id=1, source_target_pairs={{0,128},{8,136},{16,144},{24,152},{32,160},{40,168},{48,176},{56,1... | collective-permute-start | bytes 786440 | tf_op jit(solution)/shard_map/ppermute | solution.py:279
  12.3 18.2 %collective-permute-start.4 = (bf16[8,32,512]{2,1,0:T(8,128)(2,1)S(1)}, bf16[8,32,512]{2,1,0:T(8,128)(2,1)S(1)}, u32[]{:S(2)}, u32[]{:S(2)}) collective-permute-start(bf16[8,32,512]{2,1,0:T(8,128)(2,1)S(1)} %get-tuple-element.46), channel_id=1, source_target_pairs={{0,224},{8,104},{16,240},{24,120},{32,192},{40,72},{48,208},{56,88... | collective-permute-start | bytes 786440 | tf_op jit(solution)/shard_map/ppermute | solution.py:279
  17.3 15.0 %collective-permute-start.5 = (bf16[8,32,512]{2,1,0:T(8,128)(2,1)S(1)}, bf16[8,32,512]{2,1,0:T(8,128)(2,1)S(1)}, u32[]{:S(2)}, u32[]{:S(2)}) collective-permute-start(bf16[8,32,512]{2,1,0:T(8,128)(2,1)S(1)} %get-tuple-element.44), channel_id=1, source_target_pairs={{0,32},{8,40},{16,48},{24,56},{32,0},{40,8},{48,16},{56,24},{64,96... | collective-permute-start | bytes 786440 | tf_op jit(solution)/shard_map/ppermute | solution.py:279
  21.1 11.2 %collective-permute-start.6 = (bf16[8,32,512]{2,1,0:T(8,128)(2,1)S(1)}, bf16[8,32,512]{2,1,0:T(8,128)(2,1)S(1)}, u32[]{:S(2)}, u32[]{:S(2)}) collective-permute-start(bf16[8,32,512]{2,1,0:T(8,128)(2,1)S(1)} %get-tuple-element.43), channel_id=1, source_target_pairs={{0,64},{8,200},{16,80},{24,216},{32,96},{40,232},{48,112},{56,248}... | collective-permute-start | bytes 786440 | tf_op jit(solution)/shard_map/ppermute | solution.py:279
  26.9 5.4 %copy-start = (s32[32,512]{1,0:T(8,128)S(1)}, s32[32,512]{1,0:T(8,128)}, u32[]{:S(2)}) copy-start(s32[32,512]{1,0:T(8,128)} %refs_3_) | copy-start | bytes 196612
  32.5 7.2 %collective-permute-start.8 = (f32[16,512]{1,0:T(8,128)S(1)}, f32[16,512]{1,0:T(8,128)S(1)}, u32[]{:S(2)}, u32[]{:S(2)}) collective-permute-start(f32[16,512]{1,0:T(8,128)S(1)} %get-tuple-element.38), channel_id=1, source_target_pairs={{0,1},{1,0},{2,3},{3,2},{4,5},{5,4},{6,7},{7,6},{8,16},{9,17},{10,... | collective-permute-start | bytes 98312 | tf_op jit(solution)/shard_map/ppermute | solution.py:317
  32.7 7.0 %collective-permute-start.9 = (f32[16,512]{1,0:T(8,128)S(1)}, f32[16,512]{1,0:T(8,128)S(1)}, u32[]{:S(2)}, u32[]{:S(2)}) collective-permute-start(f32[16,512]{1,0:T(8,128)S(1)} %get-tuple-element.39), channel_id=1, source_target_pairs={{0,8},{1,9},{2,10},{3,11},{4,12},{5,13},{6,14},{7,15},{8,0},{9,1},... | collective-permute-start | bytes 98312 | tf_op jit(solution)/shard_map/ppermute | solution.py:316
  33.7 6.0 %collective-permute-start.10 = (f32[40,128]{1,0:T(8,128)S(1)}, f32[40,128]{1,0:T(8,128)S(1)}, u32[]{:S(2)}, u32[]{:S(2)}) collective-permute-start(f32[40,128]{1,0:T(8,128)S(1)} %get-tuple-element.40), channel_id=1, source_target_pairs={{0,1},{1,0},{2,3},{3,2},{4,5},{5,4},{6,7},{7,6},{8,9},{9,8},{10,11... | collective-permute-start | bytes 61448 | tf_op jit(solution)/shard_map/ppermute | solution.py:318
  34.6 5.1 %collective-permute-start.7 = (f32[32,128]{1,0:T(8,128)S(1)}, f32[32,128]{1,0:T(8,128)S(1)}, u32[]{:S(2)}, u32[]{:S(2)}) collective-permute-start(f32[32,128]{1,0:T(8,128)S(1)} %get-tuple-element.37), channel_id=1, source_target_pairs={{0,8},{1,2},{2,1},{3,4},{4,3},{5,6},{6,5},{7,15},{8,0},{9,10},{10,... | collective-permute-start | bytes 49160 | tf_op jit(solution)/shard_map/ppermute | solution.py:315

commit v7 on v6

--- a/solution.py
+++ b/solution.py
@@ -197,15 +197,13 @@
     epochs, rows, cols = held_ref.shape
     deep = len(blocks) * blocks[0].shape[0] * SUB
     start = w_ref.shape[1] - deep
-    parts = [slice(t * SUB, (t + 1) * SUB) for t in range(rows // SUB)]
-    stacks = [stacked(blocks, part) for part in parts]
     copies = []
-    for n, e in enumerate(range(0, epochs, CUT)):
-        for part, stack in zip(parts, stacks):
-            found = jnp.dot(w_ref[e * SUB : (e + CUT) * SUB, start:], stack, preferred_element_type=F32)
-            found = found.reshape(CUT, SUB, cols) + series_ref[e : e + CUT, part, :]
-            held_ref[e : e + CUT, part, :] = found.astype(BF16)
-        copies.append(pltpu.make_async_copy(held_ref.at[e : e + CUT], out_ref.at[e : e + CUT], sem.at[n]))
+    for t in range(rows // SUB):
+        part = slice(t * SUB, (t + 1) * SUB)
+        found = jnp.dot(w_ref[:, start:], stacked(blocks, part), preferred_element_type=F32)
+        found = found.reshape(epochs, SUB, cols) + series_ref[:, part, :]
+        held_ref[:, part, :] = found.astype(BF16)
+        copies.append(pltpu.make_async_copy(held_ref.at[:, part], out_ref.at[:, part], sem.at[t]))
         copies[-1].start()
     for copy in copies:
         copy.wait()
@@ -325,7 +323,7 @@
         out_specs=pl.BlockSpec(memory_space=pl.ANY),
         scratch_shapes=[
             pltpu.VMEM((epochs, rows, cols), BF16),
-            pltpu.SemaphoreType.DMA((epochs // CUT,)),
+            pltpu.SemaphoreType.DMA((rows // SUB,)),
         ],
     )(w, series, *late)
 

time: 40.8 us -> 40.8 us (level)
  transfers between devices with their start and end apart: 11 -> 11, of which waited for: 4 -> 4; matrix products, arithmetic and copies ran while one was open for 3% -> 3% of each run, Pallas kernels for 10% -> 11%
where the time goes in v7:
time: 40.8 us; the launch traced here: 40.7 us
  starting transfers between devices  23.4 us (57%)
  waiting for transfers between devices  8.5 us (21%)
  Pallas kernels  5.41 us (13%)
  local copies, waits for them, and re-layouts  2.63 us (6%)
  between operations  0.78 us (2%)
    ppermute x7, starting transfers between devices, send(): lax.ppermute(cut(name), both, swap_pairs(name))  18 us
    ppermute x7, waiting for transfers between devices, send(): lax.ppermute(cut(name), both, swap_pairs(name))  8.49 us
    ppermute x1, starting transfers between devices, on_device(): lax.ppermute(right, everywhere, neighbour_pairs(tiles, columns, 1, 1))  3.29 us
    squeeze x2, local copies, waits for them, and re-layouts, cut(): lax.dynamic_index_in_dim(phase, partner(name, x, y, core, jnp.where), 1,...  2.61 us
    pallas_call x1, Pallas kernels, on_device(): call(displacement_kernel, [VMEM] * (2 + len(late)), shape(epochs, rows, c...  1.87 us
    pallas_call x1, Pallas kernels, on_device(): call(series_kernel, [VMEM] * (2 + len(early)), (shape(epochs, rows, cols)...  1.52 us
    ppermute x1, starting transfers between devices, on_device(): one = lax.ppermute(one, everywhere, neighbour_pairs(tiles, columns, 0, 0))  1.06 us
    pallas_call x1, Pallas kernels, on_device(): call(gradient_kernel, [VMEM] * 5, (shape(rows, cols), shape(rows, cols)),...  0.92 us
  transfers between devices with their start and end apart: 11, of which 4 were waited for; matrix products, arithmetic and copies ran while one was open for 3% of the time, Pallas kernels for 11%

profile of v7, /device:TPU:96, one launch (start us, length us, event | category | flops | bytes accessed | tf_op | source)
XLA Modules:
  0.0 40.7 jit_solution(2318629590489170936)
XLA Ops:
  0.7 0.0 copy-start.1
  0.7 1.4 %dynamic-slice_bitcast_fusion.2 = (bf16[8,32,512]{2,1,0:T(8,128)(2,1)S(1)}, bf16[8,32,512]{2,1,0:T(8,128)(2,1)S(1)}, bf16[8,32,512]{2,1,0:T(8,128)(2,1)S(1)}, bf...) fusion(bf16[8,8,32,512]{3,2,1,0:T(8,128)(2,1)} %param.5, s32[]{:T(128)S(6)} %select_n.41, s32[]{:T(128)S(6)} %select_n.39, ...), kind=kLoop, calls=%fused_computation.2 | loop fusion | bytes 2621460 | tf_op jit(solution)/shard_map/jit(dynamic_index_in_dim)/squeeze | solution.py:274
  2.1 5.7 %collective-permute-start = (bf16[8,32,512]{2,1,0:T(8,128)(2,1)S(1)}, bf16[8,32,512]{2,1,0:T(8,128)(2,1)S(1)}, u32[]{:S(2)}, u32[]{:S(2)}) collective-permute-start(bf16[8,32,512]{2,1,0:T(8,128)(2,1)S(1)} %get-tuple-element.49), channel_id=1, source_target_pairs={{0,160},{8,168},{16,176},{24,184},{32,128},{40,136},{48,144},{56,1... | collective-permute-start | bytes 786440 | tf_op jit(solution)/shard_map/ppermute | solution.py:277
  7.9 1.1 %collective-permute-start.1 = (bf16[8,32,512]{2,1,0:T(8,128)(2,1)S(1)}, bf16[8,32,512]{2,1,0:T(8,128)(2,1)S(1)}, u32[]{:S(2)}, u32[]{:S(2)}) collective-permute-start(bf16[8,32,512]{2,1,0:T(8,128)(2,1)S(1)} %get-tuple-element.48), channel_id=1, source_target_pairs={{0,192},{8,72},{16,208},{24,88},{32,224},{40,104},{48,240},{56,120... | collective-permute-start | bytes 786440 | tf_op jit(solution)/shard_map/ppermute | solution.py:277
  9.0 0.0 collective-permute-start.2
  9.0 3.3 %collective-permute-start.3 = (bf16[8,32,512]{2,1,0:T(8,128)(2,1)S(1)}, bf16[8,32,512]{2,1,0:T(8,128)(2,1)S(1)}, u32[]{:S(2)}, u32[]{:S(2)}) collective-permute-start(bf16[8,32,512]{2,1,0:T(8,128)(2,1)S(1)} %get-tuple-element.50), channel_id=1, source_target_pairs={{0,128},{8,136},{16,144},{24,152},{32,160},{40,168},{48,176},{56,1... | collective-permute-start | bytes 786440 | tf_op jit(solution)/shard_map/ppermute | solution.py:277
  12.3 3.8 %collective-permute-start.4 = (bf16[8,32,512]{2,1,0:T(8,128)(2,1)S(1)}, bf16[8,32,512]{2,1,0:T(8,128)(2,1)S(1)}, u32[]{:S(2)}, u32[]{:S(2)}) collective-permute-start(bf16[8,32,512]{2,1,0:T(8,128)(2,1)S(1)} %get-tuple-element.46), channel_id=1, source_target_pairs={{0,224},{8,104},{16,240},{24,120},{32,192},{40,72},{48,208},{56,88... | collective-permute-start | bytes 786440 | tf_op jit(solution)/shard_map/ppermute | solution.py:277
  16.1 0.0 collective-permute-done.refs_1_
  16.1 1.2 %dynamic-slice_bitcast_fusion = (bf16[8,32,512]{2,1,0:T(8,128)(2,1)S(1)}, bf16[8,32,512]{2,1,0:T(8,128)(2,1)S(1)}, bf16[8,32,512]{2,1,0:T(8,128)(2,1)S(1)}) fusion(bf16[8,8,32,512]{3,2,1,0:T(8,128)(2,1)} %param.5, s32[]{:T(128)S(6)} %select_n.43, s32[]{:T(128)S(6)} %select_n.42, s32[]{:T(128)S(6)} %select_n.35), kind=kLoop, calls=%fused_computation | loop fusion | bytes 1572876 | tf_op jit(solution)/shard_map/jit(dynamic_index_in_dim)/squeeze | solution.py:274
  17.3 2.5 %collective-permute-start.5 = (bf16[8,32,512]{2,1,0:T(8,128)(2,1)S(1)}, bf16[8,32,512]{2,1,0:T(8,128)(2,1)S(1)}, u32[]{:S(2)}, u32[]{:S(2)}) collective-permute-start(bf16[8,32,512]{2,1,0:T(8,128)(2,1)S(1)} %get-tuple-element.44), channel_id=1, source_target_pairs={{0,32},{8,40},{16,48},{24,56},{32,0},{40,8},{48,16},{56,24},{64,96... | collective-permute-start | bytes 786440 | tf_op jit(solution)/shard_map/ppermute | solution.py:277
  19.8 1.3 %collective-permute-done.1.refs_2_ = bf16[8,32,512]{2,1,0:T(8,128)(2,1)S(1)} collective-permute-done((bf16[8,32,512]{2,1,0:T(8,128)(2,1)S(1)}, bf16[8,32,512]{2,1,0:T(8,128)(2,1)S(1)}, u32[]{:S(2)}, u32[]{:S(2)}) %collective-permute-start.1) | collective-permute-done | bytes 262176 | tf_op jit(solution)/shard_map/ppermute | solution.py:277
  21.1 1.5 %collective-permute-start.6 = (bf16[8,32,512]{2,1,0:T(8,128)(2,1)S(1)}, bf16[8,32,512]{2,1,0:T(8,128)(2,1)S(1)}, u32[]{:S(2)}, u32[]{:S(2)}) collective-permute-start(bf16[8,32,512]{2,1,0:T(8,128)(2,1)S(1)} %get-tuple-element.43), channel_id=1, source_target_pairs={{0,64},{8,200},{16,80},{24,216},{32,96},{40,232},{48,112},{56,248}... | collective-permute-start | bytes 786440 | tf_op jit(solution)/shard_map/ppermute | solution.py:277
  22.6 0.0 copy-done.1
  22.6 0.0 copy-done.3
  22.6 0.9 %shard_map.76 = (bf16[768,1024]{1,0:T(8,128)(2,1)S(1)}, f32[32,512]{1,0:T(8,128)S(1)}, f32[64,128]{1,0:T(8,128)S(1)}) custom-call(f32[4,3]{1,0:T(4,128)S(1)} %copy-done.3, bf16[48,64]{1,0:T(8,128)(2,1)S(1)} %copy-done.2, s32[32,512]{1,0:T(8,128)S(1)} %copy-done.1), custom_call_target="tpu_custom_call" | custom-call | flops 100663296 | bytes 1572864 | tf_op jit(solution)/shard_map/pallas_call | solution.py:286
  23.5 0.0 collective-permute-done.2.refs_3_
  23.6 3.3 %collective-permute-done.3.refs_4_ = bf16[8,32,512]{2,1,0:T(8,128)(2,1)S(1)} collective-permute-done((bf16[8,32,512]{2,1,0:T(8,128)(2,1)S(1)}, bf16[8,32,512]{2,1,0:T(8,128)(2,1)S(1)}, u32[]{:S(2)}, u32[]{:S(2)}) %collective-permute-start.3) | collective-permute-done | bytes 262176 | tf_op jit(solution)/shard_map/ppermute | solution.py:277
  26.9 1.5 %shard_map.77 = (f32[48,32,512]{2,1,0:T(8,128)S(1)}, f32[32,512]{1,0:T(8,128)S(1)}) custom-call(bf16[768,1024]{1,0:T(8,128)(2,1)S(1)} %get-tuple-element.26.w_ref, f32[64,128]{1,0:T(8,128)S(1)} %get-tuple-element.27.weight_ref, bf16[8,32,512]{2,1,0:T(8,128)(2,1)S(1)} %get-tuple-element.45.refs_0_, bf16[8,32,512]{2,1,0:T(8,128)(2,1)S(1)} %collective-permute-done.refs_1_, ...), custom_call_target="tpu_custom_call" | custom-call | flops 1610612736 | bytes 2097152 | tf_op jit(solution)/shard_map/pallas_call | solution.py:294
  28.4 2.1 %collective-permute-done.4.refs_0_ = bf16[8,32,512]{2,1,0:T(8,128)(2,1)S(1)} collective-permute-done((bf16[8,32,512]{2,1,0:T(8,128)(2,1)S(1)}, bf16[8,32,512]{2,1,0:T(8,128)(2,1)S(1)}, u32[]{:S(2)}, u32[]{:S(2)}) %collective-permute-start.4) | collective-permute-done | bytes 262176 | tf_op jit(solution)/shard_map/ppermute | solution.py:277
  30.5 1.8 %collective-permute-done.5.refs_1_ = bf16[8,32,512]{2,1,0:T(8,128)(2,1)S(1)} collective-permute-done((bf16[8,32,512]{2,1,0:T(8,128)(2,1)S(1)}, bf16[8,32,512]{2,1,0:T(8,128)(2,1)S(1)}, u32[]{:S(2)}, u32[]{:S(2)}) %collective-permute-start.5) | collective-permute-done | bytes 262176 | tf_op jit(solution)/shard_map/ppermute | solution.py:277
  32.3 0.0 collective-permute-done.6.refs_2_
  32.3 0.2 shard_map.79
  32.5 0.2 collective-permute-start.8
  32.7 1.1 %collective-permute-start.9 = (f32[16,512]{1,0:T(8,128)S(1)}, f32[16,512]{1,0:T(8,128)S(1)}, u32[]{:S(2)}, u32[]{:S(2)}) collective-permute-start(f32[16,512]{1,0:T(8,128)S(1)} %get-tuple-element.39), channel_id=1, source_target_pairs={{0,8},{1,9},{2,10},{3,11},{4,12},{5,13},{6,14},{7,15},{8,0},{9,1},... | collective-permute-start | bytes 98312 | tf_op jit(solution)/shard_map/ppermute | solution.py:314
  33.7 0.9 %collective-permute-start.10 = (f32[40,128]{1,0:T(8,128)S(1)}, f32[40,128]{1,0:T(8,128)S(1)}, u32[]{:S(2)}, u32[]{:S(2)}) collective-permute-start(f32[40,128]{1,0:T(8,128)S(1)} %get-tuple-element.40), channel_id=1, source_target_pairs={{0,1},{1,0},{2,3},{3,2},{4,5},{5,4},{6,7},{7,6},{8,9},{9,8},{10,11... | collective-permute-start | bytes 61448 | tf_op jit(solution)/shard_map/ppermute | solution.py:316
  34.6 3.3 %collective-permute-start.7 = (f32[32,128]{1,0:T(8,128)S(1)}, f32[32,128]{1,0:T(8,128)S(1)}, u32[]{:S(2)}, u32[]{:S(2)}) collective-permute-start(f32[32,128]{1,0:T(8,128)S(1)} %get-tuple-element.37), channel_id=1, source_target_pairs={{0,8},{1,2},{2,1},{3,4},{4,3},{5,6},{6,5},{7,15},{8,0},{9,10},{10,... | collective-permute-start | bytes 49160 | tf_op jit(solution)/shard_map/ppermute | solution.py:313
  37.9 1.9 %shard_map.78 = bf16[48,32,512]{2,1,0:T(8,128)(2,1)} custom-call(bf16[768,1024]{1,0:T(8,128)(2,1)S(1)} %get-tuple-element.26.w_ref, f32[48,32,512]{2,1,0:T(8,128)S(1)} %get-tuple-element.32.series_ref, bf16[8,32,512]{2,1,0:T(8,128)(2,1)S(1)} %collective-permute-done.4.refs_0_, bf16[8,32,512]{2,1,0:T(8,128)(2,1)S(1)} %collective-permute-done.5.refs_1_, ...), custom_call_target="tpu_custom_call" | custom-call | flops 805306368 | bytes 1572864 | tf_op jit(solution)/shard_map/pallas_call | solution.py:317
  39.8 0.0 collective-permute-done.7.right_ref
  39.8 0.0 collective-permute-done.10.left_ref
  39.8 0.0 collective-permute-done.8.two_ref
  39.8 0.0 collective-permute-done.9.one_ref
  39.8 0.9 %shard_map.80 = (f32[32,512]{1,0:T(8,128)}, f32[32,512]{1,0:T(8,128)}) custom-call(f32[32,512]{1,0:T(8,128)S(1)} %get-tuple-element.36.v_ref, f32[32,128]{1,0:T(8,128)S(1)} %collective-permute-done.7.right_ref, f32[16,512]{1,0:T(8,128)S(1)} %collective-permute-done.8.two_ref, f32[16,512]{1,0:T(8,128)S(1)} %collective-permute-done.9.one_ref, ...), custom_call_target="tpu_custom_call" | custom-call | flops 6553600 | bytes 262144 | tf_op jit(solution)/shard_map/pallas_call | solution.py:330
  (5 shorter events, 0.0 us)
Async XLA Ops:
  0.7 22.0 %copy-start.1 = (s32[32,512]{1,0:T(8,128)S(1)}, s32[32,512]{1,0:T(8,128)}, u32[]{:S(2)}) copy-start(s32[32,512]{1,0:T(8,128)} %plate_ref) | copy-start | bytes 196612
  0.7 21.9 %copy-start.2 = (bf16[48,64]{1,0:T(8,128)(2,1)S(1)}, bf16[48,64]{1,0:T(8,128)(2,1)}, u32[]{:S(2)}) copy-start(bf16[48,64]{1,0:T(8,128)(2,1)} %pinv_ref) | copy-start | bytes 18436
  0.7 21.9 %copy-start.3 = (f32[4,3]{1,0:T(4,128)S(1)}, f32[4,3]{1,0:T(4,128)}, u32[]{:S(2)}) copy-start(f32[4,3]{1,0:T(4,128)} %rot_ref) | copy-start | bytes 148
  2.1 14.0 %collective-permute-start = (bf16[8,32,512]{2,1,0:T(8,128)(2,1)S(1)}, bf16[8,32,512]{2,1,0:T(8,128)(2,1)S(1)}, u32[]{:S(2)}, u32[]{:S(2)}) collective-permute-start(bf16[8,32,512]{2,1,0:T(8,128)(2,1)S(1)} %get-tuple-element.49), channel_id=1, source_target_pairs={{0,160},{8,168},{16,176},{24,184},{32,128},{40,136},{48,144},{56,1... | collective-permute-start | bytes 786440 | tf_op jit(solution)/shard_map/ppermute | solution.py:277
  7.9 13.2 %collective-permute-start.1 = (bf16[8,32,512]{2,1,0:T(8,128)(2,1)S(1)}, bf16[8,32,512]{2,1,0:T(8,128)(2,1)S(1)}, u32[]{:S(2)}, u32[]{:S(2)}) collective-permute-start(bf16[8,32,512]{2,1,0:T(8,128)(2,1)S(1)} %get-tuple-element.48), channel_id=1, source_target_pairs={{0,192},{8,72},{16,208},{24,88},{32,224},{40,104},{48,240},{56,120... | collective-permute-start | bytes 786440 | tf_op jit(solution)/shard_map/ppermute | solution.py:277
  9.0 14.5 %collective-permute-start.2 = (bf16[8,32,512]{2,1,0:T(8,128)(2,1)S(1)}, bf16[8,32,512]{2,1,0:T(8,128)(2,1)S(1)}, u32[]{:S(2)}, u32[]{:S(2)}) collective-permute-start(bf16[8,32,512]{2,1,0:T(8,128)(2,1)S(1)} %get-tuple-element.47), channel_id=1, source_target_pairs={{0,96},{8,232},{16,112},{24,248},{32,64},{40,200},{48,80},{56,216}... | collective-permute-start | bytes 786440 | tf_op jit(solution)/shard_map/ppermute | solution.py:277
  9.0 17.9 %collective-permute-start.3 = (bf16[8,32,512]{2,1,0:T(8,128)(2,1)S(1)}, bf16[8,32,512]{2,1,0:T(8,128)(2,1)S(1)}, u32[]{:S(2)}, u32[]{:S(2)}) collective-permute-start(bf16[8,32,512]{2,1,0:T(8,128)(2,1)S(1)} %get-tuple-element.50), channel_id=1, source_target_pairs={{0,128},{8,136},{16,144},{24,152},{32,160},{40,168},{48,176},{56,1... | collective-permute-start | bytes 786440 | tf_op jit(solution)/shard_map/ppermute | solution.py:277
  12.3 18.2 %collective-permute-start.4 = (bf16[8,32,512]{2,1,0:T(8,128)(2,1)S(1)}, bf16[8,32,512]{2,1,0:T(8,128)(2,1)S(1)}, u32[]{:S(2)}, u32[]{:S(2)}) collective-permute-start(bf16[8,32,512]{2,1,0:T(8,128)(2,1)S(1)} %get-tuple-element.46), channel_id=1, source_target_pairs={{0,224},{8,104},{16,240},{24,120},{32,192},{40,72},{48,208},{56,88... | collective-permute-start | bytes 786440 | tf_op jit(solution)/shard_map/ppermute | solution.py:277
  17.3 15.0 %collective-permute-start.5 = (bf16[8,32,512]{2,1,0:T(8,128)(2,1)S(1)}, bf16[8,32,512]{2,1,0:T(8,128)(2,1)S(1)}, u32[]{:S(2)}, u32[]{:S(2)}) collective-permute-start(bf16[8,32,512]{2,1,0:T(8,128)(2,1)S(1)} %get-tuple-element.44), channel_id=1, source_target_pairs={{0,32},{8,40},{16,48},{24,56},{32,0},{40,8},{48,16},{56,24},{64,96... | collective-permute-start | bytes 786440 | tf_op jit(solution)/shard_map/ppermute | solution.py:277
  21.1 11.2 %collective-permute-start.6 = (bf16[8,32,512]{2,1,0:T(8,128)(2,1)S(1)}, bf16[8,32,512]{2,1,0:T(8,128)(2,1)S(1)}, u32[]{:S(2)}, u32[]{:S(2)}) collective-permute-start(bf16[8,32,512]{2,1,0:T(8,128)(2,1)S(1)} %get-tuple-element.43), channel_id=1, source_target_pairs={{0,64},{8,200},{16,80},{24,216},{32,96},{40,232},{48,112},{56,248}... | collective-permute-start | bytes 786440 | tf_op jit(solution)/shard_map/ppermute | solution.py:277
  26.9 5.4 %copy-start = (s32[32,512]{1,0:T(8,128)S(1)}, s32[32,512]{1,0:T(8,128)}, u32[]{:S(2)}) copy-start(s32[32,512]{1,0:T(8,128)} %refs_3_) | copy-start | bytes 196612
  32.5 7.3 %collective-permute-start.8 = (f32[16,512]{1,0:T(8,128)S(1)}, f32[16,512]{1,0:T(8,128)S(1)}, u32[]{:S(2)}, u32[]{:S(2)}) collective-permute-start(f32[16,512]{1,0:T(8,128)S(1)} %get-tuple-element.38), channel_id=1, source_target_pairs={{0,1},{1,0},{2,3},{3,2},{4,5},{5,4},{6,7},{7,6},{8,16},{9,17},{10,... | collective-permute-start | bytes 98312 | tf_op jit(solution)/shard_map/ppermute | solution.py:315
  32.7 7.1 %collective-permute-start.9 = (f32[16,512]{1,0:T(8,128)S(1)}, f32[16,512]{1,0:T(8,128)S(1)}, u32[]{:S(2)}, u32[]{:S(2)}) collective-permute-start(f32[16,512]{1,0:T(8,128)S(1)} %get-tuple-element.39), channel_id=1, source_target_pairs={{0,8},{1,9},{2,10},{3,11},{4,12},{5,13},{6,14},{7,15},{8,0},{9,1},... | collective-permute-start | bytes 98312 | tf_op jit(solution)/shard_map/ppermute | solution.py:314
  33.7 6.0 %collective-permute-start.10 = (f32[40,128]{1,0:T(8,128)S(1)}, f32[40,128]{1,0:T(8,128)S(1)}, u32[]{:S(2)}, u32[]{:S(2)}) collective-permute-start(f32[40,128]{1,0:T(8,128)S(1)} %get-tuple-element.40), channel_id=1, source_target_pairs={{0,1},{1,0},{2,3},{3,2},{4,5},{5,4},{6,7},{7,6},{8,9},{9,8},{10,11... | collective-permute-start | bytes 61448 | tf_op jit(solution)/shard_map/ppermute | solution.py:316
  34.6 5.2 %collective-permute-start.7 = (f32[32,128]{1,0:T(8,128)S(1)}, f32[32,128]{1,0:T(8,128)S(1)}, u32[]{:S(2)}, u32[]{:S(2)}) collective-permute-start(f32[32,128]{1,0:T(8,128)S(1)} %get-tuple-element.37), channel_id=1, source_target_pairs={{0,8},{1,2},{2,1},{3,4},{4,3},{5,6},{6,5},{7,15},{8,0},{9,10},{10,... | collective-permute-start | bytes 49160 | tf_op jit(solution)/shard_map/ppermute | solution.py:313
